TPU v7x, 256 devices: a whole 4x4x8 slice. The times are simulated.
256 devices in a mesh: blk: 128 (over z, x, y), grp: 2 (over core).
Axes of the slice: x: 4, y: 4, z: 8, core: 2. Of those that a mesh axis runs over, the one named last changes fastest.
Arguments:
- emission: float32 [8192, 32, 128], P('blk'), may hold values from 0.05 to 2
- positions: float32 [3, 8192, 128], P(None, 'blk'), may hold values from 0 to 6
- patch_area: float32 [8192, 128], P('blk'), may hold values from 0.03 to 0.3
- facing: float32 [8192, 128], P('blk'), may hold values from 0.2 to 1
- albedo_class: int32 [8192, 128], P('blk'), may hold values from 0 to 7
- albedo_table: float32 [8], replicated, may hold values from 0.1 to 0.7
- fetch_block: int32 [32768], P('blk'), may hold values from 0 to 63
- pair_rows: int32 [163840], P(('blk', 'grp')), may hold values from 0 to 63
- pair_slots: int32 [163840], P(('blk', 'grp')), may hold values from 0 to 255
- pair_code: int32 [163840], P(('blk', 'grp')), may hold values from 0 to 131071
Outputs:
- radiosity: float32 [8192, 32, 128], P('blk')
Inputs may be any that keep to these rules, and one draw needn't show every extreme that they name: `fetch_block`: slot s of index b of blk names a block owned by index s // 2 of blk.
All inputs are finite; a program needn't handle non-finite values.
Results may differ from a plain program's by a relative error of at most 0.0003.
Values may be sent and summed in bfloat16 or wider, within the bound.
No kernel may reach another device: no remote copies, remote signals or barrier semaphores. Data moves between devices by JAX's collectives and lax.ppermute only.
A program may use at most 128 MiB of HBM per device.

v0:
```python
import math

import jax
import jax.numpy as jnp
from jax import lax
from jax.sharding import PartitionSpec as P

BLOCK = 128
NCLASS = 8
SWEEPS = 2


def visible(pair_kind):
    patch_ids = jnp.arange(BLOCK, dtype=jnp.int32)
    hashed = (
        pair_kind[:, None, None] * (BLOCK * BLOCK)
        + patch_ids[None, :, None] * BLOCK
        + patch_ids[None, None, :]
    )
    hashed = hashed * 747796405
    hashed = hashed ^ jnp.left_shift(hashed, 13)
    hashed = hashed ^ lax.shift_right_logical(hashed, jnp.full_like(hashed, 17))
    hashed = hashed ^ jnp.left_shift(hashed, 5)
    return (lax.shift_right_logical(hashed, jnp.full_like(hashed, 7)) & 1).astype(jnp.float32)


def build_tiles(geo_near, geo_far, pair_kind):
    distance_sq = jnp.zeros((geo_near.shape[0], BLOCK, BLOCK), jnp.float32)
    for component in range(3):
        offset = geo_near[:, component, :, None] - geo_far[:, component, None, :]
        distance_sq = distance_sq + offset * offset
    soften = geo_near[:, 3, :, None] + geo_far[:, 3, None, :]
    facing_pair = geo_near[:, 4, :, None] * geo_far[:, 4, None, :]
    return (visible(pair_kind) * facing_pair / (math.pi * (distance_sq + soften))).astype(
        jnp.bfloat16
    )


def local(
    emission,
    positions,
    patch_area,
    facing,
    albedo_class,
    albedo_table,
    fetch_block,
    pair_rows,
    pair_slots,
    pair_code,
):
    blk_dev = emission.shape[0]
    hour_count = emission.shape[1]
    owners = lax.axis_size("blk")
    slot_count = fetch_block.shape[0]
    per_owner = slot_count // owners
    pair_count = pair_rows.shape[0]
    per_turn = 128
    turn_count = pair_count // per_turn
    geo_rows = jnp.stack([positions[0], positions[1], positions[2], patch_area, facing], axis=1)
    class_ids = jnp.arange(NCLASS, dtype=jnp.int32)
    albedo = jnp.sum(
        jnp.where(albedo_class[..., None] == class_ids, albedo_table, jnp.float32(0.0)), axis=-1
    )
    requests = lax.all_to_all(
        fetch_block.reshape(owners, per_owner), "blk", split_axis=0, concat_axis=0, tiled=True
    )
    geo_slots = lax.all_to_all(
        geo_rows[requests], "blk", split_axis=0, concat_axis=0, tiled=True
    ).reshape(slot_count, 5, BLOCK)
    row_turns = pair_rows.reshape(turn_count, per_turn)
    slot_turns = pair_slots.reshape(turn_count, per_turn)
    kind_turns = pair_code.reshape(turn_count, per_turn)
    turn_ids = jnp.arange(turn_count, dtype=jnp.int32)

    def make_tile(row_ids, slot_ids, kind_ids):
        return build_tiles(geo_rows[row_ids], geo_slots[slot_ids], kind_ids)

    def fetch_tile(row_ids, slot_ids, kind_ids):
        return make_tile(row_ids, slot_ids, kind_ids)

    radiance = emission
    for sweep_number in range(SWEEPS):
        exitance = (patch_area[:, None, :] * radiance).astype(jnp.bfloat16)
        fetched = lax.all_to_all(
            exitance[requests], "blk", split_axis=0, concat_axis=0, tiled=True
        ).reshape(slot_count, hour_count, BLOCK)

        def accumulate(totals, inputs):
            to_local, to_slots = totals
            turn_index, row_ids, slot_ids, kind_ids = inputs
            form_tile = fetch_tile(row_ids, slot_ids, kind_ids)
            to_rows = jnp.einsum(
                "bpq,bhq->bhp", form_tile, fetched[slot_ids], preferred_element_type=jnp.float32
            )
            to_cols = jnp.einsum(
                "bpq,bhp->bhq", form_tile, exitance[row_ids], preferred_element_type=jnp.float32
            )
            to_local = to_local + jax.ops.segment_sum(to_rows, row_ids, num_segments=blk_dev)
            to_slots = to_slots + jax.ops.segment_sum(to_cols, slot_ids, num_segments=slot_count)
            return ((to_local, to_slots), None)

        start_local = jnp.zeros((blk_dev, hour_count, BLOCK), jnp.float32)
        start_slots = jnp.zeros((slot_count, hour_count, BLOCK), jnp.float32)
        to_local, to_slots = lax.scan(
            accumulate, (start_local, start_slots), (turn_ids, row_turns, slot_turns, kind_turns)
        )[0]
        outgoing = to_slots.reshape(owners, per_owner, hour_count, BLOCK)
        returned = lax.all_to_all(outgoing, "blk", split_axis=0, concat_axis=0, tiled=True)
        received = jax.ops.segment_sum(
            returned.reshape(slot_count, hour_count, BLOCK),
            requests.reshape(slot_count),
            num_segments=blk_dev,
        )
        irradiance = lax.psum(to_local + received, "grp")
        radiance = emission + albedo[:, None, :] * irradiance
    return radiance


def solution(mesh):
    in_specs = (
        P("blk", None, None),
        P(None, "blk", None),
        P("blk", None),
        P("blk", None),
        P("blk", None),
        P(),
        P("blk"),
        P(("blk", "grp")),
        P(("blk", "grp")),
        P(("blk", "grp")),
    )
    out_specs = P("blk", None, None)
    return jax.shard_map(local, mesh=mesh, in_specs=in_specs, out_specs=out_specs, check_vma=False)
```

profile of v0, /device:TPU:1, one launch (start us, length us, event | category | flops | bytes accessed | tf_op | source)
XLA Modules:
  0.0 1264.8 jit_solution(16228512198080957550)
XLA Ops:
  8.1 16.3 %all-to-all-start = ((s32[128,1,2]{2,1,0:T(1,128)}), s32[128,1,2]{2,1,0:T(1,128)S(1)}, u32[]{:S(2)}, u32[]{:S(2)}) async-start(s32[128,1,2]{2,1,0:T(1,128)} %bitcast.36), calls=%async_computation | async-start | bytes 131072 | tf_op jit(solution)/shard_map/all_to_all | solution.py:64
  46.6 17.2 %all-to-all-done.2 = f32[128,2,5,128]{3,1,2,0:T(2,128)S(1)} async-done(((f32[128,2,5,128]{3,1,2,0:T(2,128)}), f32[128,2,5,128]{3,1,2,0:T(2,128)S(1)}, u32[]{:S(2)}, u32[]{:S(2)}) %all-to-all-start.2) | async-done | bytes 655392 | tf_op jit(solution)/shard_map/all_to_all | solution.py:67
  73.6 45.9 %all-to-all-done.1 = bf16[128,2,32,128]{3,2,1,0:T(8,128)(2,1)} async-done(((bf16[128,2,32,128]{3,2,1,0:T(8,128)(2,1)}), bf16[128,2,32,128]{3,2,1,0:T(8,128)(2,1)}, u32[]{:S(2)}, u32[]{:S(2)}) %all-to-all-start.1) | async-done | bytes 2097184 | tf_op jit(solution)/shard_map/all_to_all | solution.py:84
  122.1 373.1 %while.24 = (s32[]{:T(128)}, f32[64,32,128]{2,1,0:T(8,128)S(1)}, f32[256,32,128]{2,1,0:T(8,128)}, s32[5,128]{1,0:T(8,128)S(1)}, s32[5,128]{1,0:T(8,128)S(1)}, /*...) while((s32[]{:T(128)}, f32[64,32,128]{2,1,0:T(8,128)S(1)}, ...), condition=%wide.region_4.5_spmd, body=%wide.region_1.4_spmd.sunk | while | flops 378555392 | bytes 29586328 | solution.py:104
  128.1 17.8 %fusion.79 = f32[128,32,128]{2,1,0:T(8,128)} fusion(bf16[128,32,128]{2,1,0:T(8,128)(2,1)} %gather_fusion.3, f32[128,128]{1,0:T(8,128)} %bitcast.156, f32[128,128]{1,0:T(8,128)} %bitcast.176, f32[128,128]{1,0:T(8,128)S(1)} %bitcast.150, f32[128,128]{1,0:T(8,128)} %bitcast.170, f32[128,128]{1,0:T(8,128)} %bitcast.152, f32[128,128]{1,0:T(8,128)} %bitcast.172, ...), kind=kOutput, calls=%fused_computation.41.clone.2 | convolution fusion | flops 188743680 | bytes 3866624 | tf_op jit(solution)/shard_map/while/body/eval_jaxpr/bpq,bhp->bhq/dot_general | solution.py:95
  146.7 17.4 %scatter_fusion.1 = f32[256,32,128]{2,1,0:T(8,128)} fusion(f32[256,32,128]{2,1,0:T(8,128)} %get-tuple-element.437, s32[128]{0:T(128)S(1)} %fusion.78, f32[128,32,128]{2,1,0:T(8,128)} %fusion.79), kind=kCustom, calls=%fused_computation.12.clone.1 | custom fusion | flops 524288 | bytes 6291968 | tf_op jit(solution)/shard_map/while/body/eval_jaxpr/scatter-add | solution.py:99
  167.4 17.6 %fusion.77 = f32[128,32,128]{2,1,0:T(8,128)} fusion(bf16[128,32,128]{2,1,0:T(8,128)(2,1)} %gather_fusion, f32[128,128]{1,0:T(8,128)S(1)} %bitcast.157, f32[128,128]{1,0:T(8,128)S(1)} %bitcast.177, f32[128,128]{1,0:T(8,128)S(1)} %bitcast.151, f32[128,128]{1,0:T(8,128)S(1)} %bitcast.171, f32[128,128]{1,0:T(8,128)S(1)} %bitcast.153, ...), kind=kOutput, calls=%fused_computation.42.clone.2 | convolution fusion | flops 188743680 | bytes 3866624 | tf_op jit(solution)/shard_map/while/body/eval_jaxpr/bpq,bhq->bhp/dot_general | solution.py:92
  202.7 17.8 %fusion.79 = f32[128,32,128]{2,1,0:T(8,128)} fusion(bf16[128,32,128]{2,1,0:T(8,128)(2,1)} %gather_fusion.3, f32[128,128]{1,0:T(8,128)} %bitcast.156, f32[128,128]{1,0:T(8,128)} %bitcast.176, f32[128,128]{1,0:T(8,128)S(1)} %bitcast.150, f32[128,128]{1,0:T(8,128)} %bitcast.170, f32[128,128]{1,0:T(8,128)} %bitcast.152, f32[128,128]{1,0:T(8,128)} %bitcast.172, ...), kind=kOutput, calls=%fused_computation.41.clone.2 | convolution fusion | flops 188743680 | bytes 3866624 | tf_op jit(solution)/shard_map/while/body/eval_jaxpr/bpq,bhp->bhq/dot_general | solution.py:95
  221.3 17.4 %scatter_fusion.1 = f32[256,32,128]{2,1,0:T(8,128)} fusion(f32[256,32,128]{2,1,0:T(8,128)} %get-tuple-element.437, s32[128]{0:T(128)S(1)} %fusion.78, f32[128,32,128]{2,1,0:T(8,128)} %fusion.79), kind=kCustom, calls=%fused_computation.12.clone.1 | custom fusion | flops 524288 | bytes 6291968 | tf_op jit(solution)/shard_map/while/body/eval_jaxpr/scatter-add | solution.py:99
  242.0 17.6 %fusion.77 = f32[128,32,128]{2,1,0:T(8,128)} fusion(bf16[128,32,128]{2,1,0:T(8,128)(2,1)} %gather_fusion, f32[128,128]{1,0:T(8,128)S(1)} %bitcast.157, f32[128,128]{1,0:T(8,128)S(1)} %bitcast.177, f32[128,128]{1,0:T(8,128)S(1)} %bitcast.151, f32[128,128]{1,0:T(8,128)S(1)} %bitcast.171, f32[128,128]{1,0:T(8,128)S(1)} %bitcast.153, ...), kind=kOutput, calls=%fused_computation.42.clone.2 | convolution fusion | flops 188743680 | bytes 3866624 | tf_op jit(solution)/shard_map/while/body/eval_jaxpr/bpq,bhq->bhp/dot_general | solution.py:92
  259.7 11.7 scatter_fusion
  277.3 17.8 %fusion.79 = f32[128,32,128]{2,1,0:T(8,128)} fusion(bf16[128,32,128]{2,1,0:T(8,128)(2,1)} %gather_fusion.3, f32[128,128]{1,0:T(8,128)} %bitcast.156, f32[128,128]{1,0:T(8,128)} %bitcast.176, f32[128,128]{1,0:T(8,128)S(1)} %bitcast.150, f32[128,128]{1,0:T(8,128)} %bitcast.170, f32[128,128]{1,0:T(8,128)} %bitcast.152, f32[128,128]{1,0:T(8,128)} %bitcast.172, ...), kind=kOutput, calls=%fused_computation.41.clone.2 | convolution fusion | flops 188743680 | bytes 3866624 | tf_op jit(solution)/shard_map/while/body/eval_jaxpr/bpq,bhp->bhq/dot_general | solution.py:95
  295.9 17.4 %scatter_fusion.1 = f32[256,32,128]{2,1,0:T(8,128)} fusion(f32[256,32,128]{2,1,0:T(8,128)} %get-tuple-element.437, s32[128]{0:T(128)S(1)} %fusion.78, f32[128,32,128]{2,1,0:T(8,128)} %fusion.79), kind=kCustom, calls=%fused_computation.12.clone.1 | custom fusion | flops 524288 | bytes 6291968 | tf_op jit(solution)/shard_map/while/body/eval_jaxpr/scatter-add | solution.py:99
  316.6 17.6 %fusion.77 = f32[128,32,128]{2,1,0:T(8,128)} fusion(bf16[128,32,128]{2,1,0:T(8,128)(2,1)} %gather_fusion, f32[128,128]{1,0:T(8,128)S(1)} %bitcast.157, f32[128,128]{1,0:T(8,128)S(1)} %bitcast.177, f32[128,128]{1,0:T(8,128)S(1)} %bitcast.151, f32[128,128]{1,0:T(8,128)S(1)} %bitcast.171, f32[128,128]{1,0:T(8,128)S(1)} %bitcast.153, ...), kind=kOutput, calls=%fused_computation.42.clone.2 | convolution fusion | flops 188743680 | bytes 3866624 | tf_op jit(solution)/shard_map/while/body/eval_jaxpr/bpq,bhq->bhp/dot_general | solution.py:92
  334.3 11.7 scatter_fusion
  351.9 17.8 %fusion.79 = f32[128,32,128]{2,1,0:T(8,128)} fusion(bf16[128,32,128]{2,1,0:T(8,128)(2,1)} %gather_fusion.3, f32[128,128]{1,0:T(8,128)} %bitcast.156, f32[128,128]{1,0:T(8,128)} %bitcast.176, f32[128,128]{1,0:T(8,128)S(1)} %bitcast.150, f32[128,128]{1,0:T(8,128)} %bitcast.170, f32[128,128]{1,0:T(8,128)} %bitcast.152, f32[128,128]{1,0:T(8,128)} %bitcast.172, ...), kind=kOutput, calls=%fused_computation.41.clone.2 | convolution fusion | flops 188743680 | bytes 3866624 | tf_op jit(solution)/shard_map/while/body/eval_jaxpr/bpq,bhp->bhq/dot_general | solution.py:95
  370.5 17.4 %scatter_fusion.1 = f32[256,32,128]{2,1,0:T(8,128)} fusion(f32[256,32,128]{2,1,0:T(8,128)} %get-tuple-element.437, s32[128]{0:T(128)S(1)} %fusion.78, f32[128,32,128]{2,1,0:T(8,128)} %fusion.79), kind=kCustom, calls=%fused_computation.12.clone.1 | custom fusion | flops 524288 | bytes 6291968 | tf_op jit(solution)/shard_map/while/body/eval_jaxpr/scatter-add | solution.py:99
  391.3 17.6 %fusion.77 = f32[128,32,128]{2,1,0:T(8,128)} fusion(bf16[128,32,128]{2,1,0:T(8,128)(2,1)} %gather_fusion, f32[128,128]{1,0:T(8,128)S(1)} %bitcast.157, f32[128,128]{1,0:T(8,128)S(1)} %bitcast.177, f32[128,128]{1,0:T(8,128)S(1)} %bitcast.151, f32[128,128]{1,0:T(8,128)S(1)} %bitcast.171, f32[128,128]{1,0:T(8,128)S(1)} %bitcast.153, ...), kind=kOutput, calls=%fused_computation.42.clone.2 | convolution fusion | flops 188743680 | bytes 3866624 | tf_op jit(solution)/shard_map/while/body/eval_jaxpr/bpq,bhq->bhp/dot_general | solution.py:92
  408.9 11.7 scatter_fusion
  426.5 17.8 %fusion.79 = f32[128,32,128]{2,1,0:T(8,128)} fusion(bf16[128,32,128]{2,1,0:T(8,128)(2,1)} %gather_fusion.3, f32[128,128]{1,0:T(8,128)} %bitcast.156, f32[128,128]{1,0:T(8,128)} %bitcast.176, f32[128,128]{1,0:T(8,128)S(1)} %bitcast.150, f32[128,128]{1,0:T(8,128)} %bitcast.170, f32[128,128]{1,0:T(8,128)} %bitcast.152, f32[128,128]{1,0:T(8,128)} %bitcast.172, ...), kind=kOutput, calls=%fused_computation.41.clone.2 | convolution fusion | flops 188743680 | bytes 3866624 | tf_op jit(solution)/shard_map/while/body/eval_jaxpr/bpq,bhp->bhq/dot_general | solution.py:95
  445.1 17.4 %scatter_fusion.1 = f32[256,32,128]{2,1,0:T(8,128)} fusion(f32[256,32,128]{2,1,0:T(8,128)} %get-tuple-element.437, s32[128]{0:T(128)S(1)} %fusion.78, f32[128,32,128]{2,1,0:T(8,128)} %fusion.79), kind=kCustom, calls=%fused_computation.12.clone.1 | custom fusion | flops 524288 | bytes 6291968 | tf_op jit(solution)/shard_map/while/body/eval_jaxpr/scatter-add | solution.py:99
  465.9 17.6 %fusion.77 = f32[128,32,128]{2,1,0:T(8,128)} fusion(bf16[128,32,128]{2,1,0:T(8,128)(2,1)} %gather_fusion, f32[128,128]{1,0:T(8,128)S(1)} %bitcast.157, f32[128,128]{1,0:T(8,128)S(1)} %bitcast.177, f32[128,128]{1,0:T(8,128)S(1)} %bitcast.151, f32[128,128]{1,0:T(8,128)S(1)} %bitcast.171, f32[128,128]{1,0:T(8,128)S(1)} %bitcast.153, ...), kind=kOutput, calls=%fused_computation.42.clone.2 | convolution fusion | flops 188743680 | bytes 3866624 | tf_op jit(solution)/shard_map/while/body/eval_jaxpr/bpq,bhq->bhp/dot_general | solution.py:92
  507.4 90.0 %all-to-all-done.3 = f32[128,2,32,128]{3,2,1,0:T(8,128)} async-done(((f32[128,2,32,128]{3,2,1,0:T(8,128)}), f32[128,2,32,128]{3,2,1,0:T(8,128)}, u32[]{:S(2)}, u32[]{:S(2)}) %all-to-all-start.3) | async-done | bytes 4194336 | tf_op jit(solution)/shard_map/all_to_all | solution.py:108
  597.4 22.5 %scatter_fusion.4 = f32[64,32,128]{2,1,0:T(8,128)S(1)} fusion(f32[64,32,128]{2,1,0:T(8,128)S(1)} %get-tuple-element.508, s32[256]{0:T(256)S(1)} %reshape.418, f32[256,32,128]{2,1,0:T(8,128)} %bitcast.49), kind=kCustom, calls=%fused_computation.15 | custom fusion | flops 1048576 | bytes 12583936 | tf_op jit(solution)/shard_map/scatter-add | solution.py:109
  621.1 31.3 %all-reduce.3.cloned.1.call-done = f32[64,32,128]{2,1,0:T(8,128)} async-done(((f32[64,32,128]{2,1,0:T(8,128)}), f32[64,32,128]{2,1,0:T(8,128)}) %all-reduce.3.cloned.1.call-update) | async-done | bytes 1048592 | tf_op jit(solution)/shard_map/psum | solution.py:114
  656.5 63.9 %all_to_all.37 = bf16[128,2,32,128]{3,2,1,0:T(8,128)(2,1)} all-to-all(bf16[128,2,32,128]{3,2,1,0:T(8,128)(2,1)} %bitcast.145), channel_id=1, replica_groups=mesh['blk'=128,'grp'=2] {'blk'}, dimensions={0} | all-to-all | bytes 4194304 | tf_op jit(solution)/shard_map/all_to_all | solution.py:84
  723.0 376.2 %while.25 = (s32[]{:T(128)}, f32[64,32,128]{2,1,0:T(8,128)S(1)}, f32[256,32,128]{2,1,0:T(8,128)}, s32[5,128]{1,0:T(8,128)S(1)}, s32[5,128]{1,0:T(8,128)}, /*inde...) while((s32[]{:T(128)}, f32[64,32,128]{2,1,0:T(8,128)S(1)}, ...), condition=%wide.region_10.11_spmd, body=%wide.region_7.10_spmd.sunk | while | flops 378555392 | bytes 29576052 | solution.py:104
  729.6 17.8 %fusion.90 = f32[128,32,128]{2,1,0:T(8,128)} fusion(bf16[128,32,128]{2,1,0:T(8,128)(2,1)} %gather_fusion.7, f32[128,128]{1,0:T(8,128)} %bitcast.166, f32[128,128]{1,0:T(8,128)} %bitcast.186, f32[128,128]{1,0:T(8,128)S(1)} %bitcast.160, f32[128,128]{1,0:T(8,128)} %bitcast.180, f32[128,128]{1,0:T(8,128)} %bitcast.162, f32[128,128]{1,0:T(8,128)} %bitcast.182, ...), kind=kOutput, calls=%fused_computation.67.clone.1 | convolution fusion | flops 188743680 | bytes 3866624 | tf_op jit(solution)/shard_map/while/body/eval_jaxpr/bpq,bhp->bhq/dot_general | solution.py:95
  748.2 17.4 %scatter_fusion.3 = f32[256,32,128]{2,1,0:T(8,128)} fusion(f32[256,32,128]{2,1,0:T(8,128)} %get-tuple-element.470, s32[128]{0:T(128)S(1)} %fusion.89, f32[128,32,128]{2,1,0:T(8,128)} %fusion.90), kind=kCustom, calls=%fused_computation.14.clone.1 | custom fusion | flops 524288 | bytes 6291968 | tf_op jit(solution)/shard_map/while/body/eval_jaxpr/scatter-add | solution.py:99
  768.9 17.6 %fusion.88 = f32[128,32,128]{2,1,0:T(8,128)} fusion(bf16[128,32,128]{2,1,0:T(8,128)(2,1)} %gather_fusion.4, f32[128,128]{1,0:T(8,128)S(1)} %bitcast.167, f32[128,128]{1,0:T(8,128)S(1)} %bitcast.187, f32[128,128]{1,0:T(8,128)S(1)} %bitcast.161, f32[128,128]{1,0:T(8,128)S(1)} %bitcast.181, f32[128,128]{1,0:T(8,128)S(1)} %bitcast.163, ...), kind=kOutput, calls=%fused_computation.68.clone.1 | convolution fusion | flops 188743680 | bytes 3866624 | tf_op jit(solution)/shard_map/while/body/eval_jaxpr/bpq,bhq->bhp/dot_general | solution.py:92
  804.8 17.8 %fusion.90 = f32[128,32,128]{2,1,0:T(8,128)} fusion(bf16[128,32,128]{2,1,0:T(8,128)(2,1)} %gather_fusion.7, f32[128,128]{1,0:T(8,128)} %bitcast.166, f32[128,128]{1,0:T(8,128)} %bitcast.186, f32[128,128]{1,0:T(8,128)S(1)} %bitcast.160, f32[128,128]{1,0:T(8,128)} %bitcast.180, f32[128,128]{1,0:T(8,128)} %bitcast.162, f32[128,128]{1,0:T(8,128)} %bitcast.182, ...), kind=kOutput, calls=%fused_computation.67.clone.1 | convolution fusion | flops 188743680 | bytes 3866624 | tf_op jit(solution)/shard_map/while/body/eval_jaxpr/bpq,bhp->bhq/dot_general | solution.py:95
  823.4 17.4 %scatter_fusion.3 = f32[256,32,128]{2,1,0:T(8,128)} fusion(f32[256,32,128]{2,1,0:T(8,128)} %get-tuple-element.470, s32[128]{0:T(128)S(1)} %fusion.89, f32[128,32,128]{2,1,0:T(8,128)} %fusion.90), kind=kCustom, calls=%fused_computation.14.clone.1 | custom fusion | flops 524288 | bytes 6291968 | tf_op jit(solution)/shard_map/while/body/eval_jaxpr/scatter-add | solution.py:99
  844.1 17.6 %fusion.88 = f32[128,32,128]{2,1,0:T(8,128)} fusion(bf16[128,32,128]{2,1,0:T(8,128)(2,1)} %gather_fusion.4, f32[128,128]{1,0:T(8,128)S(1)} %bitcast.167, f32[128,128]{1,0:T(8,128)S(1)} %bitcast.187, f32[128,128]{1,0:T(8,128)S(1)} %bitcast.161, f32[128,128]{1,0:T(8,128)S(1)} %bitcast.181, f32[128,128]{1,0:T(8,128)S(1)} %bitcast.163, ...), kind=kOutput, calls=%fused_computation.68.clone.1 | convolution fusion | flops 188743680 | bytes 3866624 | tf_op jit(solution)/shard_map/while/body/eval_jaxpr/bpq,bhq->bhp/dot_general | solution.py:92
  861.8 11.7 scatter_fusion.2
  880.0 17.8 %fusion.90 = f32[128,32,128]{2,1,0:T(8,128)} fusion(bf16[128,32,128]{2,1,0:T(8,128)(2,1)} %gather_fusion.7, f32[128,128]{1,0:T(8,128)} %bitcast.166, f32[128,128]{1,0:T(8,128)} %bitcast.186, f32[128,128]{1,0:T(8,128)S(1)} %bitcast.160, f32[128,128]{1,0:T(8,128)} %bitcast.180, f32[128,128]{1,0:T(8,128)} %bitcast.162, f32[128,128]{1,0:T(8,128)} %bitcast.182, ...), kind=kOutput, calls=%fused_computation.67.clone.1 | convolution fusion | flops 188743680 | bytes 3866624 | tf_op jit(solution)/shard_map/while/body/eval_jaxpr/bpq,bhp->bhq/dot_general | solution.py:95
  898.6 17.4 %scatter_fusion.3 = f32[256,32,128]{2,1,0:T(8,128)} fusion(f32[256,32,128]{2,1,0:T(8,128)} %get-tuple-element.470, s32[128]{0:T(128)S(1)} %fusion.89, f32[128,32,128]{2,1,0:T(8,128)} %fusion.90), kind=kCustom, calls=%fused_computation.14.clone.1 | custom fusion | flops 524288 | bytes 6291968 | tf_op jit(solution)/shard_map/while/body/eval_jaxpr/scatter-add | solution.py:99
  919.3 17.6 %fusion.88 = f32[128,32,128]{2,1,0:T(8,128)} fusion(bf16[128,32,128]{2,1,0:T(8,128)(2,1)} %gather_fusion.4, f32[128,128]{1,0:T(8,128)S(1)} %bitcast.167, f32[128,128]{1,0:T(8,128)S(1)} %bitcast.187, f32[128,128]{1,0:T(8,128)S(1)} %bitcast.161, f32[128,128]{1,0:T(8,128)S(1)} %bitcast.181, f32[128,128]{1,0:T(8,128)S(1)} %bitcast.163, ...), kind=kOutput, calls=%fused_computation.68.clone.1 | convolution fusion | flops 188743680 | bytes 3866624 | tf_op jit(solution)/shard_map/while/body/eval_jaxpr/bpq,bhq->bhp/dot_general | solution.py:92
  937.0 11.7 scatter_fusion.2
  955.2 17.8 %fusion.90 = f32[128,32,128]{2,1,0:T(8,128)} fusion(bf16[128,32,128]{2,1,0:T(8,128)(2,1)} %gather_fusion.7, f32[128,128]{1,0:T(8,128)} %bitcast.166, f32[128,128]{1,0:T(8,128)} %bitcast.186, f32[128,128]{1,0:T(8,128)S(1)} %bitcast.160, f32[128,128]{1,0:T(8,128)} %bitcast.180, f32[128,128]{1,0:T(8,128)} %bitcast.162, f32[128,128]{1,0:T(8,128)} %bitcast.182, ...), kind=kOutput, calls=%fused_computation.67.clone.1 | convolution fusion | flops 188743680 | bytes 3866624 | tf_op jit(solution)/shard_map/while/body/eval_jaxpr/bpq,bhp->bhq/dot_general | solution.py:95
  973.9 17.4 %scatter_fusion.3 = f32[256,32,128]{2,1,0:T(8,128)} fusion(f32[256,32,128]{2,1,0:T(8,128)} %get-tuple-element.470, s32[128]{0:T(128)S(1)} %fusion.89, f32[128,32,128]{2,1,0:T(8,128)} %fusion.90), kind=kCustom, calls=%fused_computation.14.clone.1 | custom fusion | flops 524288 | bytes 6291968 | tf_op jit(solution)/shard_map/while/body/eval_jaxpr/scatter-add | solution.py:99
  994.6 17.6 %fusion.88 = f32[128,32,128]{2,1,0:T(8,128)} fusion(bf16[128,32,128]{2,1,0:T(8,128)(2,1)} %gather_fusion.4, f32[128,128]{1,0:T(8,128)S(1)} %bitcast.167, f32[128,128]{1,0:T(8,128)S(1)} %bitcast.187, f32[128,128]{1,0:T(8,128)S(1)} %bitcast.161, f32[128,128]{1,0:T(8,128)S(1)} %bitcast.181, f32[128,128]{1,0:T(8,128)S(1)} %bitcast.163, ...), kind=kOutput, calls=%fused_computation.68.clone.1 | convolution fusion | flops 188743680 | bytes 3866624 | tf_op jit(solution)/shard_map/while/body/eval_jaxpr/bpq,bhq->bhp/dot_general | solution.py:92
  1012.2 11.7 scatter_fusion.2
  1030.5 17.8 %fusion.90 = f32[128,32,128]{2,1,0:T(8,128)} fusion(bf16[128,32,128]{2,1,0:T(8,128)(2,1)} %gather_fusion.7, f32[128,128]{1,0:T(8,128)} %bitcast.166, f32[128,128]{1,0:T(8,128)} %bitcast.186, f32[128,128]{1,0:T(8,128)S(1)} %bitcast.160, f32[128,128]{1,0:T(8,128)} %bitcast.180, f32[128,128]{1,0:T(8,128)} %bitcast.162, f32[128,128]{1,0:T(8,128)} %bitcast.182, ...), kind=kOutput, calls=%fused_computation.67.clone.1 | convolution fusion | flops 188743680 | bytes 3866624 | tf_op jit(solution)/shard_map/while/body/eval_jaxpr/bpq,bhp->bhq/dot_general | solution.py:95
  1049.1 17.4 %scatter_fusion.3 = f32[256,32,128]{2,1,0:T(8,128)} fusion(f32[256,32,128]{2,1,0:T(8,128)} %get-tuple-element.470, s32[128]{0:T(128)S(1)} %fusion.89, f32[128,32,128]{2,1,0:T(8,128)} %fusion.90), kind=kCustom, calls=%fused_computation.14.clone.1 | custom fusion | flops 524288 | bytes 6291968 | tf_op jit(solution)/shard_map/while/body/eval_jaxpr/scatter-add | solution.py:99
  1069.8 17.6 %fusion.88 = f32[128,32,128]{2,1,0:T(8,128)} fusion(bf16[128,32,128]{2,1,0:T(8,128)(2,1)} %gather_fusion.4, f32[128,128]{1,0:T(8,128)S(1)} %bitcast.167, f32[128,128]{1,0:T(8,128)S(1)} %bitcast.187, f32[128,128]{1,0:T(8,128)S(1)} %bitcast.161, f32[128,128]{1,0:T(8,128)S(1)} %bitcast.181, f32[128,128]{1,0:T(8,128)S(1)} %bitcast.163, ...), kind=kOutput, calls=%fused_computation.68.clone.1 | convolution fusion | flops 188743680 | bytes 3866624 | tf_op jit(solution)/shard_map/while/body/eval_jaxpr/bpq,bhq->bhp/dot_general | solution.py:92
  1099.2 101.3 %all_to_all.38 = f32[128,2,32,128]{3,2,1,0:T(8,128)} all-to-all(f32[128,2,32,128]{3,2,1,0:T(8,128)} %bitcast.140), channel_id=1, replica_groups=mesh['blk'=128,'grp'=2] {'blk'}, dimensions={0} | all-to-all | bytes 8388608 | tf_op jit(solution)/shard_map/all_to_all | solution.py:108
  1200.5 22.4 %scatter_fusion.5 = f32[64,32,128]{2,1,0:T(8,128)S(1)} fusion(f32[64,32,128]{2,1,0:T(8,128)S(1)} %get-tuple-element.113, s32[256]{0:T(256)S(1)} %copy-done.33, f32[256,32,128]{2,1,0:T(8,128)} %bitcast.143), kind=kCustom, calls=%fused_computation.16 | custom fusion | flops 1048576 | bytes 12583936 | tf_op jit(solution)/shard_map/scatter-add | solution.py:109
  1223.9 31.5 %all-reduce.5.cloned.1.call-done = f32[64,32,128]{2,1,0:T(8,128)} async-done(((f32[64,32,128]{2,1,0:T(8,128)}), f32[64,32,128]{2,1,0:T(8,128)}) %all-reduce.5.cloned.1.call-update) | async-done | bytes 1048592 | tf_op jit(solution)/shard_map/psum | solution.py:114
  (391 shorter events, 207.9 us)
Async XLA Ops:
  6.5 37.8 %copy-start.28 = (f32[64,128]{1,0:T(8,128)S(1)}, f32[64,128]{1,0:T(8,128)}, u32[]{:S(2)}) copy-start(f32[64,128]{1,0:T(8,128)} %param.16) | copy-start | bytes 98308
  6.5 37.8 %copy-start.4 = (f32[64,32,128]{2,1,0:T(8,128)S(1)}, f32[64,32,128]{2,1,0:T(8,128)}, u32[]{:S(2)}) copy-start(f32[64,32,128]{2,1,0:T(8,128)} %param.14) | copy-start | bytes 3145732
  8.1 27.0 %all-to-all-start = ((s32[128,1,2]{2,1,0:T(1,128)}), s32[128,1,2]{2,1,0:T(1,128)S(1)}, u32[]{:S(2)}, u32[]{:S(2)}) async-start(s32[128,1,2]{2,1,0:T(1,128)} %bitcast.36), calls=%async_computation | async-start | bytes 131072 | tf_op jit(solution)/shard_map/all_to_all | solution.py:64
  38.1 25.8 %all-to-all-start.2 = ((f32[128,2,5,128]{3,1,2,0:T(2,128)}), f32[128,2,5,128]{3,1,2,0:T(2,128)S(1)}, u32[]{:S(2)}, u32[]{:S(2)}) async-start(f32[128,2,5,128]{3,1,2,0:T(2,128)} %copy.25), calls=%async_computation.2 | async-start | bytes 1310720 | tf_op jit(solution)/shard_map/all_to_all | solution.py:67
  63.9 55.6 %all-to-all-start.1 = ((bf16[128,2,32,128]{3,2,1,0:T(8,128)(2,1)}), bf16[128,2,32,128]{3,2,1,0:T(8,128)(2,1)}, u32[]{:S(2)}, u32[]{:S(2)}) async-start(bf16[128,2,32,128]{3,2,1,0:T(8,128)(2,1)} %bitcast.144), calls=%async_computation.1 | async-start | bytes 4194304 | tf_op jit(solution)/shard_map/all_to_all | solution.py:84
  72.9 49.2 %copy-start.31 = (s32[640]{0:T(1024)S(1)}, s32[640]{0:T(1024)}, u32[]{:S(2)}) copy-start(s32[640]{0:T(1024)} %param.21) | copy-start | bytes 7684
  72.9 49.2 %copy-start.34 = (s32[640]{0:T(1024)S(1)}, s32[640]{0:T(1024)}, u32[]{:S(2)}) copy-start(s32[640]{0:T(1024)} %param.22) | copy-start | bytes 7684
  146.6 20.7 %copy-start.12 = (f32[128,1,128]{2,1,0:T(1,128)S(1)}, f32[128,1,128]{2,1,0:T(1,128)}, u32[]{:S(2)}) copy-start(f32[128,1,128]{2,1,0:T(1,128)} %get-tuple-element.398) | copy-start | bytes 196612 | tf_op jit(solution)/shard_map/while
  146.6 20.7 %copy-start.13 = (f32[128,1,128]{2,1,0:T(1,128)S(1)}, f32[128,1,128]{2,1,0:T(1,128)}, u32[]{:S(2)}) copy-start(f32[128,1,128]{2,1,0:T(1,128)} %get-tuple-element.392) | copy-start | bytes 196612 | tf_op jit(solution)/shard_map/while
  146.6 20.7 %copy-start.14 = (f32[128,1,128]{2,1,0:T(1,128)S(1)}, f32[128,1,128]{2,1,0:T(1,128)}, u32[]{:S(2)}) copy-start(f32[128,1,128]{2,1,0:T(1,128)} %get-tuple-element.394) | copy-start | bytes 196612 | tf_op jit(solution)/shard_map/while
  146.6 20.7 %copy-start.15 = (f32[128,1,128]{2,1,0:T(1,128)S(1)}, f32[128,1,128]{2,1,0:T(1,128)}, u32[]{:S(2)}) copy-start(f32[128,1,128]{2,1,0:T(1,128)} %get-tuple-element.396) | copy-start | bytes 196612 | tf_op jit(solution)/shard_map/while
  146.7 20.7 %copy-start.16 = (f32[128,1,128]{2,1,0:T(1,128)S(1)}, f32[128,1,128]{2,1,0:T(1,128)}, u32[]{:S(2)}) copy-start(f32[128,1,128]{2,1,0:T(1,128)} %get-tuple-element.390) | copy-start | bytes 196612 | tf_op jit(solution)/shard_map/while
  221.2 20.7 %copy-start.12 = (f32[128,1,128]{2,1,0:T(1,128)S(1)}, f32[128,1,128]{2,1,0:T(1,128)}, u32[]{:S(2)}) copy-start(f32[128,1,128]{2,1,0:T(1,128)} %get-tuple-element.398) | copy-start | bytes 196612 | tf_op jit(solution)/shard_map/while
  221.2 20.7 %copy-start.13 = (f32[128,1,128]{2,1,0:T(1,128)S(1)}, f32[128,1,128]{2,1,0:T(1,128)}, u32[]{:S(2)}) copy-start(f32[128,1,128]{2,1,0:T(1,128)} %get-tuple-element.392) | copy-start | bytes 196612 | tf_op jit(solution)/shard_map/while
  221.3 20.7 %copy-start.14 = (f32[128,1,128]{2,1,0:T(1,128)S(1)}, f32[128,1,128]{2,1,0:T(1,128)}, u32[]{:S(2)}) copy-start(f32[128,1,128]{2,1,0:T(1,128)} %get-tuple-element.394) | copy-start | bytes 196612 | tf_op jit(solution)/shard_map/while
  221.3 20.7 %copy-start.15 = (f32[128,1,128]{2,1,0:T(1,128)S(1)}, f32[128,1,128]{2,1,0:T(1,128)}, u32[]{:S(2)}) copy-start(f32[128,1,128]{2,1,0:T(1,128)} %get-tuple-element.396) | copy-start | bytes 196612 | tf_op jit(solution)/shard_map/while
  221.3 20.7 %copy-start.16 = (f32[128,1,128]{2,1,0:T(1,128)S(1)}, f32[128,1,128]{2,1,0:T(1,128)}, u32[]{:S(2)}) copy-start(f32[128,1,128]{2,1,0:T(1,128)} %get-tuple-element.390) | copy-start | bytes 196612 | tf_op jit(solution)/shard_map/while
  370.4 20.8 %copy-start.6 = (f32[128,1,128]{2,1,0:T(1,128)S(1)}, f32[128,1,128]{2,1,0:T(1,128)}, u32[]{:S(2)}) copy-start(f32[128,1,128]{2,1,0:T(1,128)} %get-tuple-element.393) | copy-start | bytes 196612 | tf_op jit(solution)/shard_map/while
  370.4 20.8 %copy-start.7 = (f32[128,1,128]{2,1,0:T(1,128)S(1)}, f32[128,1,128]{2,1,0:T(1,128)}, u32[]{:S(2)}) copy-start(f32[128,1,128]{2,1,0:T(1,128)} %get-tuple-element.395) | copy-start | bytes 196612 | tf_op jit(solution)/shard_map/while
  370.4 20.8 %copy-start.8 = (f32[128,1,128]{2,1,0:T(1,128)S(1)}, f32[128,1,128]{2,1,0:T(1,128)}, u32[]{:S(2)}) copy-start(f32[128,1,128]{2,1,0:T(1,128)} %get-tuple-element.388) | copy-start | bytes 196612 | tf_op jit(solution)/shard_map/while
  370.4 20.8 %copy-start.12 = (f32[128,1,128]{2,1,0:T(1,128)S(1)}, f32[128,1,128]{2,1,0:T(1,128)}, u32[]{:S(2)}) copy-start(f32[128,1,128]{2,1,0:T(1,128)} %get-tuple-element.398) | copy-start | bytes 196612 | tf_op jit(solution)/shard_map/while
  370.5 20.8 %copy-start.13 = (f32[128,1,128]{2,1,0:T(1,128)S(1)}, f32[128,1,128]{2,1,0:T(1,128)}, u32[]{:S(2)}) copy-start(f32[128,1,128]{2,1,0:T(1,128)} %get-tuple-element.392) | copy-start | bytes 196612 | tf_op jit(solution)/shard_map/while
  370.5 20.8 %copy-start.14 = (f32[128,1,128]{2,1,0:T(1,128)S(1)}, f32[128,1,128]{2,1,0:T(1,128)}, u32[]{:S(2)}) copy-start(f32[128,1,128]{2,1,0:T(1,128)} %get-tuple-element.394) | copy-start | bytes 196612 | tf_op jit(solution)/shard_map/while
  370.5 20.8 %copy-start.15 = (f32[128,1,128]{2,1,0:T(1,128)S(1)}, f32[128,1,128]{2,1,0:T(1,128)}, u32[]{:S(2)}) copy-start(f32[128,1,128]{2,1,0:T(1,128)} %get-tuple-element.396) | copy-start | bytes 196612 | tf_op jit(solution)/shard_map/while
  370.5 20.8 %copy-start.16 = (f32[128,1,128]{2,1,0:T(1,128)S(1)}, f32[128,1,128]{2,1,0:T(1,128)}, u32[]{:S(2)}) copy-start(f32[128,1,128]{2,1,0:T(1,128)} %get-tuple-element.390) | copy-start | bytes 196612 | tf_op jit(solution)/shard_map/while
  495.2 102.1 %all-to-all-start.3 = ((f32[128,2,32,128]{3,2,1,0:T(8,128)}), f32[128,2,32,128]{3,2,1,0:T(8,128)}, u32[]{:S(2)}, u32[]{:S(2)}) async-start(f32[128,2,32,128]{3,2,1,0:T(8,128)} %bitcast.141), calls=%async_computation.3 | async-start | bytes 8388608 | tf_op jit(solution)/shard_map/all_to_all | solution.py:108
  505.9 146.5 %all-reduce.3.cloned.1.call-start = ((), (), s32[]{:S(2)}) async-start(), calls=%async_computation.6 | async-start | bytes 2097152 | tf_op jit(solution)/shard_map/psum | solution.py:114
  507.4 112.4 %copy-start.32 = (s32[256]{0:T(256)}, s32[256]{0:T(256)S(1)}, u32[]{:S(2)}) copy-start(s32[256]{0:T(256)S(1)} %reshape.418) | copy-start | bytes 3076
  597.4 23.5 %copy-start.30 = (s32[64,128]{1,0:T(8,128)S(1)}, s32[64,128]{1,0:T(8,128)}, u32[]{:S(2)}) copy-start(s32[64,128]{1,0:T(8,128)} %param.18) | copy-start | bytes 98308
  597.4 23.5 %copy-start.36 = (f32[8]{0:T(128)S(1)}, f32[8]{0:T(128)}, u32[]{:S(2)}) copy-start(f32[8]{0:T(128)} %param.19) | copy-start | bytes 100
  597.4 55.0 %copy-start.29 = (f32[64,128]{1,0:T(8,128)S(1)}, f32[64,128]{1,0:T(8,128)}, u32[]{:S(2)}) copy-start(f32[64,128]{1,0:T(8,128)} %param.16) | copy-start | bytes 98308
  597.4 56.9 %copy-start.3 = (s32[1024]{0:T(1024)S(1)}, s32[1024]{0:T(1024)}, u32[]{:S(2)}) copy-start(s32[1024]{0:T(1024)} %copy-done.2) | copy-start | bytes 12292
  620.9 634.6 %all-reduce.5.cloned.1.call-start = ((), (), s32[]{:S(2)}) async-start(), calls=%async_computation.7 | async-start | bytes 2097152 | tf_op jit(solution)/shard_map/psum | solution.py:114
  621.1 99.3 %copy-start.26 = (f32[64,128]{1,0:T(8,128)}, f32[64,128]{1,0:T(8,128)S(1)}, u32[]{:S(2)}) copy-start(f32[64,128]{1,0:T(8,128)S(1)} %select_reduce_fusion) | copy-start | bytes 98308
  823.3 20.7 %copy-start.9 = (f32[128,1,128]{2,1,0:T(1,128)S(1)}, f32[128,1,128]{2,1,0:T(1,128)}, u32[]{:S(2)}) copy-start(f32[128,1,128]{2,1,0:T(1,128)} %get-tuple-element.417) | copy-start | bytes 196612 | tf_op jit(solution)/shard_map/while
  823.3 20.7 %copy-start.10 = (f32[128,1,128]{2,1,0:T(1,128)S(1)}, f32[128,1,128]{2,1,0:T(1,128)}, u32[]{:S(2)}) copy-start(f32[128,1,128]{2,1,0:T(1,128)} %get-tuple-element.419) | copy-start | bytes 196612 | tf_op jit(solution)/shard_map/while
  823.3 20.7 %copy-start.11 = (f32[128,1,128]{2,1,0:T(1,128)S(1)}, f32[128,1,128]{2,1,0:T(1,128)}, u32[]{:S(2)}) copy-start(f32[128,1,128]{2,1,0:T(1,128)} %get-tuple-element.412) | copy-start | bytes 196612 | tf_op jit(solution)/shard_map/while
  823.3 20.7 %copy-start.17 = (f32[128,1,128]{2,1,0:T(1,128)S(1)}, f32[128,1,128]{2,1,0:T(1,128)}, u32[]{:S(2)}) copy-start(f32[128,1,128]{2,1,0:T(1,128)} %get-tuple-element.422) | copy-start | bytes 196612 | tf_op jit(solution)/shard_map/while
  823.3 20.7 %copy-start.18 = (f32[128,1,128]{2,1,0:T(1,128)S(1)}, f32[128,1,128]{2,1,0:T(1,128)}, u32[]{:S(2)}) copy-start(f32[128,1,128]{2,1,0:T(1,128)} %get-tuple-element.416) | copy-start | bytes 196612 | tf_op jit(solution)/shard_map/while
  823.4 20.7 %copy-start.19 = (f32[128,1,128]{2,1,0:T(1,128)S(1)}, f32[128,1,128]{2,1,0:T(1,128)}, u32[]{:S(2)}) copy-start(f32[128,1,128]{2,1,0:T(1,128)} %get-tuple-element.418) | copy-start | bytes 196612 | tf_op jit(solution)/shard_map/while
  823.4 20.7 %copy-start.20 = (f32[128,1,128]{2,1,0:T(1,128)S(1)}, f32[128,1,128]{2,1,0:T(1,128)}, u32[]{:S(2)}) copy-start(f32[128,1,128]{2,1,0:T(1,128)} %get-tuple-element.420) | copy-start | bytes 196612 | tf_op jit(solution)/shard_map/while
  823.4 20.7 %copy-start.21 = (f32[128,1,128]{2,1,0:T(1,128)S(1)}, f32[128,1,128]{2,1,0:T(1,128)}, u32[]{:S(2)}) copy-start(f32[128,1,128]{2,1,0:T(1,128)} %get-tuple-element.414) | copy-start | bytes 196612 | tf_op jit(solution)/shard_map/while
  1049.0 20.7 %copy-start.17 = (f32[128,1,128]{2,1,0:T(1,128)S(1)}, f32[128,1,128]{2,1,0:T(1,128)}, u32[]{:S(2)}) copy-start(f32[128,1,128]{2,1,0:T(1,128)} %get-tuple-element.422) | copy-start | bytes 196612 | tf_op jit(solution)/shard_map/while
  1049.1 20.7 %copy-start.18 = (f32[128,1,128]{2,1,0:T(1,128)S(1)}, f32[128,1,128]{2,1,0:T(1,128)}, u32[]{:S(2)}) copy-start(f32[128,1,128]{2,1,0:T(1,128)} %get-tuple-element.416) | copy-start | bytes 196612 | tf_op jit(solution)/shard_map/while
  1049.1 20.7 %copy-start.19 = (f32[128,1,128]{2,1,0:T(1,128)S(1)}, f32[128,1,128]{2,1,0:T(1,128)}, u32[]{:S(2)}) copy-start(f32[128,1,128]{2,1,0:T(1,128)} %get-tuple-element.418) | copy-start | bytes 196612 | tf_op jit(solution)/shard_map/while
  1099.2 101.3 %copy-start.33 = (s32[256]{0:T(256)S(1)}, s32[256]{0:T(256)}, u32[]{:S(2)}) copy-start(s32[256]{0:T(256)} %copy-done.32) | copy-start | bytes 3076
  1200.5 55.0 %copy-start.5 = (f32[64,32,128]{2,1,0:T(8,128)S(1)}, f32[64,32,128]{2,1,0:T(8,128)}, u32[]{:S(2)}) copy-start(f32[64,32,128]{2,1,0:T(8,128)} %param.14) | copy-start | bytes 3145732
  1200.5 55.0 %copy-start.27 = (f32[64,128]{1,0:T(8,128)S(1)}, f32[64,128]{1,0:T(8,128)}, u32[]{:S(2)}) copy-start(f32[64,128]{1,0:T(8,128)} %copy-done.26) | copy-start | bytes 98308
  (71 other events, 1318.3 us)
Sparse Core Ops, SparseCore 0:
  621.0 31.3 all-reduce.2
  1224.1 31.3 all-reduce.4
where the time goes:
time: 1270 us; the launch traced here: 1260 us
  matrix products  355 us (28%)
  other arithmetic  353 us (28%)
  waiting for transfers between devices  225 us (18%)
  blocking collectives  165 us (13%)
  local copies, waits for them, and re-layouts  109 us (9%)
  starting transfers between devices  42.3 us (3%)
  between operations  13.7 us (1%)
    dot_general x10, matrix products, accumulate(): jnp.einsum('bpq,bhp->bhq', form_tile, exitance[row_ids], preferred_elemen...  178 us
    dot_general x10, matrix products, accumulate(): jnp.einsum('bpq,bhq->bhp', form_tile, fetched[slot_ids], preferred_elemen...  176 us
    scatter-add x10, other arithmetic, accumulate(): jax.ops.segment_sum(to_cols, slot_ids, num_segments=slot_count)  174 us
    scatter-add x10, other arithmetic, accumulate(): jax.ops.segment_sum(to_rows, row_ids, num_segments=blk_dev)  117 us
    all_to_all x1, blocking collectives, local(): lax.all_to_all(outgoing, 'blk', split_axis=0, concat_axis=0, tiled=True)  101 us
    all_to_all x1, waiting for transfers between devices, local(): lax.all_to_all(outgoing, 'blk', split_axis=0, concat_axis=0, tiled=True)  90 us
    all_to_all x1, blocking collectives, local(): lax.all_to_all(exitance[requests], 'blk', split_axis=0, concat_axis=0, ti...  63.9 us
    psum x2, waiting for transfers between devices, local(): irradiance = lax.psum(to_local + received, 'grp')  62.8 us
  transfers between devices with their start and end apart: 6, of which 6 were waited for; matrix products, arithmetic and copies ran while one was open for 1% of the time, Pallas kernels for 0%

commit v1 on v0

v1 whole, which is shorter than its diff:
```python
import math

import jax
import jax.numpy as jnp
import numpy as np
from jax import lax
from jax.experimental import pallas as pl
from jax.experimental.pallas import tpu as pltpu
from jax.sharding import PartitionSpec as P

BLOCK = 128
NCLASS = 8
HASH = 747796405
FEATURES = 32
UNROLL = 16
DEPTH = 8
VMEM = 48 * 1024 * 1024

SPARE = 64 | (128 << 7)


def hash_pattern():
    at = (np.arange(BLOCK * BLOCK, dtype=np.uint64) * HASH) & 0xFFFFFFFF
    odd = (at >> 2) ^ (at >> 6) ^ (at >> 7) ^ (at >> 11)
    word = (((at >> 14) << 21) + ((odd & 1) << 31)) & 0xFFFFFFFF
    return word.astype(np.uint32).astype(np.int32).reshape(BLOCK, BLOCK)


def row_of(word):
    return word & 127


def slot_of(word):
    return lax.shift_right_logical(word, jnp.int32(7)) & 255


def list_kernel(words_ref, list_ref, steps_ref):
    total = words_ref.shape[0]

    def take(turn, count):
        for j in range(8):
            word = words_ref[turn * 8 + j]
            list_ref[count] = word
            count = count + 1 - (lax.shift_right_logical(word, jnp.int32(6)) & 1)
        return count

    count = lax.fori_loop(0, total // 8, take, jnp.int32(0))
    for j in range(UNROLL):
        list_ref[count + j] = jnp.int32(SPARE)
    steps_ref[0] = jnp.maximum((count + UNROLL - 1) // UNROLL, 1)


def pair_list(words):
    total = words.shape[0]
    smem = pl.BlockSpec(memory_space=pltpu.SMEM)
    return pl.pallas_call(
        list_kernel,
        out_shape=(
            jax.ShapeDtypeStruct((total + UNROLL,), jnp.int32),
            jax.ShapeDtypeStruct((1,), jnp.int32),
        ),
        in_specs=[smem],
        out_specs=(smem, smem),
        cost_estimate=pl.CostEstimate(flops=10_000_000, bytes_accessed=10_000_000, transcendentals=0),
    )(words)


def encode(acc, out_ref):
    def one(slot, carry):
        value = acc[slot]
        top = jnp.max(value, axis=0, keepdims=True)
        exponent = jnp.ceil(jnp.log2(jnp.maximum(top, 1e-30)))
        level = jnp.minimum(jnp.round(value * jnp.exp2(15.0 - exponent)), 32767.0).astype(jnp.int32)
        biased = exponent.astype(jnp.int32) + 128
        places = lax.broadcasted_iota(jnp.int32, value.shape, 0)
        mark = jnp.where(places < 8, lax.shift_right_logical(biased, jnp.minimum(places, 8)) & 1, 0)
        out_ref[slot] = (level ^ -mark).astype(jnp.int16)
        return carry

    lax.fori_loop(0, out_ref.shape[0], one, 0, unroll=4)


def decode(code):
    code = code.astype(jnp.int32)
    head = code[:8]
    places = lax.broadcasted_iota(jnp.int32, head.shape, 0)
    bits = jnp.where(head < 0, jnp.left_shift(jnp.ones_like(head), places), 0).astype(jnp.float32)
    biased = jnp.sum(bits, axis=0, keepdims=True)
    level = code ^ lax.shift_right_arithmetic(code, jnp.full_like(code, 31))
    return level.astype(jnp.float32) * jnp.exp2(biased - (128.0 + 15.0))


def tile_copy(tiles_ref, held, sems, step, out):
    buffer = lax.rem(step, DEPTH)
    away = tiles_ref.at[pl.ds(step * UNROLL, UNROLL)]
    here = held.at[buffer]
    source, target = (here, away) if out else (away, here)
    return pltpu.make_async_copy(source, target, sems.at[buffer])


def build_kernel(
    list_ref, steps_ref, pattern_ref, near_ref, far_ref, ex_ref, tiles_ref, out_ref, acc, held, sems
):
    steps = steps_ref[0]
    acc[...] = jnp.zeros_like(acc)

    def turn(step, carry):
        buffer = lax.rem(step, DEPTH)

        @pl.when(step >= DEPTH)
        def _():
            tile_copy(tiles_ref, held, sems, step - DEPTH, True).wait()

        for j in range(UNROLL):
            word = list_ref[step * UNROLL + j]
            row, slot = row_of(word) & 63, slot_of(word)
            shift = jnp.left_shift(lax.shift_right_logical(word, jnp.int32(15)) * jnp.int32(HASH), 21)
            scaled = jnp.dot(near_ref[row], far_ref[slot & 127], preferred_element_type=jnp.float32)
            mixed = pattern_ref[...] + shift
            mixed = mixed ^ jnp.left_shift(mixed, 5)
            tile = jnp.where(mixed < 0, pl.reciprocal(scaled, approx=True), 0.0).astype(jnp.bfloat16)
            held[buffer, j] = tile
            acc[slot] += jnp.dot(ex_ref[row], tile, preferred_element_type=jnp.float32)
        tile_copy(tiles_ref, held, sems, step, True).start()
        return carry

    lax.fori_loop(0, steps, turn, 0)
    encode(acc, out_ref)

    def drain(step, carry):
        tile_copy(tiles_ref, held, sems, step, True).wait()
        return carry

    lax.fori_loop(jnp.maximum(steps - DEPTH, 0), steps, drain, 0)


def stream(steps, tiles_ref, held, sems, use):
    def fetch(step, carry):
        tile_copy(tiles_ref, held, sems, step, False).start()
        return carry

    lax.fori_loop(0, jnp.minimum(steps, DEPTH - 1), fetch, 0)

    def turn(step, carry):
        @pl.when(step + DEPTH - 1 < steps)
        def _():
            fetch(step + DEPTH - 1, 0)

        tile_copy(tiles_ref, held, sems, step, False).wait()
        use(step, lax.rem(step, DEPTH))
        return carry

    lax.fori_loop(0, steps, turn, 0)


def columns_kernel(list_ref, steps_ref, tiles_ref, ex_ref, out_ref, acc, held, sems):
    acc[...] = jnp.zeros_like(acc)

    def use(step, buffer):
        for j in range(UNROLL):
            word = list_ref[step * UNROLL + j]
            row, slot = row_of(word) & 63, slot_of(word)
            acc[slot] += jnp.dot(ex_ref[row], held[buffer, j], preferred_element_type=jnp.float32)

    stream(steps_ref[0], tiles_ref, held, sems, use)
    encode(acc, out_ref)


def rows_kernel(list_ref, steps_ref, tiles_ref, ex_ref, out_ref, held, sems):
    out_ref[...] = jnp.zeros_like(out_ref)

    def use(step, buffer):
        for j in range(UNROLL):
            word = list_ref[step * UNROLL + j]
            row, slot = row_of(word), slot_of(word) & 127
            out_ref[row] += lax.dot_general(
                ex_ref[slot], held[buffer, j], (((1,), (1,)), ((), ())),
                preferred_element_type=jnp.float32,
            )

    stream(steps_ref[0], tiles_ref, held, sems, use)


SMEM_SPEC = pl.BlockSpec(memory_space=pltpu.SMEM)
VMEM_SPEC = pl.BlockSpec(memory_space=pltpu.VMEM)
ANY_SPEC = pl.BlockSpec(memory_space=pl.ANY)
HELD = pltpu.VMEM((DEPTH, UNROLL, BLOCK, BLOCK), jnp.bfloat16)
SEMS = pltpu.SemaphoreType.DMA((DEPTH,))


def build(pairs, steps, pattern, near, far, exitance, pair_max):
    slots, hours = far.shape[0], exitance.shape[1]
    return pl.pallas_call(
        build_kernel,
        in_specs=[SMEM_SPEC] * 2 + [VMEM_SPEC] * 4,
        out_specs=[ANY_SPEC, VMEM_SPEC],
        out_shape=[
            jax.ShapeDtypeStruct((pair_max, BLOCK, BLOCK), jnp.bfloat16),
            jax.ShapeDtypeStruct((slots, hours, BLOCK), jnp.int16),
        ],
        scratch_shapes=[pltpu.VMEM((slots + 1, hours, BLOCK), jnp.float32), HELD, SEMS],
        compiler_params=pltpu.CompilerParams(vmem_limit_bytes=VMEM),
        cost_estimate=pl.CostEstimate(
            flops=20_000_000_000, bytes_accessed=60_000_000, transcendentals=10_000_000
        ),
    )(pairs, steps, pattern, near, far, exitance)


def columns(pairs, steps, tiles, exitance, slots):
    hours = exitance.shape[1]
    return pl.pallas_call(
        columns_kernel,
        in_specs=[SMEM_SPEC] * 2 + [ANY_SPEC, VMEM_SPEC],
        out_specs=VMEM_SPEC,
        out_shape=jax.ShapeDtypeStruct((slots, hours, BLOCK), jnp.int16),
        scratch_shapes=[pltpu.VMEM((slots + 1, hours, BLOCK), jnp.float32), HELD, SEMS],
        compiler_params=pltpu.CompilerParams(vmem_limit_bytes=VMEM),
        cost_estimate=pl.CostEstimate(flops=10_000_000_000, bytes_accessed=40_000_000, transcendentals=0),
    )(pairs, steps, tiles, exitance)


def rows(pairs, steps, tiles, fetched, row_blocks):
    hours = fetched.shape[1]
    return pl.pallas_call(
        rows_kernel,
        in_specs=[SMEM_SPEC] * 2 + [ANY_SPEC, VMEM_SPEC],
        out_specs=VMEM_SPEC,
        out_shape=jax.ShapeDtypeStruct((row_blocks + 1, hours, BLOCK), jnp.float32),
        scratch_shapes=[HELD, SEMS],
        compiler_params=pltpu.CompilerParams(vmem_limit_bytes=VMEM),
        cost_estimate=pl.CostEstimate(flops=10_000_000_000, bytes_accessed=40_000_000, transcendentals=0),
    )(pairs, steps, tiles, fetched)


def gather_into(acc, mine_ref, other_ref, got_ref, got_other_ref, asked_ref, asked_other_ref):
    blocks = acc.shape[0]
    acc[...] = mine_ref[:blocks] + other_ref[:blocks]

    def add(at, carry):
        for asked, got in ((asked_ref, got_ref), (asked_other_ref, got_other_ref)):
            acc[asked[at]] += decode(got[at])
        return carry

    lax.fori_loop(0, got_ref.shape[0], add, 0, unroll=4)


def middle_kernel(
    asked_ref, asked_other_ref, mine_ref, other_ref, got_ref, got_other_ref,
    emission_ref, albedo_ref, area_ref, ex_ref, send_ref, acc,
):
    gather_into(acc, mine_ref, other_ref, got_ref, got_other_ref, asked_ref, asked_other_ref)
    ex_ref[...] = (area_ref[...] * (emission_ref[...] + albedo_ref[...] * acc[...])).astype(jnp.bfloat16)

    def put(at, carry):
        send_ref[at] = ex_ref[asked_ref[at]]
        return carry

    lax.fori_loop(0, send_ref.shape[0], put, 0, unroll=8)


def last_kernel(
    asked_ref, asked_other_ref, mine_ref, other_ref, got_ref, got_other_ref,
    emission_ref, albedo_ref, out_ref, acc,
):
    gather_into(acc, mine_ref, other_ref, got_ref, got_other_ref, asked_ref, asked_other_ref)
    out_ref[...] = emission_ref[...] + albedo_ref[...] * acc[...]


def update(kernel, asked, asked_other, arrays, out_shape):
    smem, vmem = pl.BlockSpec(memory_space=pltpu.SMEM), pl.BlockSpec(memory_space=pltpu.VMEM)
    blocks, hours, block = arrays[4].shape
    return pl.pallas_call(
        kernel,
        in_specs=[smem, smem] + [vmem] * len(arrays),
        out_specs=jax.tree.map(lambda _: vmem, out_shape),
        out_shape=out_shape,
        scratch_shapes=[pltpu.VMEM((blocks, hours, block), jnp.float32)],
        compiler_params=pltpu.CompilerParams(vmem_limit_bytes=VMEM),
    )(asked, asked_other, *arrays)


def three_parts(value):
    top = lax.reduce_precision(value, 8, 7)
    value = value - top
    middle = lax.reduce_precision(value, 8, 7)
    return top, middle, lax.reduce_precision(value - middle, 8, 7)


def features(geometry, near):
    x, y, z = (geometry[:, i] - 3.0 for i in range(3))
    unit = (math.pi if near else 1.0) / geometry[:, 4]
    norm = unit * (x * x + y * y + z * z + geometry[:, 3])
    if near:
        terms = (norm, unit, -2.0 * unit * x, -2.0 * unit * y, -2.0 * unit * z)
        order = (0, 0, 1, 1, 0, 2)
    else:
        terms = (unit, norm, unit * x, unit * y, unit * z)
        order = (0, 1, 0, 1, 2, 0)
    columns_ = []
    for term in terms:
        parts = three_parts(term)
        columns_ += [parts[i] for i in order]
    columns_ += [jnp.zeros_like(x)] * (FEATURES - len(columns_))
    return jnp.stack(columns_, axis=1).astype(jnp.bfloat16)


def local(
    emission, positions, patch_area, facing, albedo_class, albedo_table, fetch_block,
    pair_rows, pair_slots, pair_code,
):
    blocks, hours = emission.shape[:2]
    owners = lax.axis_size("blk")
    core = lax.axis_index("grp")

    def exchange(array):
        return lax.all_to_all(array, "blk", split_axis=0, concat_axis=0, tiled=True)

    def swap(array):
        return lax.ppermute(array, "grp", [(0, 1), (1, 0)])

    wanted = lax.dynamic_slice_in_dim(fetch_block.reshape(owners, 2), core, 1, axis=1)
    asked = exchange(wanted.reshape(owners, 1, 1)).reshape(owners)
    asked_other = swap(asked)
    mine = jnp.stack([pair_rows, pair_slots, pair_code])
    pair_row, pair_slot, code = jnp.concatenate([mine, swap(mine)], axis=1)
    skip = (pair_slot & 1) ^ core
    words = pair_row | (skip << 6) | ((pair_slot >> 1) << 7) | jnp.left_shift(code, 15)
    pairs, steps = pair_list(words)

    geometry = jnp.stack([positions[0], positions[1], positions[2], patch_area, facing], axis=1)
    near = features(geometry, True).transpose(0, 2, 1)
    geometry_slots = exchange(geometry.reshape(blocks, 1, 5 * BLOCK)[asked])
    exitance = (patch_area[:, None, :] * emission).astype(jnp.bfloat16)
    send = exitance[asked]
    send, geometry_slots = lax.optimization_barrier((send, geometry_slots))
    far = features(geometry_slots.reshape(owners, 5, BLOCK), False)

    class_ids = jnp.arange(NCLASS, dtype=jnp.int32)
    albedo = jnp.sum(
        jnp.where(albedo_class[..., None] == class_ids, albedo_table, jnp.float32(0.0)), axis=-1
    )[:, None, :]
    area = patch_area[:, None, :]

    fetched = exchange(send)
    tiles, back = build(
        pairs, steps, jnp.asarray(hash_pattern()), near, far, exitance, 2 * pair_rows.shape[0]
    )
    back, fetched = lax.optimization_barrier((back, fetched))
    got = exchange(back)
    to_rows = rows(pairs, steps, tiles, fetched, blocks)
    to_rows_other = swap(to_rows)
    exitance, send = update(
        middle_kernel, asked, asked_other,
        (to_rows, to_rows_other, got, swap(got), emission, albedo, area),
        [
            jax.ShapeDtypeStruct((blocks, hours, BLOCK), jnp.bfloat16),
            jax.ShapeDtypeStruct((owners, hours, BLOCK), jnp.bfloat16),
        ],
    )

    fetched = exchange(send)
    back = columns(pairs, steps, tiles, exitance, owners)
    back, fetched = lax.optimization_barrier((back, fetched))
    got = exchange(back)
    to_rows = rows(pairs, steps, tiles, fetched, blocks)
    to_rows_other = swap(to_rows)
    return update(
        last_kernel, asked, asked_other,
        (to_rows, to_rows_other, got, swap(got), emission, albedo),
        jax.ShapeDtypeStruct((blocks, hours, BLOCK), jnp.float32),
    )


def solution(mesh):
    in_specs = (
        P("blk", None, None),
        P(None, "blk", None),
        P("blk", None),
        P("blk", None),
        P("blk", None),
        P(),
        P("blk"),
        P(("blk", "grp")),
        P(("blk", "grp")),
        P(("blk", "grp")),
    )
    out_specs = P("blk", None, None)
    return jax.shard_map(local, mesh=mesh, in_specs=in_specs, out_specs=out_specs, check_vma=False)
```

time: 1270 us -> 340 us (0.27)
  matrix products: 355 us -> 0 us
  other arithmetic: 353 us -> 6.04 us
  waiting for transfers between devices: 225 us -> 38.8 us
  blocking collectives: 165 us -> 0 us
  Pallas kernels: 0 us -> 87.7 us
  starting transfers between devices: 42.3 us -> 81.2 us
  between operations: 13.7 us -> 0.35 us
    dot_general x20 -> x0, matrix products: 355 us -> none  [the longest x10 178 us: accumulate(): jnp.einsum('bpq,bhp->bhq', form_tile, exitance[row_ids], preferred_elemen...]
    scatter-add x22 -> x0, other arithmetic: 336 us -> none  [the longest x10 174 us: accumulate(): jax.ops.segment_sum(to_cols, slot_ids, num_segments=slot_count)]
    all_to_all x2 -> x0, blocking collectives: 165 us -> none  [the longest x1 101 us: local(): lax.all_to_all(outgoing, 'blk', split_axis=0, concat_axis=0, tiled=True)]
    all_to_all x4 -> x6, waiting for transfers between devices: 162 us -> 34 us  [exchange(): return lax.all_to_all(array, 'blk', split_axis=0, concat_axis=0, tiled=True)]
    another operation x5 -> x22, local copies, waits for them, and re-layouts: 5.4 us -> 104 us  [the longest x9 83.2 us: features(): return jnp.stack(columns_, axis=1).astype(jnp.bfloat16)]
    pallas_call x0 -> x7, Pallas kernels: none -> 87.7 us  [the longest x2 36.3 us: rows(): pl.pallas_call(rows_kernel, in_specs=[SMEM_SPEC] * 2 + [ANY_SPEC, VMEM_SP...]
    gather x44 -> x3, local copies, waits for them, and re-layouts: 70.8 us -> 3.54 us  [the longest x2 1.88 us: local(): geometry_slots = exchange(geometry.reshape(blocks, 1, 5 * BLOCK)[asked])]
    psum x2 -> x0, waiting for transfers between devices: 62.8 us -> none  [local(): irradiance = lax.psum(to_local + received, 'grp')]
  transfers between devices with their start and end apart: 6 -> 12, of which waited for: 6 -> 7; matrix products, arithmetic and copies ran while one was open for 1% -> 35% of each run, Pallas kernels for 0% -> 24%
where the time goes in v1:
time: 340 us; the launch traced here: 333 us
  local copies, waits for them, and re-layouts  119 us (35%)
  Pallas kernels  87.7 us (26%)
  starting transfers between devices  81.2 us (24%)
  waiting for transfers between devices  38.8 us (11%)
  other arithmetic  6.04 us (2%)
    another operation x9, local copies, waits for them, and re-layouts, features(): return jnp.stack(columns_, axis=1).astype(jnp.bfloat16)  83.2 us
    all_to_all x6, starting transfers between devices, exchange(): return lax.all_to_all(array, 'blk', split_axis=0, concat_axis=0, tiled=True)  61.4 us
    pallas_call x2, Pallas kernels, rows(): pl.pallas_call(rows_kernel, in_specs=[SMEM_SPEC] * 2 + [ANY_SPEC, VMEM_SP...  36.3 us
    all_to_all x6, waiting for transfers between devices, exchange(): return lax.all_to_all(array, 'blk', split_axis=0, concat_axis=0, tiled=True)  34 us
    pallas_call x1, Pallas kernels, build(): pl.pallas_call(build_kernel, in_specs=[SMEM_SPEC] * 2 + [VMEM_SPEC] * 4,...  23.9 us
    ppermute x6, starting transfers between devices, swap(): return lax.ppermute(array, 'grp', [(0, 1), (1, 0)])  19.9 us
    another operation x10, local copies, waits for them, and re-layouts  18.5 us
    pallas_call x1, Pallas kernels, columns(): pl.pallas_call(columns_kernel, in_specs=[SMEM_SPEC] * 2 + [ANY_SPEC, VMEM...  15.1 us
  transfers between devices with their start and end apart: 12, of which 7 were waited for; matrix products, arithmetic and copies ran while one was open for 35% of the time, Pallas kernels for 24%

profile of v1, /device:TPU:1, one launch (start us, length us, event | category | flops | bytes accessed | tf_op | source)
XLA Modules:
  0.0 333.1 jit_solution(5786799152413620140)
XLA Ops:
  2.1 3.3 collective-permute-start.1
  7.0 13.8 %all-to-all-start = ((s32[128,1,1]{2,1,0:T(1,128)}), s32[128,1,1]{2,1,0:T(1,128)S(1)}, u32[]{:S(2)}, u32[]{:S(2)}) async-start(s32[128,1,1]{2,1,0:T(1,128)} %bitcast), calls=%async_computation | async-start | bytes 131072 | tf_op jit(solution)/shard_map/all_to_all | solution.py:316
  22.6 8.8 %all-to-all-done = s32[128,1,1]{2,1,0:T(1,128)S(1)} async-done(((s32[128,1,1]{2,1,0:T(1,128)}), s32[128,1,1]{2,1,0:T(1,128)S(1)}, u32[]{:S(2)}, u32[]{:S(2)}) %all-to-all-start) | async-done | bytes 544 | tf_op jit(solution)/shard_map/all_to_all | solution.py:316
  31.4 2.3 reduce.asked_ref
  34.7 1.1 copy.275
  35.7 6.4 %all-to-all-start.1 = ((f32[128,1,640]{2,1,0:T(1,128)}), f32[128,1,640]{2,1,0:T(1,128)S(1)}, u32[]{:S(2)}, u32[]{:S(2)}) async-start(f32[128,1,640]{2,1,0:T(1,128)} %copy.275), calls=%async_computation.1 | async-start | bytes 655360 | tf_op jit(solution)/shard_map/all_to_all | solution.py:316
  42.4 1.9 copy.245
  44.2 1.9 copy.272
  46.1 1.8 copy.243
  47.9 1.8 copy.269
  49.8 1.9 copy.263
  51.7 1.9 copy.266
  53.5 1.8 copy.257
  55.4 1.8 copy.260
  57.2 1.8 copy.255
  59.0 1.8 copy.261
  60.9 1.9 copy.248
  62.8 1.9 copy.267
  64.6 1.9 copy.249
  66.5 1.9 copy.251
  68.4 1.8 copy.254
  70.2 1.8 stack.147
  72.0 62.9 %stack.148 = bf16[64,32,128]{1,2,0:T(8,128)(2,1)} concatenate(bf16[64,1,128]{1,2,0:T(8,128)(2,1)} %copy.243, bf16[64,1,128]{1,2,0:T(8,128)(2,1)} %copy.243, bf16[64,1,128]{1,2,0:T(8,128)(2,1)} %copy.245, bf16[64,1,128]{1,2,0:T(8,128)(2,1)} %copy.245, bf16[64,1,128]{1,2,0:T(8,128)(2,1)} %copy.243, bf16[64,1,128]{1,2,0:T(8,128)(2,1)} %copy.248, bf16[64,1,128]{1,2,0:T(8,128)(2,1)} %copy.249, ...), dimensions={1} | concatenate | bytes 1048576 | tf_op jit(solution)/shard_map/stack | solution.py:304
  134.9 1.7 gather_fusion
  137.2 4.6 %shard_map.109 = (s32[1296]{0:T(1024)}, s32[1]{0:T(128)}) custom-call(s32[1280]{0:T(1024)} %fusion.42.words_ref), custom_call_target="tpu_custom_call" | custom-call | flops 10000000 | bytes 10000000 | tf_op jit(solution)/shard_map/pallas_call | solution.py:56
  142.8 13.0 %all-to-all-start.2 = ((bf16[128,32,128]{2,1,0:T(8,128)(2,1)}), bf16[128,32,128]{2,1,0:T(8,128)(2,1)S(1)}, u32[]{:S(2)}, u32[]{:S(2)}) async-start(bf16[128,32,128]{2,1,0:T(8,128)(2,1)} %gather_fusion), calls=%async_computation.2 | async-start | bytes 2097152 | tf_op jit(solution)/shard_map/all_to_all | solution.py:316
  157.6 2.4 reduce-precision_convert_fusion
  160.8 8.6 %stack.152.far_ref = bf16[128,32,128]{2,1,0:T(8,128)(2,1)} concatenate(bf16[128,1,128]{2,1,0:T(2,128)(2,1)S(1)} %get-tuple-element.66, bf16[128,1,128]{2,1,0:T(2,128)(2,1)S(1)} %get-tuple-element.65, bf16[128,1,128]{2,1,0:T(2,128)(2,1)S(1)} %get-tuple-element.66, bf16[128,1,128]{2,1,0:T(2,128)(2,1)S(1)} %get-tuple-element.65, bf16[128,1,128]{2,1,0:T(2,128)(2,1)} %get-tuple-element.64, ...), dimensions={1} | concatenate | bytes 2097152 | tf_op jit(solution)/shard_map/stack | solution.py:304
  169.4 1.6 copy-done.1
  171.0 1.2 copy-done.2
  172.2 23.9 %shard_map.110 = (bf16[1280,128,128]{2,1,0:T(8,128)(2,1)}, s16[128,32,128]{2,1,0:T(8,128)(2,1)S(1)}) custom-call(s32[1296]{0:T(1024)S(1)} %copy-done.8, s32[1]{0:T(128)} %get-tuple-element.18.steps_ref, s32[128,128]{1,0:T(8,128)S(1)} %copy-done.9, bf16[64,128,32]{2,1,0:T(8,128)(2,1)S(1)} %bitcast.95, bf16[128,32,128]{2,1,0:T(8,128)(2,1)S(1)} %copy-done.2, ...), custom_call_target="tpu_custom_call" | custom-call | flops 20000000000 | bytes 60000000 | tf_op jit(solution)/shard_map/pallas_call | solution.py:193
  197.2 14.2 %all-to-all-start.3 = ((s16[128,32,128]{2,1,0:T(8,128)(2,1)}), s16[128,32,128]{2,1,0:T(8,128)(2,1)}, u32[]{:S(2)}, u32[]{:S(2)}) async-start(s16[128,32,128]{2,1,0:T(8,128)(2,1)} %copy-done.3), calls=%async_computation.3 | async-start | bytes 2097152 | tf_op jit(solution)/shard_map/all_to_all | solution.py:316
  211.4 18.2 %shard_map.111.mine_ref = f32[65,32,128]{2,1,0:T(8,128)S(1)} custom-call(s32[1296]{0:T(1024)S(1)} %copy-done.8, s32[1]{0:T(128)} %get-tuple-element.18.steps_ref, bf16[1280,128,128]{2,1,0:T(8,128)(2,1)} %get-tuple-element.20.tiles_ref, bf16[128,32,128]{2,1,0:T(8,128)(2,1)S(1)} %all-to-all-done.2.ex_ref), custom_call_target="tpu_custom_call" | custom-call | flops 10000000000 | bytes 40000000 | tf_op jit(solution)/shard_map/pallas_call | solution.py:224
  229.6 3.3 collective-permute-start.2
  232.8 4.9 %all-to-all-done.3.got_ref = s16[128,32,128]{2,1,0:T(8,128)(2,1)} async-done(((s16[128,32,128]{2,1,0:T(8,128)(2,1)}), s16[128,32,128]{2,1,0:T(8,128)(2,1)}, u32[]{:S(2)}, u32[]{:S(2)}) %all-to-all-start.3) | async-done | bytes 1048608 | tf_op jit(solution)/shard_map/all_to_all | solution.py:316
  237.7 5.4 %collective-permute-start.3 = (s16[128,32,128]{2,1,0:T(8,128)(2,1)}, s16[128,32,128]{2,1,0:T(8,128)(2,1)S(1)}, u32[]{:S(2)}, u32[]{:S(2)}) collective-permute-start(s16[128,32,128]{2,1,0:T(8,128)(2,1)} %all-to-all-done.3.got_ref), channel_id=1, source_target_pairs={{0,1},{1,0},{2,3},{3,2},{4,5},{5,4},{6,7},{7,6},{8,9},{9,8},{10,11... | collective-permute-start | bytes 3145736 | tf_op jit(solution)/shard_map/ppermute | solution.py:319
  243.3 2.0 collective-permute-done.asked_other_ref
  245.7 3.6 %shard_map.112 = (bf16[64,32,128]{2,1,0:T(8,128)(2,1)S(1)}, bf16[128,32,128]{2,1,0:T(8,128)(2,1)S(1)}) custom-call(s32[128]{0:T(128)S(1)} %reduce.asked_ref, s32[128]{0:T(128)S(1)} %collective-permute-done.asked_other_ref, f32[65,32,128]{2,1,0:T(8,128)S(1)} %shard_map.111.mine_ref, f32[65,32,128]{2,1,0:T(8,128)} %collective-permute-done.2.other_ref, ...), custom_call_target="tpu_custom_call" | custom-call | tf_op jit(solution)/shard_map/pallas_call | solution.py:272
  251.1 6.3 %all-to-all-start.4 = ((bf16[128,32,128]{2,1,0:T(8,128)(2,1)}), bf16[128,32,128]{2,1,0:T(8,128)(2,1)S(1)}, u32[]{:S(2)}, u32[]{:S(2)}) async-start(bf16[128,32,128]{2,1,0:T(8,128)(2,1)} %copy-done.4), calls=%async_computation.4 | async-start | bytes 2097152 | tf_op jit(solution)/shard_map/all_to_all | solution.py:316
  257.4 15.1 %shard_map.113 = s16[128,32,128]{2,1,0:T(8,128)(2,1)} custom-call(s32[1296]{0:T(1024)S(1)} %copy-done.8, s32[1]{0:T(128)} %get-tuple-element.18.steps_ref, bf16[1280,128,128]{2,1,0:T(8,128)(2,1)} %get-tuple-element.20.tiles_ref, bf16[64,32,128]{2,1,0:T(8,128)(2,1)S(1)} %copy-done.6), custom_call_target="tpu_custom_call" | custom-call | flops 10000000000 | bytes 40000000 | tf_op jit(solution)/shard_map/pallas_call | solution.py:211
  272.5 14.5 %all-to-all-done.4.ex_ref = bf16[128,32,128]{2,1,0:T(8,128)(2,1)S(1)} async-done(((bf16[128,32,128]{2,1,0:T(8,128)(2,1)}), bf16[128,32,128]{2,1,0:T(8,128)(2,1)S(1)}, u32[]{:S(2)}, u32[]{:S(2)}) %all-to-all-start.4) | async-done | bytes 1048608 | tf_op jit(solution)/shard_map/all_to_all | solution.py:316
  287.0 7.7 %all-to-all-start.5 = ((s16[128,32,128]{2,1,0:T(8,128)(2,1)}), s16[128,32,128]{2,1,0:T(8,128)(2,1)}, u32[]{:S(2)}, u32[]{:S(2)}) async-start(s16[128,32,128]{2,1,0:T(8,128)(2,1)} %shard_map.113), calls=%async_computation.5 | async-start | bytes 2097152 | tf_op jit(solution)/shard_map/all_to_all | solution.py:316
  294.7 18.1 %shard_map.114.mine_ref = f32[65,32,128]{2,1,0:T(8,128)S(1)} custom-call(s32[1296]{0:T(1024)S(1)} %copy-done.8, s32[1]{0:T(128)} %get-tuple-element.18.steps_ref, bf16[1280,128,128]{2,1,0:T(8,128)(2,1)} %get-tuple-element.20.tiles_ref, bf16[128,32,128]{2,1,0:T(8,128)(2,1)S(1)} %all-to-all-done.4.ex_ref), custom_call_target="tpu_custom_call" | custom-call | flops 10000000000 | bytes 40000000 | tf_op jit(solution)/shard_map/pallas_call | solution.py:224
  312.9 2.8 collective-permute-start.4
  315.6 5.8 %all-to-all-done.5.got_ref = s16[128,32,128]{2,1,0:T(8,128)(2,1)} async-done(((s16[128,32,128]{2,1,0:T(8,128)(2,1)}), s16[128,32,128]{2,1,0:T(8,128)(2,1)}, u32[]{:S(2)}, u32[]{:S(2)}) %all-to-all-start.5) | async-done | bytes 1048608 | tf_op jit(solution)/shard_map/all_to_all | solution.py:316
  321.4 5.1 %collective-permute-start.5 = (s16[128,32,128]{2,1,0:T(8,128)(2,1)}, s16[128,32,128]{2,1,0:T(8,128)(2,1)S(1)}, u32[]{:S(2)}, u32[]{:S(2)}) collective-permute-start(s16[128,32,128]{2,1,0:T(8,128)(2,1)} %all-to-all-done.5.got_ref), channel_id=1, source_target_pairs={{0,1},{1,0},{2,3},{3,2},{4,5},{5,4},{6,7},{7,6},{8,9},{9,8},{10,11... | collective-permute-start | bytes 3145736 | tf_op jit(solution)/shard_map/ppermute | solution.py:319
  326.5 2.5 collective-permute-done.5.got_other_ref
  329.0 4.1 %shard_map.115 = f32[64,32,128]{2,1,0:T(8,128)} custom-call(s32[128]{0:T(128)S(1)} %reduce.asked_ref, s32[128]{0:T(128)S(1)} %collective-permute-done.asked_other_ref, f32[65,32,128]{2,1,0:T(8,128)S(1)} %shard_map.114.mine_ref, f32[65,32,128]{2,1,0:T(8,128)S(1)} %collective-permute-done.4.other_ref, s16[128,32,128]{2,1,0:T(8,128)(2,1)} %all-to-all-done.5.got_ref, ...), custom_call_target="tpu_custom_call" | custom-call | tf_op jit(solution)/shard_map/pallas_call | solution.py:272
  (61 shorter events, 13.9 us)
Async XLA Ops:
  2.1 134.5 %collective-permute-start.1 = (s32[3,640]{1,0:T(4,128)S(1)}, s32[3,640]{1,0:T(4,128)S(1)}, u32[]{:S(2)}, u32[]{:S(2)}) collective-permute-start(s32[3,640]{1,0:T(4,128)S(1)} %pad_add_fusion), channel_id=1, source_target_pairs={{0,1},{1,0},{2,3},{3,2},{4,5},{5,4},{6,7},{7,6},{8,9},{9,8},{10,11... | collective-permute-start | bytes 23048 | tf_op jit(solution)/shard_map/ppermute | solution.py:319
  7.0 24.5 %all-to-all-start = ((s32[128,1,1]{2,1,0:T(1,128)}), s32[128,1,1]{2,1,0:T(1,128)S(1)}, u32[]{:S(2)}, u32[]{:S(2)}) async-start(s32[128,1,1]{2,1,0:T(1,128)} %bitcast), calls=%async_computation | async-start | bytes 131072 | tf_op jit(solution)/shard_map/all_to_all | solution.py:316
  33.8 8.3 %copy-start.7 = (f32[64,128]{1,0:T(8,128)S(1)}, f32[64,128]{1,0:T(8,128)}, u32[]{:S(2)}) copy-start(f32[64,128]{1,0:T(8,128)} %param.13) | copy-start | bytes 98308
  33.8 8.3 %copy-start.10 = (f32[3,64,128]{2,1,0:T(8,128)S(1)}, f32[3,64,128]{2,1,0:T(8,128)}, u32[]{:S(2)}) copy-start(f32[3,64,128]{2,1,0:T(8,128)} %param.12) | copy-start | bytes 294916
  33.8 8.3 %copy-start.11 = (f32[64,128]{1,0:T(8,128)S(1)}, f32[64,128]{1,0:T(8,128)}, u32[]{:S(2)}) copy-start(f32[64,128]{1,0:T(8,128)} %param.14) | copy-start | bytes 98308
  33.8 8.4 %copy-start = (f32[64,32,128]{2,1,0:T(8,128)S(1)}, f32[64,32,128]{2,1,0:T(8,128)}, u32[]{:S(2)}) copy-start(f32[64,32,128]{2,1,0:T(8,128)} %emission_ref.3) | copy-start | bytes 3145732
  35.7 106.1 %all-to-all-start.1 = ((f32[128,1,640]{2,1,0:T(1,128)}), f32[128,1,640]{2,1,0:T(1,128)S(1)}, u32[]{:S(2)}, u32[]{:S(2)}) async-start(f32[128,1,640]{2,1,0:T(1,128)} %copy.275), calls=%async_computation.1 | async-start | bytes 655360 | tf_op jit(solution)/shard_map/all_to_all | solution.py:316
  142.8 54.4 %all-to-all-start.2 = ((bf16[128,32,128]{2,1,0:T(8,128)(2,1)}), bf16[128,32,128]{2,1,0:T(8,128)(2,1)S(1)}, u32[]{:S(2)}, u32[]{:S(2)}) async-start(bf16[128,32,128]{2,1,0:T(8,128)(2,1)} %gather_fusion), calls=%async_computation.2 | async-start | bytes 2097152 | tf_op jit(solution)/shard_map/all_to_all | solution.py:316
  157.6 11.8 %copy-start.8 = (s32[1296]{0:T(1024)S(1)}, s32[1296]{0:T(1024)}, u32[]{:S(2)}) copy-start(s32[1296]{0:T(1024)} %get-tuple-element.17.list_ref) | copy-start | bytes 15556
  157.6 11.8 %copy-start.9 = (s32[128,128]{1,0:T(8,128)S(1)}, s32[128,128]{1,0:T(8,128)}, u32[]{:S(2)}) copy-start(s32[128,128]{1,0:T(8,128)} %constant.42.clone.pattern_ref) | copy-start | bytes 196612
  169.4 1.6 copy-start.1
  171.0 1.2 copy-start.2
  196.2 1.0 copy-start.3
  197.2 40.6 %all-to-all-start.3 = ((s16[128,32,128]{2,1,0:T(8,128)(2,1)}), s16[128,32,128]{2,1,0:T(8,128)(2,1)}, u32[]{:S(2)}, u32[]{:S(2)}) async-start(s16[128,32,128]{2,1,0:T(8,128)(2,1)} %copy-done.3), calls=%async_computation.3 | async-start | bytes 2097152 | tf_op jit(solution)/shard_map/all_to_all | solution.py:316
  211.4 31.8 %copy-start.12 = (s32[64,128]{1,0:T(8,128)S(1)}, s32[64,128]{1,0:T(8,128)}, u32[]{:S(2)}) copy-start(s32[64,128]{1,0:T(8,128)} %param.15) | copy-start | bytes 98308
  211.4 31.8 %copy-start.13 = (f32[8]{0:T(128)S(1)}, f32[8]{0:T(128)}, u32[]{:S(2)}) copy-start(f32[8]{0:T(128)} %param.16) | copy-start | bytes 100
  229.6 15.7 %collective-permute-start.2 = (f32[65,32,128]{2,1,0:T(8,128)S(1)}, f32[65,32,128]{2,1,0:T(8,128)}, u32[]{:S(2)}, u32[]{:S(2)}) collective-permute-start(f32[65,32,128]{2,1,0:T(8,128)S(1)} %shard_map.111.mine_ref), channel_id=1, source_target_pairs={{0,1},{1,0},{2,3},{3,2},{4,5},{5,4},{6,7},{7,6},{8,9},{9,8},{10,11... | collective-permute-start | bytes 3194888 | tf_op jit(solution)/shard_map/ppermute | solution.py:319
  237.7 7.9 %collective-permute-start.3 = (s16[128,32,128]{2,1,0:T(8,128)(2,1)}, s16[128,32,128]{2,1,0:T(8,128)(2,1)S(1)}, u32[]{:S(2)}, u32[]{:S(2)}) collective-permute-start(s16[128,32,128]{2,1,0:T(8,128)(2,1)} %all-to-all-done.3.got_ref), channel_id=1, source_target_pairs={{0,1},{1,0},{2,3},{3,2},{4,5},{5,4},{6,7},{7,6},{8,9},{9,8},{10,11... | collective-permute-start | bytes 3145736 | tf_op jit(solution)/shard_map/ppermute | solution.py:319
  243.2 2.1 collective-permute-start
  249.3 1.0 copy-start.4
  250.3 0.8 copy-start.5
  251.1 6.3 %copy-start.6 = (bf16[64,32,128]{2,1,0:T(8,128)(2,1)S(1)}, bf16[64,32,128]{2,1,0:T(8,128)(2,1)}, u32[]{:S(2)}) copy-start(bf16[64,32,128]{2,1,0:T(8,128)(2,1)} %copy-done.5) | copy-start | bytes 1572868
  251.1 35.9 %all-to-all-start.4 = ((bf16[128,32,128]{2,1,0:T(8,128)(2,1)}), bf16[128,32,128]{2,1,0:T(8,128)(2,1)S(1)}, u32[]{:S(2)}, u32[]{:S(2)}) async-start(bf16[128,32,128]{2,1,0:T(8,128)(2,1)} %copy-done.4), calls=%async_computation.4 | async-start | bytes 2097152 | tf_op jit(solution)/shard_map/all_to_all | solution.py:316
  287.0 34.4 %all-to-all-start.5 = ((s16[128,32,128]{2,1,0:T(8,128)(2,1)}), s16[128,32,128]{2,1,0:T(8,128)(2,1)}, u32[]{:S(2)}, u32[]{:S(2)}) async-start(s16[128,32,128]{2,1,0:T(8,128)(2,1)} %shard_map.113), calls=%async_computation.5 | async-start | bytes 2097152 | tf_op jit(solution)/shard_map/all_to_all | solution.py:316
  312.9 13.6 %collective-permute-start.4 = (f32[65,32,128]{2,1,0:T(8,128)S(1)}, f32[65,32,128]{2,1,0:T(8,128)S(1)}, u32[]{:S(2)}, u32[]{:S(2)}) collective-permute-start(f32[65,32,128]{2,1,0:T(8,128)S(1)} %shard_map.114.mine_ref), channel_id=1, source_target_pairs={{0,1},{1,0},{2,3},{3,2},{4,5},{5,4},{6,7},{7,6},{8,9},{9,8},{10,11... | collective-permute-start | bytes 3194888 | tf_op jit(solution)/shard_map/ppermute | solution.py:319
  321.4 7.6 %collective-permute-start.5 = (s16[128,32,128]{2,1,0:T(8,128)(2,1)}, s16[128,32,128]{2,1,0:T(8,128)(2,1)S(1)}, u32[]{:S(2)}, u32[]{:S(2)}) collective-permute-start(s16[128,32,128]{2,1,0:T(8,128)(2,1)} %all-to-all-done.5.got_ref), channel_id=1, source_target_pairs={{0,1},{1,0},{2,3},{3,2},{4,5},{5,4},{6,7},{7,6},{8,9},{9,8},{10,11... | collective-permute-start | bytes 3145736 | tf_op jit(solution)/shard_map/ppermute | solution.py:319

commit v2 on v1

--- a/solution.py
+++ b/solution.py
@@ -14,7 +14,10 @@
 FEATURES = 32
 UNROLL = 16
 DEPTH = 8
-VMEM = 48 * 1024 * 1024
+VMEM = 60 * 1024 * 1024
+SMEM_SPEC = pl.BlockSpec(memory_space=pltpu.SMEM)
+VMEM_SPEC = pl.BlockSpec(memory_space=pltpu.VMEM)
+ANY_SPEC = pl.BlockSpec(memory_space=pl.ANY)
 
 SPARE = 64 | (128 << 7)
 
@@ -52,15 +55,14 @@
 
 def pair_list(words):
     total = words.shape[0]
-    smem = pl.BlockSpec(memory_space=pltpu.SMEM)
     return pl.pallas_call(
         list_kernel,
         out_shape=(
             jax.ShapeDtypeStruct((total + UNROLL,), jnp.int32),
             jax.ShapeDtypeStruct((1,), jnp.int32),
         ),
-        in_specs=[smem],
-        out_specs=(smem, smem),
+        in_specs=[SMEM_SPEC],
+        out_specs=(SMEM_SPEC, SMEM_SPEC),
         cost_estimate=pl.CostEstimate(flops=10_000_000, bytes_accessed=10_000_000, transcendentals=0),
     )(words)
 
@@ -181,9 +183,6 @@
     stream(steps_ref[0], tiles_ref, held, sems, use)
 
 
-SMEM_SPEC = pl.BlockSpec(memory_space=pltpu.SMEM)
-VMEM_SPEC = pl.BlockSpec(memory_space=pltpu.VMEM)
-ANY_SPEC = pl.BlockSpec(memory_space=pl.ANY)
 HELD = pltpu.VMEM((DEPTH, UNROLL, BLOCK, BLOCK), jnp.bfloat16)
 SEMS = pltpu.SemaphoreType.DMA((DEPTH,))
 
@@ -238,7 +237,7 @@
 
     def add(at, carry):
         for asked, got in ((asked_ref, got_ref), (asked_other_ref, got_other_ref)):
-            acc[asked[at]] += decode(got[at])
+            acc[asked[at, 0]] += decode(got[at])
         return carry
 
     lax.fori_loop(0, got_ref.shape[0], add, 0, unroll=4)
@@ -252,7 +251,7 @@
     ex_ref[...] = (area_ref[...] * (emission_ref[...] + albedo_ref[...] * acc[...])).astype(jnp.bfloat16)
 
     def put(at, carry):
-        send_ref[at] = ex_ref[asked_ref[at]]
+        send_ref[at] = ex_ref[asked_ref[at, 0]]
         return carry
 
     lax.fori_loop(0, send_ref.shape[0], put, 0, unroll=8)
@@ -267,41 +266,141 @@
 
 
 def update(kernel, asked, asked_other, arrays, out_shape):
-    smem, vmem = pl.BlockSpec(memory_space=pltpu.SMEM), pl.BlockSpec(memory_space=pltpu.VMEM)
     blocks, hours, block = arrays[4].shape
     return pl.pallas_call(
         kernel,
-        in_specs=[smem, smem] + [vmem] * len(arrays),
-        out_specs=jax.tree.map(lambda _: vmem, out_shape),
+        in_specs=[SMEM_SPEC] * 2 + [VMEM_SPEC] * len(arrays),
+        out_specs=jax.tree.map(lambda _: VMEM_SPEC, out_shape),
         out_shape=out_shape,
         scratch_shapes=[pltpu.VMEM((blocks, hours, block), jnp.float32)],
-        compiler_params=pltpu.CompilerParams(vmem_limit_bytes=VMEM),
+        compiler_params=pltpu.CompilerParams(vmem_limit_bytes=VMEM // 4),
     )(asked, asked_other, *arrays)
 
 
-def three_parts(value):
-    top = lax.reduce_precision(value, 8, 7)
-    value = value - top
-    middle = lax.reduce_precision(value, 8, 7)
-    return top, middle, lax.reduce_precision(value - middle, 8, 7)
-
-
-def features(geometry, near):
-    x, y, z = (geometry[:, i] - 3.0 for i in range(3))
-    unit = (math.pi if near else 1.0) / geometry[:, 4]
-    norm = unit * (x * x + y * y + z * z + geometry[:, 3])
+def ask_kernel(core_ref, fetch_ref, out_ref):
+    core = core_ref[0]
+    for owner in range(out_ref.shape[0]):
+        out_ref[owner] = jnp.full((1, BLOCK), fetch_ref[2 * owner + core], jnp.int32)
+
+
+def ask(core, fetch_block, owners):
+    return pl.pallas_call(
+        ask_kernel,
+        in_specs=[SMEM_SPEC] * 2,
+        out_specs=VMEM_SPEC,
+        out_shape=jax.ShapeDtypeStruct((owners, 1, BLOCK), jnp.int32),
+    )(core.reshape(1), fetch_block)
+
+
+def place_kernel(asked_ref, positions_ref, area_ref, facing_ref, out_ref):
+    def put(at, carry):
+        block = pl.ds(asked_ref[at, 0], 1)
+        for i in range(3):
+            out_ref[at, :, i * BLOCK : (i + 1) * BLOCK] = positions_ref[i, block, :]
+        out_ref[at, :, 3 * BLOCK : 4 * BLOCK] = area_ref[block, :]
+        out_ref[at, :, 4 * BLOCK : 5 * BLOCK] = facing_ref[block, :]
+        return carry
+
+    lax.fori_loop(0, out_ref.shape[0], put, 0, unroll=8)
+
+
+def place(asked, positions, patch_area, facing):
+    return pl.pallas_call(
+        place_kernel,
+        in_specs=[SMEM_SPEC] + [VMEM_SPEC] * 3,
+        out_specs=VMEM_SPEC,
+        out_shape=jax.ShapeDtypeStruct((asked.shape[0], 1, 5 * BLOCK), jnp.float32),
+        compiler_params=pltpu.CompilerParams(vmem_limit_bytes=VMEM),
+    )(asked, positions, patch_area, facing)
+
+
+def first_kernel(asked_ref, emission_ref, area_ref, ex_ref, send_ref):
+    ex_ref[...] = (area_ref[...] * emission_ref[...]).astype(jnp.bfloat16)
+
+    def put(at, carry):
+        send_ref[at] = ex_ref[asked_ref[at, 0]]
+        return carry
+
+    lax.fori_loop(0, send_ref.shape[0], put, 0, unroll=8)
+
+
+def first(asked, emission, area):
+    blocks, hours, block = emission.shape
+    return pl.pallas_call(
+        first_kernel,
+        in_specs=[SMEM_SPEC] + [VMEM_SPEC] * 2,
+        out_specs=[VMEM_SPEC] * 2,
+        out_shape=[
+            jax.ShapeDtypeStruct((blocks, hours, block), jnp.bfloat16),
+            jax.ShapeDtypeStruct((asked.shape[0], hours, block), jnp.bfloat16),
+        ],
+        compiler_params=pltpu.CompilerParams(vmem_limit_bytes=VMEM),
+        cost_estimate=pl.CostEstimate(flops=1_000_000, bytes_accessed=4_000_000, transcendentals=0),
+    )(asked, emission, area)
+
+
+def factor_rows(x, y, z, area, facing, near):
+    x, y, z = x - 3.0, y - 3.0, z - 3.0
+    unit = (math.pi if near else 1.0) / facing
+    norm = unit * (x * x + y * y + z * z + area)
     if near:
         terms = (norm, unit, -2.0 * unit * x, -2.0 * unit * y, -2.0 * unit * z)
         order = (0, 0, 1, 1, 0, 2)
     else:
         terms = (unit, norm, unit * x, unit * y, unit * z)
         order = (0, 1, 0, 1, 2, 0)
-    columns_ = []
+    found = []
     for term in terms:
-        parts = three_parts(term)
-        columns_ += [parts[i] for i in order]
-    columns_ += [jnp.zeros_like(x)] * (FEATURES - len(columns_))
-    return jnp.stack(columns_, axis=1).astype(jnp.bfloat16)
+        parts = []
+        for _ in range(3):
+            part = term.astype(jnp.bfloat16).astype(jnp.float32)
+            parts.append(part)
+            term = term - part
+        found += [parts[i] for i in order]
+    return found + [jnp.zeros_like(x)] * (FEATURES - len(found))
+
+
+def factor_blocks(read, count, turned, near, put):
+    def group(at, carry):
+        for i, feature in enumerate(factor_rows(*read(pl.ds(pl.multiple_of(at * 8, 8), 8)), near)):
+            turned[8 * i : 8 * i + 8, :] = feature
+        for i in range(8):
+            put(at * 8 + i, turned[pl.ds(i, FEATURES, stride=8), :])
+        return carry
+
+    lax.fori_loop(0, count // 8, group, 0)
+
+
+def near_kernel(positions_ref, area_ref, facing_ref, out_ref, turned):
+    def read(at):
+        return [positions_ref[i, at, :] for i in range(3)] + [area_ref[at, :], facing_ref[at, :]]
+
+    def put(at, block):
+        out_ref[at] = block.T.astype(jnp.bfloat16)
+
+    factor_blocks(read, out_ref.shape[0], turned, True, put)
+
+
+def far_kernel(geometry_ref, out_ref, turned):
+    def read(at):
+        return [geometry_ref[at, 0, i * BLOCK : (i + 1) * BLOCK] for i in range(5)]
+
+    def put(at, block):
+        out_ref[at] = block.astype(jnp.bfloat16)
+
+    factor_blocks(read, out_ref.shape[0], turned, False, put)
+
+
+def factors(kernel, arrays, shape):
+    return pl.pallas_call(
+        kernel,
+        in_specs=[VMEM_SPEC] * len(arrays),
+        out_specs=VMEM_SPEC,
+        out_shape=jax.ShapeDtypeStruct(shape, jnp.bfloat16),
+        scratch_shapes=[pltpu.VMEM((8 * FEATURES, BLOCK), jnp.float32)],
+        compiler_params=pltpu.CompilerParams(vmem_limit_bytes=VMEM),
+        cost_estimate=pl.CostEstimate(flops=10_000_000, bytes_accessed=8_000_000, transcendentals=0),
+    )(*arrays)
 
 
 def local(
@@ -318,34 +417,31 @@
     def swap(array):
         return lax.ppermute(array, "grp", [(0, 1), (1, 0)])
 
-    wanted = lax.dynamic_slice_in_dim(fetch_block.reshape(owners, 2), core, 1, axis=1)
-    asked = exchange(wanted.reshape(owners, 1, 1)).reshape(owners)
-    asked_other = swap(asked)
+    asked = exchange(ask(core, fetch_block, owners)).reshape(owners, BLOCK)
     mine = jnp.stack([pair_rows, pair_slots, pair_code])
     pair_row, pair_slot, code = jnp.concatenate([mine, swap(mine)], axis=1)
     skip = (pair_slot & 1) ^ core
     words = pair_row | (skip << 6) | ((pair_slot >> 1) << 7) | jnp.left_shift(code, 15)
     pairs, steps = pair_list(words)
-
-    geometry = jnp.stack([positions[0], positions[1], positions[2], patch_area, facing], axis=1)
-    near = features(geometry, True).transpose(0, 2, 1)
-    geometry_slots = exchange(geometry.reshape(blocks, 1, 5 * BLOCK)[asked])
-    exitance = (patch_area[:, None, :] * emission).astype(jnp.bfloat16)
-    send = exitance[asked]
-    send, geometry_slots = lax.optimization_barrier((send, geometry_slots))
-    far = features(geometry_slots.reshape(owners, 5, BLOCK), False)
+    area = patch_area[:, None, :]
+
+    near = factors(near_kernel, (positions, patch_area, facing), (blocks, BLOCK, FEATURES))
+    asked, near, pairs, steps = lax.optimization_barrier((asked, near, pairs, steps))
+    geometry = exchange(place(asked, positions, patch_area, facing))
+    asked_other = swap(asked)
+    exitance, send = first(asked, emission, area)
+    send, geometry = lax.optimization_barrier((send, geometry))
+    far = factors(far_kernel, (geometry,), (owners, FEATURES, BLOCK))
 
     class_ids = jnp.arange(NCLASS, dtype=jnp.int32)
     albedo = jnp.sum(
         jnp.where(albedo_class[..., None] == class_ids, albedo_table, jnp.float32(0.0)), axis=-1
     )[:, None, :]
-    area = patch_area[:, None, :]
 
     fetched = exchange(send)
     tiles, back = build(
         pairs, steps, jnp.asarray(hash_pattern()), near, far, exitance, 2 * pair_rows.shape[0]
     )
-    back, fetched = lax.optimization_barrier((back, fetched))
     got = exchange(back)
     to_rows = rows(pairs, steps, tiles, fetched, blocks)
     to_rows_other = swap(to_rows)
@@ -360,7 +456,6 @@
 
     fetched = exchange(send)
     back = columns(pairs, steps, tiles, exitance, owners)
-    back, fetched = lax.optimization_barrier((back, fetched))
     got = exchange(back)
     to_rows = rows(pairs, steps, tiles, fetched, blocks)
     to_rows_other = swap(to_rows)

time: 340 us -> 242 us (0.71); the launches traced: 333 us -> 241 us
  local copies, waits for them, and re-layouts: 119 us -> 6.93 us
  Pallas kernels: 87.7 us -> 113 us
  other arithmetic: 6.04 us -> 0.8 us
    another operation x20 -> x0, local copies, waits for them, and re-layouts: 103 us -> none  [the longest x9 83.2 us: features(): return jnp.stack(columns_, axis=1).astype(jnp.bfloat16)]
    pallas_call x2 -> x7, Pallas kernels: 7.75 us -> 25.2 us  [the longest x2 10.3 us: update(): pl.pallas_call(kernel, in_specs=[SMEM_SPEC] * 2 + [VMEM_SPEC] * len(array...]
    pallas_call x2, Pallas kernels: 36.3 us -> 40.6 us  [rows(): pl.pallas_call(rows_kernel, in_specs=[SMEM_SPEC] * 2 + [ANY_SPEC, VMEM_SP...]
    all_to_all x6, starting transfers between devices: 61.4 us -> 65.4 us  [exchange(): return lax.all_to_all(array, 'blk', split_axis=0, concat_axis=0, tiled=True)]
    gather x3 -> x0, local copies, waits for them, and re-layouts: 3.54 us -> none  [the longest x2 1.88 us: local(): geometry_slots = exchange(geometry.reshape(blocks, 1, 5 * BLOCK)[asked])]
    unnamed x34 -> x26, local copies, waits for them, and re-layouts: 7.97 us -> 4.86 us
  transfers between devices with their start and end apart: 12 -> 12, of which waited for: 7 -> 6; matrix products, arithmetic and copies ran while one was open for 35% -> 1% of each run, Pallas kernels for 24% -> 41%
where the time goes in v2:
time: 242 us; the launch traced here: 241 us
  Pallas kernels  113 us (47%)
  starting transfers between devices  83.6 us (35%)
  waiting for transfers between devices  36.6 us (15%)
  local copies, waits for them, and re-layouts  6.93 us (3%)
    all_to_all x6, starting transfers between devices, exchange(): return lax.all_to_all(array, 'blk', split_axis=0, concat_axis=0, tiled=True)  65.4 us
    pallas_call x2, Pallas kernels, rows(): pl.pallas_call(rows_kernel, in_specs=[SMEM_SPEC] * 2 + [ANY_SPEC, VMEM_SP...  40.6 us
    all_to_all x6, waiting for transfers between devices, exchange(): return lax.all_to_all(array, 'blk', split_axis=0, concat_axis=0, tiled=True)  32.1 us
    pallas_call x1, Pallas kernels, build(): pl.pallas_call(build_kernel, in_specs=[SMEM_SPEC] * 2 + [VMEM_SPEC] * 4,...  26.8 us
    ppermute x6, starting transfers between devices, swap(): return lax.ppermute(array, 'grp', [(0, 1), (1, 0)])  18.2 us
    pallas_call x1, Pallas kernels, columns(): pl.pallas_call(columns_kernel, in_specs=[SMEM_SPEC] * 2 + [ANY_SPEC, VMEM...  15.9 us
    pallas_call x2, Pallas kernels, update(): pl.pallas_call(kernel, in_specs=[SMEM_SPEC] * 2 + [VMEM_SPEC] * len(array...  10.3 us
    pallas_call x2, Pallas kernels, factors(): pl.pallas_call(kernel, in_specs=[VMEM_SPEC] * len(arrays), out_specs=VMEM...  7.37 us
  transfers between devices with their start and end apart: 12, of which 6 were waited for; matrix products, arithmetic and copies ran while one was open for 1% of the time, Pallas kernels for 41%

profile of v2, /device:TPU:1, one launch (start us, length us, event | category | flops | bytes accessed | tf_op | source)
XLA Modules:
  0.0 241.4 jit_solution(6126262217129579264)
XLA Ops:
  0.0 1.4 shard_map.109
  1.4 16.3 %all-to-all-start = ((s32[128,1,128]{2,1,0:T(1,128)}), s32[128,1,128]{2,1,0:T(1,128)S(1)}, u32[]{:S(2)}, u32[]{:S(2)}) async-start(s32[128,1,128]{2,1,0:T(1,128)} %shard_map.109), calls=%async_computation | async-start | bytes 131072 | tf_op jit(solution)/shard_map/all_to_all | solution.py:415
  17.7 0.7 stack.12
  18.4 0.7 stack.13
  19.1 0.7 stack.14
  19.8 1.0 collective-permute-start
  20.9 3.6 %shard_map.110.near_ref = bf16[64,128,32]{2,1,0:T(8,128)(2,1)} custom-call(f32[3,64,128]{2,1,0:T(8,128)} %positions_ref.3, f32[64,128]{1,0:T(8,128)} %area_ref.3, f32[64,128]{1,0:T(8,128)} %facing_ref.3), custom_call_target="tpu_custom_call" | custom-call | flops 10000000 | bytes 8000000 | tf_op jit(solution)/shard_map/pallas_call | solution.py:395
  24.5 0.6 fusion.3.words_ref
  25.1 4.6 %shard_map.111 = (s32[1296]{0:T(1024)}, s32[1]{0:T(128)}) custom-call(s32[1280]{0:T(1024)} %fusion.3.words_ref), custom_call_target="tpu_custom_call" | custom-call | flops 10000000 | bytes 10000000 | tf_op jit(solution)/shard_map/pallas_call | solution.py:58
  29.8 0.6 copy-done.3
  30.4 3.0 %shard_map.113 = f32[128,1,640]{2,1,0:T(1,128)} custom-call(s32[128,128]{1,0:T(8,128)} %bitcast.4, f32[3,64,128]{2,1,0:T(8,128)} %positions_ref.3, f32[64,128]{1,0:T(8,128)} %area_ref.3, f32[64,128]{1,0:T(8,128)} %facing_ref.3), custom_call_target="tpu_custom_call" | custom-call | tf_op jit(solution)/shard_map/pallas_call | solution.py:308
  33.4 13.5 %all-to-all-start.1 = ((f32[128,1,640]{2,1,0:T(1,128)}), f32[128,1,640]{2,1,0:T(1,128)S(1)}, u32[]{:S(2)}, u32[]{:S(2)}) async-start(f32[128,1,640]{2,1,0:T(1,128)} %shard_map.113), calls=%async_computation.1 | async-start | bytes 655360 | tf_op jit(solution)/shard_map/all_to_all | solution.py:415
  46.9 3.1 %shard_map.112 = (bf16[64,32,128]{2,1,0:T(8,128)(2,1)}, bf16[128,32,128]{2,1,0:T(8,128)(2,1)}) custom-call(s32[128,128]{1,0:T(8,128)} %bitcast.5, f32[64,32,128]{2,1,0:T(8,128)} %emission_ref.5, f32[64,1,128]{2,1,0:T(1,128)} %bitcast.9), custom_call_target="tpu_custom_call" | custom-call | flops 1000000 | bytes 4000000 | tf_op jit(solution)/shard_map/pallas_call | solution.py:329
  50.0 12.3 %all-to-all-done.1.geometry_ref = f32[128,1,640]{2,1,0:T(1,128)S(1)} async-done(((f32[128,1,640]{2,1,0:T(1,128)}), f32[128,1,640]{2,1,0:T(1,128)S(1)}, u32[]{:S(2)}, u32[]{:S(2)}) %all-to-all-start.1) | async-done | bytes 327712 | tf_op jit(solution)/shard_map/all_to_all | solution.py:415
  62.4 6.2 %all-to-all-start.2 = ((bf16[128,32,128]{2,1,0:T(8,128)(2,1)}), bf16[128,32,128]{2,1,0:T(8,128)(2,1)S(1)}, u32[]{:S(2)}, u32[]{:S(2)}) async-start(bf16[128,32,128]{2,1,0:T(8,128)(2,1)} %get-tuple-element.29), calls=%async_computation.2 | async-start | bytes 2097152 | tf_op jit(solution)/shard_map/all_to_all | solution.py:415
  68.6 3.8 %shard_map.114.far_ref = bf16[128,32,128]{2,1,0:T(8,128)(2,1)} custom-call(f32[128,1,640]{2,1,0:T(1,128)} %copy-done.10), custom_call_target="tpu_custom_call" | custom-call | flops 10000000 | bytes 8000000 | tf_op jit(solution)/shard_map/pallas_call | solution.py:395
  72.3 26.8 %shard_map.115 = (bf16[1280,128,128]{2,1,0:T(8,128)(2,1)}, s16[128,32,128]{2,1,0:T(8,128)(2,1)}) custom-call(s32[1296]{0:T(1024)} %get-tuple-element.22.list_ref, s32[1]{0:T(128)} %get-tuple-element.23.steps_ref, s32[128,128]{1,0:T(8,128)} %constant.16.clone.pattern_ref, bf16[64,128,32]{2,1,0:T(8,128)(2,1)} %shard_map.110.near_ref, ...), custom_call_target="tpu_custom_call" | custom-call | flops 20000000000 | bytes 60000000 | tf_op jit(solution)/shard_map/pallas_call | solution.py:192
  99.2 0.0 all-to-all-done.2.ex_ref
  99.2 0.0 copy-start.8
  99.2 12.7 %all-to-all-start.3 = ((s16[128,32,128]{2,1,0:T(8,128)(2,1)}), s16[128,32,128]{2,1,0:T(8,128)(2,1)S(1)}, u32[]{:S(2)}, u32[]{:S(2)}) async-start(s16[128,32,128]{2,1,0:T(8,128)(2,1)} %get-tuple-element.30), calls=%async_computation.3 | async-start | bytes 2097152 | tf_op jit(solution)/shard_map/all_to_all | solution.py:415
  111.9 0.0 copy-start.11
  112.0 0.0 copy-start.12
  112.0 0.0 copy-start
  112.0 0.0 copy-start.7
  112.0 20.3 %shard_map.116.mine_ref = f32[65,32,128]{2,1,0:T(8,128)} custom-call(s32[1296]{0:T(1024)} %get-tuple-element.22.list_ref, s32[1]{0:T(128)} %get-tuple-element.23.steps_ref, bf16[1280,128,128]{2,1,0:T(8,128)(2,1)} %get-tuple-element.28.tiles_ref, bf16[128,32,128]{2,1,0:T(8,128)(2,1)} %copy-done.8), custom_call_target="tpu_custom_call" | custom-call | flops 10000000000 | bytes 40000000 | tf_op jit(solution)/shard_map/pallas_call | solution.py:223
  132.3 4.3 %collective-permute-start.2 = (f32[65,32,128]{2,1,0:T(8,128)}, f32[65,32,128]{2,1,0:T(8,128)S(1)}, u32[]{:S(2)}, u32[]{:S(2)}) collective-permute-start(f32[65,32,128]{2,1,0:T(8,128)} %shard_map.116.mine_ref), channel_id=1, source_target_pairs={{0,1},{1,0},{2,3},{3,2},{4,5},{5,4},{6,7},{7,6},{8,9},{9,8},{10,11... | collective-permute-start | bytes 3194888 | tf_op jit(solution)/shard_map/ppermute | solution.py:418
  136.7 0.3 all-to-all-done.3.got_ref
  136.9 7.2 %collective-permute-start.3 = (s16[128,32,128]{2,1,0:T(8,128)(2,1)S(1)}, s16[128,32,128]{2,1,0:T(8,128)(2,1)S(1)}, u32[]{:S(2)}, u32[]{:S(2)}) collective-permute-start(s16[128,32,128]{2,1,0:T(8,128)(2,1)S(1)} %all-to-all-done.3.got_ref), channel_id=1, source_target_pairs={{0,1},{1,0},{2,3},{3,2},{4,5},{5,4},{6,7},{7,6},{8,9},{9,8},{10,11... | collective-permute-start | bytes 3145736 | tf_op jit(solution)/shard_map/ppermute | solution.py:418
  144.2 0.0 collective-permute-start.1
  144.2 0.1 select_reduce_fusion
  144.3 2.2 collective-permute-done.1.asked_other_ref
  146.6 1.2 copy-done.2
  147.8 4.8 %shard_map.117 = (bf16[64,32,128]{2,1,0:T(8,128)(2,1)S(1)}, bf16[128,32,128]{2,1,0:T(8,128)(2,1)S(1)}) custom-call(s32[128,128]{1,0:T(8,128)S(1)} %bitcast.7, s32[128,128]{1,0:T(8,128)S(1)} %collective-permute-done.1.asked_other_ref, f32[65,32,128]{2,1,0:T(8,128)S(1)} %copy-done.2, f32[65,32,128]{2,1,0:T(8,128)S(1)} %collective-permute-done.2.other_ref, ...), custom_call_target="tpu_custom_call" | custom-call | tf_op jit(solution)/shard_map/pallas_call | solution.py:270
  152.5 0.0 copy-start.5
  152.6 1.0 copy-done.5
  153.5 0.8 copy-done.6
  154.3 9.1 %all-to-all-start.4 = ((bf16[128,32,128]{2,1,0:T(8,128)(2,1)}), bf16[128,32,128]{2,1,0:T(8,128)(2,1)S(1)}, u32[]{:S(2)}, u32[]{:S(2)}) async-start(bf16[128,32,128]{2,1,0:T(8,128)(2,1)} %copy-done.5), calls=%async_computation.4 | async-start | bytes 2097152 | tf_op jit(solution)/shard_map/all_to_all | solution.py:415
  163.4 15.9 %shard_map.119 = s16[128,32,128]{2,1,0:T(8,128)(2,1)} custom-call(s32[1296]{0:T(1024)} %get-tuple-element.22.list_ref, s32[1]{0:T(128)} %get-tuple-element.23.steps_ref, bf16[1280,128,128]{2,1,0:T(8,128)(2,1)} %get-tuple-element.28.tiles_ref, bf16[64,32,128]{2,1,0:T(8,128)(2,1)} %copy-done.6), custom_call_target="tpu_custom_call" | custom-call | flops 10000000000 | bytes 40000000 | tf_op jit(solution)/shard_map/pallas_call | solution.py:210
  179.3 13.2 %all-to-all-done.4.ex_ref = bf16[128,32,128]{2,1,0:T(8,128)(2,1)S(1)} async-done(((bf16[128,32,128]{2,1,0:T(8,128)(2,1)}), bf16[128,32,128]{2,1,0:T(8,128)(2,1)S(1)}, u32[]{:S(2)}, u32[]{:S(2)}) %all-to-all-start.4) | async-done | bytes 1048608 | tf_op jit(solution)/shard_map/all_to_all | solution.py:415
  192.5 7.6 %all-to-all-start.5 = ((s16[128,32,128]{2,1,0:T(8,128)(2,1)}), s16[128,32,128]{2,1,0:T(8,128)(2,1)S(1)}, u32[]{:S(2)}, u32[]{:S(2)}) async-start(s16[128,32,128]{2,1,0:T(8,128)(2,1)} %shard_map.119), calls=%async_computation.5 | async-start | bytes 2097152 | tf_op jit(solution)/shard_map/all_to_all | solution.py:415
  200.1 20.2 %shard_map.118.mine_ref = f32[65,32,128]{2,1,0:T(8,128)} custom-call(s32[1296]{0:T(1024)} %get-tuple-element.22.list_ref, s32[1]{0:T(128)} %get-tuple-element.23.steps_ref, bf16[1280,128,128]{2,1,0:T(8,128)(2,1)} %get-tuple-element.28.tiles_ref, bf16[128,32,128]{2,1,0:T(8,128)(2,1)} %copy-done.9), custom_call_target="tpu_custom_call" | custom-call | flops 10000000000 | bytes 40000000 | tf_op jit(solution)/shard_map/pallas_call | solution.py:223
  220.4 1.3 collective-permute-start.4
  221.7 6.3 %all-to-all-done.5.got_ref = s16[128,32,128]{2,1,0:T(8,128)(2,1)S(1)} async-done(((s16[128,32,128]{2,1,0:T(8,128)(2,1)}), s16[128,32,128]{2,1,0:T(8,128)(2,1)S(1)}, u32[]{:S(2)}, u32[]{:S(2)}) %all-to-all-start.5) | async-done | bytes 1048608 | tf_op jit(solution)/shard_map/all_to_all | solution.py:415
  228.0 4.3 %collective-permute-start.5 = (s16[128,32,128]{2,1,0:T(8,128)(2,1)S(1)}, s16[128,32,128]{2,1,0:T(8,128)(2,1)S(1)}, u32[]{:S(2)}, u32[]{:S(2)}) collective-permute-start(s16[128,32,128]{2,1,0:T(8,128)(2,1)S(1)} %all-to-all-done.5.got_ref), channel_id=1, source_target_pairs={{0,1},{1,0},{2,3},{3,2},{4,5},{5,4},{6,7},{7,6},{8,9},{9,8},{10,11... | collective-permute-start | bytes 3145736 | tf_op jit(solution)/shard_map/ppermute | solution.py:418
  232.4 2.3 collective-permute-done.5.got_other_ref
  234.6 0.0 collective-permute-done.4.other_ref
  234.6 1.2 copy-done.1
  235.9 5.5 %shard_map.120 = f32[64,32,128]{2,1,0:T(8,128)} custom-call(s32[128,128]{1,0:T(8,128)S(1)} %bitcast.8, s32[128,128]{1,0:T(8,128)S(1)} %collective-permute-done.1.asked_other_ref, f32[65,32,128]{2,1,0:T(8,128)S(1)} %copy-done.1, f32[65,32,128]{2,1,0:T(8,128)S(1)} %collective-permute-done.4.other_ref, s16[128,32,128]{2,1,0:T(8,128)(2,1)S(1)} %all-to-all-done.5.got_ref, ...), custom_call_target="tpu_custom_call" | custom-call | tf_op jit(solution)/shard_map/pallas_call | solution.py:270
  (20 shorter events, 0.1 us)
Async XLA Ops:
  1.4 28.4 %all-to-all-start = ((s32[128,1,128]{2,1,0:T(1,128)}), s32[128,1,128]{2,1,0:T(1,128)S(1)}, u32[]{:S(2)}, u32[]{:S(2)}) async-start(s32[128,1,128]{2,1,0:T(1,128)} %shard_map.109), calls=%async_computation | async-start | bytes 131072 | tf_op jit(solution)/shard_map/all_to_all | solution.py:415
  19.8 4.6 %collective-permute-start = (s32[3,640]{1,0:T(4,128)S(1)}, s32[3,640]{1,0:T(4,128)S(1)}, u32[]{:S(2)}, u32[]{:S(2)}) collective-permute-start(s32[3,640]{1,0:T(4,128)S(1)} %pad_add_fusion), channel_id=1, source_target_pairs={{0,1},{1,0},{2,3},{3,2},{4,5},{5,4},{6,7},{7,6},{8,9},{9,8},{10,11... | collective-permute-start | bytes 23048 | tf_op jit(solution)/shard_map/ppermute | solution.py:418
  29.8 0.6 copy-start.3
  33.4 29.0 %all-to-all-start.1 = ((f32[128,1,640]{2,1,0:T(1,128)}), f32[128,1,640]{2,1,0:T(1,128)S(1)}, u32[]{:S(2)}, u32[]{:S(2)}) async-start(f32[128,1,640]{2,1,0:T(1,128)} %shard_map.113), calls=%async_computation.1 | async-start | bytes 655360 | tf_op jit(solution)/shard_map/all_to_all | solution.py:415
  62.4 6.2 %copy-start.10 = (f32[128,1,640]{2,1,0:T(1,128)}, f32[128,1,640]{2,1,0:T(1,128)S(1)}, u32[]{:S(2)}) copy-start(f32[128,1,640]{2,1,0:T(1,128)S(1)} %all-to-all-done.1.geometry_ref) | copy-start | bytes 983044
  62.4 36.8 %all-to-all-start.2 = ((bf16[128,32,128]{2,1,0:T(8,128)(2,1)}), bf16[128,32,128]{2,1,0:T(8,128)(2,1)S(1)}, u32[]{:S(2)}, u32[]{:S(2)}) async-start(bf16[128,32,128]{2,1,0:T(8,128)(2,1)} %get-tuple-element.29), calls=%async_computation.2 | async-start | bytes 2097152 | tf_op jit(solution)/shard_map/all_to_all | solution.py:415
  99.2 12.7 %copy-start.8 = (bf16[128,32,128]{2,1,0:T(8,128)(2,1)}, bf16[128,32,128]{2,1,0:T(8,128)(2,1)S(1)}, u32[]{:S(2)}) copy-start(bf16[128,32,128]{2,1,0:T(8,128)(2,1)S(1)} %all-to-all-done.2.ex_ref) | copy-start | bytes 3145732
  99.2 37.7 %all-to-all-start.3 = ((s16[128,32,128]{2,1,0:T(8,128)(2,1)}), s16[128,32,128]{2,1,0:T(8,128)(2,1)S(1)}, u32[]{:S(2)}, u32[]{:S(2)}) async-start(s16[128,32,128]{2,1,0:T(8,128)(2,1)} %get-tuple-element.30), calls=%async_computation.3 | async-start | bytes 2097152 | tf_op jit(solution)/shard_map/all_to_all | solution.py:415
  111.9 32.2 %copy-start.4 = (s32[128,1,128]{2,1,0:T(1,128)S(1)}, s32[128,1,128]{2,1,0:T(1,128)}, u32[]{:S(2)}) copy-start(s32[128,1,128]{2,1,0:T(1,128)} %copy-done.3) | copy-start | bytes 196612
  111.9 32.2 %copy-start.11 = (s32[64,128]{1,0:T(8,128)S(1)}, s32[64,128]{1,0:T(8,128)}, u32[]{:S(2)}) copy-start(s32[64,128]{1,0:T(8,128)} %param.15) | copy-start | bytes 98308
  112.0 32.2 %copy-start.12 = (f32[8]{0:T(128)S(1)}, f32[8]{0:T(128)}, u32[]{:S(2)}) copy-start(f32[8]{0:T(128)} %param.16) | copy-start | bytes 100
  112.0 34.6 %copy-start = (f32[64,32,128]{2,1,0:T(8,128)S(1)}, f32[64,32,128]{2,1,0:T(8,128)}, u32[]{:S(2)}) copy-start(f32[64,32,128]{2,1,0:T(8,128)} %emission_ref.5) | copy-start | bytes 3145732
  112.0 34.6 %copy-start.7 = (f32[64,128]{1,0:T(8,128)S(1)}, f32[64,128]{1,0:T(8,128)}, u32[]{:S(2)}) copy-start(f32[64,128]{1,0:T(8,128)} %area_ref.3) | copy-start | bytes 98308
  132.3 14.2 %collective-permute-start.2 = (f32[65,32,128]{2,1,0:T(8,128)}, f32[65,32,128]{2,1,0:T(8,128)S(1)}, u32[]{:S(2)}, u32[]{:S(2)}) collective-permute-start(f32[65,32,128]{2,1,0:T(8,128)} %shard_map.116.mine_ref), channel_id=1, source_target_pairs={{0,1},{1,0},{2,3},{3,2},{4,5},{5,4},{6,7},{7,6},{8,9},{9,8},{10,11... | collective-permute-start | bytes 3194888 | tf_op jit(solution)/shard_map/ppermute | solution.py:418
  136.9 9.6 %collective-permute-start.3 = (s16[128,32,128]{2,1,0:T(8,128)(2,1)S(1)}, s16[128,32,128]{2,1,0:T(8,128)(2,1)S(1)}, u32[]{:S(2)}, u32[]{:S(2)}) collective-permute-start(s16[128,32,128]{2,1,0:T(8,128)(2,1)S(1)} %all-to-all-done.3.got_ref), channel_id=1, source_target_pairs={{0,1},{1,0},{2,3},{3,2},{4,5},{5,4},{6,7},{7,6},{8,9},{9,8},{10,11... | collective-permute-start | bytes 3145736 | tf_op jit(solution)/shard_map/ppermute | solution.py:418
  144.2 2.4 collective-permute-start.1
  146.6 1.2 copy-start.2
  152.5 1.0 copy-start.5
  153.5 0.8 copy-start.6
  154.3 38.2 %all-to-all-start.4 = ((bf16[128,32,128]{2,1,0:T(8,128)(2,1)}), bf16[128,32,128]{2,1,0:T(8,128)(2,1)S(1)}, u32[]{:S(2)}, u32[]{:S(2)}) async-start(bf16[128,32,128]{2,1,0:T(8,128)(2,1)} %copy-done.5), calls=%async_computation.4 | async-start | bytes 2097152 | tf_op jit(solution)/shard_map/all_to_all | solution.py:415
  192.5 7.6 %copy-start.9 = (bf16[128,32,128]{2,1,0:T(8,128)(2,1)}, bf16[128,32,128]{2,1,0:T(8,128)(2,1)S(1)}, u32[]{:S(2)}) copy-start(bf16[128,32,128]{2,1,0:T(8,128)(2,1)S(1)} %all-to-all-done.4.ex_ref) | copy-start | bytes 3145732
  192.5 35.5 %all-to-all-start.5 = ((s16[128,32,128]{2,1,0:T(8,128)(2,1)}), s16[128,32,128]{2,1,0:T(8,128)(2,1)S(1)}, u32[]{:S(2)}, u32[]{:S(2)}) async-start(s16[128,32,128]{2,1,0:T(8,128)(2,1)} %shard_map.119), calls=%async_computation.5 | async-start | bytes 2097152 | tf_op jit(solution)/shard_map/all_to_all | solution.py:415
  220.4 14.2 %collective-permute-start.4 = (f32[65,32,128]{2,1,0:T(8,128)}, f32[65,32,128]{2,1,0:T(8,128)S(1)}, u32[]{:S(2)}, u32[]{:S(2)}) collective-permute-start(f32[65,32,128]{2,1,0:T(8,128)} %shard_map.118.mine_ref), channel_id=1, source_target_pairs={{0,1},{1,0},{2,3},{3,2},{4,5},{5,4},{6,7},{7,6},{8,9},{9,8},{10,11... | collective-permute-start | bytes 3194888 | tf_op jit(solution)/shard_map/ppermute | solution.py:418
  228.0 6.6 %collective-permute-start.5 = (s16[128,32,128]{2,1,0:T(8,128)(2,1)S(1)}, s16[128,32,128]{2,1,0:T(8,128)(2,1)S(1)}, u32[]{:S(2)}, u32[]{:S(2)}) collective-permute-start(s16[128,32,128]{2,1,0:T(8,128)(2,1)S(1)} %all-to-all-done.5.got_ref), channel_id=1, source_target_pairs={{0,1},{1,0},{2,3},{3,2},{4,5},{5,4},{6,7},{7,6},{8,9},{9,8},{10,11... | collective-permute-start | bytes 3145736 | tf_op jit(solution)/shard_map/ppermute | solution.py:418
  234.6 1.2 copy-start.1

commit v3 on v2

--- a/solution.py
+++ b/solution.py
@@ -18,6 +18,8 @@
 SMEM_SPEC = pl.BlockSpec(memory_space=pltpu.SMEM)
 VMEM_SPEC = pl.BlockSpec(memory_space=pltpu.VMEM)
 ANY_SPEC = pl.BlockSpec(memory_space=pl.ANY)
+HBM_SPEC = pl.BlockSpec(memory_space=pltpu.HBM)
+PARTS = 4
 
 SPARE = 64 | (128 << 7)
 
@@ -37,34 +39,36 @@
     return lax.shift_right_logical(word, jnp.int32(7)) & 255
 
 
-def list_kernel(words_ref, list_ref, steps_ref):
-    total = words_ref.shape[0]
-
-    def take(turn, count):
-        for j in range(8):
-            word = words_ref[turn * 8 + j]
-            list_ref[count] = word
-            count = count + 1 - (lax.shift_right_logical(word, jnp.int32(6)) & 1)
-        return count
-
-    count = lax.fori_loop(0, total // 8, take, jnp.int32(0))
+def list_kernel(mine_ref, other_ref, list_ref, steps_ref):
+    def take_from(words_ref):
+        def take(turn, count):
+            for j in range(8):
+                word = words_ref[turn * 8 + j]
+                list_ref[count] = word
+                count = count + 1 - (lax.shift_right_logical(word, jnp.int32(6)) & 1)
+            return count
+
+        return take
+
+    turns = mine_ref.shape[0] // 8
+    count = lax.fori_loop(0, turns, take_from(mine_ref), jnp.int32(0))
+    count = lax.fori_loop(0, turns, take_from(other_ref), count)
     for j in range(UNROLL):
         list_ref[count + j] = jnp.int32(SPARE)
     steps_ref[0] = jnp.maximum((count + UNROLL - 1) // UNROLL, 1)
 
 
-def pair_list(words):
-    total = words.shape[0]
+def pair_list(mine, other):
     return pl.pallas_call(
         list_kernel,
         out_shape=(
-            jax.ShapeDtypeStruct((total + UNROLL,), jnp.int32),
+            jax.ShapeDtypeStruct((2 * mine.shape[0] + UNROLL,), jnp.int32),
             jax.ShapeDtypeStruct((1,), jnp.int32),
         ),
-        in_specs=[SMEM_SPEC],
+        in_specs=[SMEM_SPEC] * 2,
         out_specs=(SMEM_SPEC, SMEM_SPEC),
         cost_estimate=pl.CostEstimate(flops=10_000_000, bytes_accessed=10_000_000, transcendentals=0),
-    )(words)
+    )(mine, other)
 
 
 def encode(acc, out_ref):
@@ -231,50 +235,93 @@
     )(pairs, steps, tiles, fetched)
 
 
-def gather_into(acc, mine_ref, other_ref, got_ref, got_other_ref, asked_ref, asked_other_ref):
-    blocks = acc.shape[0]
-    acc[...] = mine_ref[:blocks] + other_ref[:blocks]
-
+def add_asked(acc, asked_ref, got_ref):
     def add(at, carry):
-        for asked, got in ((asked_ref, got_ref), (asked_other_ref, got_other_ref)):
-            acc[asked[at, 0]] += decode(got[at])
-        return carry
-
-    lax.fori_loop(0, got_ref.shape[0], add, 0, unroll=4)
+        acc[asked_ref[at, 0]] += decode(got_ref[at])
+        return carry
+
+    lax.fori_loop(0, got_ref.shape[0], add, 0, unroll=8)
+
+
+def own_kernel(asked_ref, got_ref, out_ref):
+    out_ref[...] = jnp.zeros_like(out_ref)
+    add_asked(out_ref, asked_ref, got_ref)
+
+
+def own(asked, got, blocks):
+    return pl.pallas_call(
+        own_kernel,
+        in_specs=[SMEM_SPEC, VMEM_SPEC],
+        out_specs=VMEM_SPEC,
+        out_shape=jax.ShapeDtypeStruct((blocks,) + got.shape[1:], jnp.float32),
+        compiler_params=pltpu.CompilerParams(vmem_limit_bytes=VMEM // 4),
+        cost_estimate=pl.CostEstimate(flops=10_000_000, bytes_accessed=4_000_000, transcendentals=0),
+    )(asked, got)
 
 
 def middle_kernel(
-    asked_ref, asked_other_ref, mine_ref, other_ref, got_ref, got_other_ref,
-    emission_ref, albedo_ref, area_ref, ex_ref, send_ref, acc,
+    asked_ref, asked_other_ref, own_ref, got_ref, base_ref, albedo_ref, area_ref, ex_out_ref, send_ref,
+    acc, ex, send, ex_sems, send_sems,
 ):
-    gather_into(acc, mine_ref, other_ref, got_ref, got_other_ref, asked_ref, asked_other_ref)
-    ex_ref[...] = (area_ref[...] * (emission_ref[...] + albedo_ref[...] * acc[...])).astype(jnp.bfloat16)
-
-    def put(at, carry):
-        send_ref[at] = ex_ref[asked_ref[at, 0]]
-        return carry
-
-    lax.fori_loop(0, send_ref.shape[0], put, 0, unroll=8)
-
-
-def last_kernel(
-    asked_ref, asked_other_ref, mine_ref, other_ref, got_ref, got_other_ref,
-    emission_ref, albedo_ref, out_ref, acc,
-):
-    gather_into(acc, mine_ref, other_ref, got_ref, got_other_ref, asked_ref, asked_other_ref)
-    out_ref[...] = emission_ref[...] + albedo_ref[...] * acc[...]
-
-
-def update(kernel, asked, asked_other, arrays, out_shape):
-    blocks, hours, block = arrays[4].shape
-    return pl.pallas_call(
-        kernel,
-        in_specs=[SMEM_SPEC] * 2 + [VMEM_SPEC] * len(arrays),
-        out_specs=jax.tree.map(lambda _: VMEM_SPEC, out_shape),
-        out_shape=out_shape,
-        scratch_shapes=[pltpu.VMEM((blocks, hours, block), jnp.float32)],
+    acc[...] = own_ref[...]
+    add_asked(acc, asked_other_ref, got_ref)
+    ex[...] = (area_ref[...] * (base_ref[...] + albedo_ref[...] * acc[...])).astype(jnp.bfloat16)
+    send_copies = part_copies(send, send_ref, send_sems)
+    ex_copies = part_copies(ex, ex_out_ref, ex_sems)
+    put_asked(asked_ref, ex, send, send_copies)
+    for copy in ex_copies:
+        copy.start()
+    for copy in ex_copies + send_copies:
+        copy.wait()
+
+
+def middle(asked, asked_other, own_sum, got, base, albedo, area):
+    blocks, hours, block = base.shape
+    owners = asked.shape[0]
+    return pl.pallas_call(
+        middle_kernel,
+        in_specs=[SMEM_SPEC] * 2 + [VMEM_SPEC] * 5,
+        out_specs=[HBM_SPEC] * 2,
+        out_shape=[
+            jax.ShapeDtypeStruct((blocks, hours, block), jnp.bfloat16),
+            jax.ShapeDtypeStruct((owners, hours, block), jnp.bfloat16),
+        ],
+        scratch_shapes=[
+            pltpu.VMEM((blocks, hours, block), jnp.float32),
+            pltpu.VMEM((blocks, hours, block), jnp.bfloat16),
+            pltpu.VMEM((owners, hours, block), jnp.bfloat16),
+            pltpu.SemaphoreType.DMA((PARTS,)),
+            pltpu.SemaphoreType.DMA((PARTS,)),
+        ],
         compiler_params=pltpu.CompilerParams(vmem_limit_bytes=VMEM // 4),
-    )(asked, asked_other, *arrays)
+    )(asked, asked_other, own_sum, got, base, albedo, area)
+
+
+def last_kernel(asked_other_ref, own_ref, got_ref, base_ref, albedo_ref, out_ref, acc, sems):
+    acc[...] = own_ref[...]
+    add_asked(acc, asked_other_ref, got_ref)
+    size = acc.shape[0] // PARTS
+    copies = part_copies(acc, out_ref, sems)
+    for i, copy in enumerate(copies):
+        part = slice(i * size, (i + 1) * size)
+        acc[part] = base_ref[part] + albedo_ref[part] * acc[part]
+        copy.start()
+    for copy in copies:
+        copy.wait()
+
+
+def last(asked_other, own_sum, got, base, albedo):
+    return pl.pallas_call(
+        last_kernel,
+        in_specs=[SMEM_SPEC] + [VMEM_SPEC] * 4,
+        out_specs=HBM_SPEC,
+        out_shape=jax.ShapeDtypeStruct(base.shape, jnp.float32),
+        scratch_shapes=[
+            pltpu.VMEM(base.shape, jnp.float32),
+            pltpu.SemaphoreType.DMA((PARTS,)),
+        ],
+        compiler_params=pltpu.CompilerParams(vmem_limit_bytes=VMEM // 4),
+    )(asked_other, own_sum, got, base, albedo)
 
 
 def ask_kernel(core_ref, fetch_ref, out_ref):
@@ -292,51 +339,72 @@
     )(core.reshape(1), fetch_block)
 
 
-def place_kernel(asked_ref, positions_ref, area_ref, facing_ref, out_ref):
+def part_copies(source, target, sems):
+    size = source.shape[0] // PARTS
+    return [
+        pltpu.make_async_copy(
+            source.at[pl.ds(i * size, size)], target.at[pl.ds(i * size, size)], sems.at[i]
+        )
+        for i in range(PARTS)
+    ]
+
+
+def put_asked(asked_ref, ex_ref, send, copies):
+    size = send.shape[0] // PARTS
+
+    def put(at, carry):
+        send[at] = ex_ref[asked_ref[at, 0]]
+        return carry
+
+    for i, copy in enumerate(copies):
+        lax.fori_loop(i * size, (i + 1) * size, put, 0, unroll=8)
+        copy.start()
+
+
+def serve_kernel(
+    asked_ref, positions_ref, area_ref, facing_ref, emission_ref, ex_ref, place_ref, send_ref,
+    placed, send, place_sems, send_sems,
+):
     def put(at, carry):
         block = pl.ds(asked_ref[at, 0], 1)
         for i in range(3):
-            out_ref[at, :, i * BLOCK : (i + 1) * BLOCK] = positions_ref[i, block, :]
-        out_ref[at, :, 3 * BLOCK : 4 * BLOCK] = area_ref[block, :]
-        out_ref[at, :, 4 * BLOCK : 5 * BLOCK] = facing_ref[block, :]
-        return carry
-
-    lax.fori_loop(0, out_ref.shape[0], put, 0, unroll=8)
-
-
-def place(asked, positions, patch_area, facing):
-    return pl.pallas_call(
-        place_kernel,
-        in_specs=[SMEM_SPEC] + [VMEM_SPEC] * 3,
-        out_specs=VMEM_SPEC,
-        out_shape=jax.ShapeDtypeStruct((asked.shape[0], 1, 5 * BLOCK), jnp.float32),
-        compiler_params=pltpu.CompilerParams(vmem_limit_bytes=VMEM),
-    )(asked, positions, patch_area, facing)
-
-
-def first_kernel(asked_ref, emission_ref, area_ref, ex_ref, send_ref):
+            placed[at, :, i * BLOCK : (i + 1) * BLOCK] = positions_ref[i, block, :]
+        placed[at, :, 3 * BLOCK : 4 * BLOCK] = area_ref[block, 0, :]
+        placed[at, :, 4 * BLOCK : 5 * BLOCK] = facing_ref[block, :]
+        return carry
+
+    place_copies = part_copies(placed, place_ref, place_sems)
+    send_copies = part_copies(send, send_ref, send_sems)
+    size = placed.shape[0] // PARTS
+    for i, copy in enumerate(place_copies):
+        lax.fori_loop(i * size, (i + 1) * size, put, 0, unroll=8)
+        copy.start()
     ex_ref[...] = (area_ref[...] * emission_ref[...]).astype(jnp.bfloat16)
-
-    def put(at, carry):
-        send_ref[at] = ex_ref[asked_ref[at, 0]]
-        return carry
-
-    lax.fori_loop(0, send_ref.shape[0], put, 0, unroll=8)
-
-
-def first(asked, emission, area):
+    put_asked(asked_ref, ex_ref, send, send_copies)
+    for copy in place_copies + send_copies:
+        copy.wait()
+
+
+def serve(asked, positions, area, facing, emission):
     blocks, hours, block = emission.shape
-    return pl.pallas_call(
-        first_kernel,
-        in_specs=[SMEM_SPEC] + [VMEM_SPEC] * 2,
-        out_specs=[VMEM_SPEC] * 2,
+    owners = asked.shape[0]
+    return pl.pallas_call(
+        serve_kernel,
+        in_specs=[SMEM_SPEC] + [VMEM_SPEC] * 4,
+        out_specs=[VMEM_SPEC, HBM_SPEC, HBM_SPEC],
         out_shape=[
             jax.ShapeDtypeStruct((blocks, hours, block), jnp.bfloat16),
-            jax.ShapeDtypeStruct((asked.shape[0], hours, block), jnp.bfloat16),
+            jax.ShapeDtypeStruct((owners, 1, 5 * block), jnp.float32),
+            jax.ShapeDtypeStruct((owners, hours, block), jnp.bfloat16),
         ],
-        compiler_params=pltpu.CompilerParams(vmem_limit_bytes=VMEM),
-        cost_estimate=pl.CostEstimate(flops=1_000_000, bytes_accessed=4_000_000, transcendentals=0),
-    )(asked, emission, area)
+        scratch_shapes=[
+            pltpu.VMEM((owners, 1, 5 * block), jnp.float32),
+            pltpu.VMEM((owners, hours, block), jnp.bfloat16),
+            pltpu.SemaphoreType.DMA((PARTS,)),
+            pltpu.SemaphoreType.DMA((PARTS,)),
+        ],
+        compiler_params=pltpu.CompilerParams(vmem_limit_bytes=VMEM // 4),
+    )(asked, positions, area, facing, emission)
 
 
 def factor_rows(x, y, z, area, facing, near):
@@ -418,20 +486,22 @@
         return lax.ppermute(array, "grp", [(0, 1), (1, 0)])
 
     asked = exchange(ask(core, fetch_block, owners)).reshape(owners, BLOCK)
-    mine = jnp.stack([pair_rows, pair_slots, pair_code])
-    pair_row, pair_slot, code = jnp.concatenate([mine, swap(mine)], axis=1)
-    skip = (pair_slot & 1) ^ core
-    words = pair_row | (skip << 6) | ((pair_slot >> 1) << 7) | jnp.left_shift(code, 15)
-    pairs, steps = pair_list(words)
-    area = patch_area[:, None, :]
-
+
+    def words(pair_row, pair_slot, code):
+        skip = (pair_slot & 1) ^ core
+        return pair_row | (skip << 6) | ((pair_slot >> 1) << 7) | jnp.left_shift(code, 15)
+
+    lists = (pair_rows, pair_slots, pair_code)
+    pairs, steps = pair_list(words(*lists), words(*map(swap, lists)))
     near = factors(near_kernel, (positions, patch_area, facing), (blocks, BLOCK, FEATURES))
     asked, near, pairs, steps = lax.optimization_barrier((asked, near, pairs, steps))
-    geometry = exchange(place(asked, positions, patch_area, facing))
+
+    area = patch_area[:, None, :]
+    exitance, place, send = serve(asked, positions, area, facing, emission)
+    geometry = exchange(place)
+    send, geometry, asked, albedo_class = lax.optimization_barrier((send, geometry, asked, albedo_class))
+    far = factors(far_kernel, (geometry,), (owners, FEATURES, BLOCK))
     asked_other = swap(asked)
-    exitance, send = first(asked, emission, area)
-    send, geometry = lax.optimization_barrier((send, geometry))
-    far = factors(far_kernel, (geometry,), (owners, FEATURES, BLOCK))
 
     class_ids = jnp.arange(NCLASS, dtype=jnp.int32)
     albedo = jnp.sum(
@@ -442,28 +512,17 @@
     tiles, back = build(
         pairs, steps, jnp.asarray(hash_pattern()), near, far, exitance, 2 * pair_rows.shape[0]
     )
-    got = exchange(back)
-    to_rows = rows(pairs, steps, tiles, fetched, blocks)
-    to_rows_other = swap(to_rows)
-    exitance, send = update(
-        middle_kernel, asked, asked_other,
-        (to_rows, to_rows_other, got, swap(got), emission, albedo, area),
-        [
-            jax.ShapeDtypeStruct((blocks, hours, BLOCK), jnp.bfloat16),
-            jax.ShapeDtypeStruct((owners, hours, BLOCK), jnp.bfloat16),
-        ],
-    )
-
+
+    def collect(back, fetched):
+        got = exchange(back)
+        to_rows = rows(pairs, steps, tiles, fetched, blocks)
+        base = emission + albedo * (to_rows[:blocks] + swap(to_rows)[:blocks])
+        return own(asked, got, blocks), swap(got), base
+
+    exitance, send = middle(asked, asked_other, *collect(back, fetched), albedo, area)
     fetched = exchange(send)
     back = columns(pairs, steps, tiles, exitance, owners)
-    got = exchange(back)
-    to_rows = rows(pairs, steps, tiles, fetched, blocks)
-    to_rows_other = swap(to_rows)
-    return update(
-        last_kernel, asked, asked_other,
-        (to_rows, to_rows_other, got, swap(got), emission, albedo),
-        jax.ShapeDtypeStruct((blocks, hours, BLOCK), jnp.float32),
-    )
+    return last(asked_other, *collect(back, fetched), albedo)
 
 
 def solution(mesh):

time: 242 us -> 235 us (0.971)
  blocking collectives: 0 us -> 27.6 us
  starting transfers between devices: 83.6 us -> 69.3 us
  waiting for transfers between devices: 36.6 us -> 24.7 us
  local copies, waits for them, and re-layouts: 6.93 us -> 0.05 us
  Pallas kernels: 113 us -> 109 us
  other arithmetic: 0.8 us -> 4.1 us
    all_to_all x0 -> x1, blocking collectives: none -> 27.6 us  [exchange(): return lax.all_to_all(array, 'blk', split_axis=0, concat_axis=0, tiled=True)]
    all_to_all x6 -> x5, starting transfers between devices: 65.4 us -> 49.2 us  [exchange(): return lax.all_to_all(array, 'blk', split_axis=0, concat_axis=0, tiled=True)]
    all_to_all x6 -> x5, waiting for transfers between devices: 32.1 us -> 24.7 us  [exchange(): return lax.all_to_all(array, 'blk', split_axis=0, concat_axis=0, tiled=True)]
    unnamed x26 -> x24, local copies, waits for them, and re-layouts: 4.86 us -> 0.05 us
    ppermute x6 -> x8, waiting for transfers between devices: 4.51 us -> 0.02 us  [swap(): return lax.ppermute(array, 'grp', [(0, 1), (1, 0)])]
    pallas_call x2, Pallas kernels: 40.6 us -> 38.1 us  [rows(): pl.pallas_call(rows_kernel, in_specs=[SMEM_SPEC] * 2 + [ANY_SPEC, VMEM_SP...]
    ppermute x6 -> x8, starting transfers between devices: 18.2 us -> 20.2 us  [swap(): return lax.ppermute(array, 'grp', [(0, 1), (1, 0)])]
    pallas_call x5 -> x6, Pallas kernels: 21.1 us -> 21.6 us  [the longest x2 5 us: own(): pl.pallas_call(own_kernel, in_specs=[SMEM_SPEC, VMEM_SPEC], out_specs=VME...]
  transfers between devices with their start and end apart: 12 -> 13, of which waited for: 6 -> 4; matrix products, arithmetic and copies ran while one was open for 1% -> 2% of each run, Pallas kernels for 41% -> 41%
where the time goes in v3:
time: 235 us
  Pallas kernels  109 us (46%)
  starting transfers between devices  69.3 us (29%)
  blocking collectives  27.6 us (12%)
  waiting for transfers between devices  24.7 us (11%)
  other arithmetic  4.1 us (2%)
    all_to_all x5, starting transfers between devices, exchange(): return lax.all_to_all(array, 'blk', split_axis=0, concat_axis=0, tiled=True)  49.2 us
    pallas_call x2, Pallas kernels, rows(): pl.pallas_call(rows_kernel, in_specs=[SMEM_SPEC] * 2 + [ANY_SPEC, VMEM_SP...  38.1 us
    all_to_all x1, blocking collectives, exchange(): return lax.all_to_all(array, 'blk', split_axis=0, concat_axis=0, tiled=True)  27.6 us
    pallas_call x1, Pallas kernels, build(): pl.pallas_call(build_kernel, in_specs=[SMEM_SPEC] * 2 + [VMEM_SPEC] * 4,...  25.2 us
    all_to_all x5, waiting for transfers between devices, exchange(): return lax.all_to_all(array, 'blk', split_axis=0, concat_axis=0, tiled=True)  24.7 us
    ppermute x8, starting transfers between devices, swap(): return lax.ppermute(array, 'grp', [(0, 1), (1, 0)])  20.2 us
    pallas_call x1, Pallas kernels, columns(): pl.pallas_call(columns_kernel, in_specs=[SMEM_SPEC] * 2 + [ANY_SPEC, VMEM...  15.1 us
    pallas_call x2, Pallas kernels, factors(): pl.pallas_call(kernel, in_specs=[VMEM_SPEC] * len(arrays), out_specs=VMEM...  7.43 us
  transfers between devices with their start and end apart: 13, of which 4 were waited for; matrix products, arithmetic and copies ran while one was open for 2% of the time, Pallas kernels for 41%

profile of v3, /device:TPU:1, one launch (start us, length us, event | category | flops | bytes accessed | tf_op | source)
XLA Modules:
  0.0 235.0 jit_solution(16345005409466842793)
XLA Ops:
  0.0 3.2 %collective-permute-start = (s32[640]{0:T(1024)}, s32[640]{0:T(1024)S(1)}, u32[]{:S(2)}, u32[]{:S(2)}) collective-permute-start(s32[640]{0:T(1024)} %param.18), channel_id=1, source_target_pairs={{0,1},{1,0},{2,3},{3,2},{4,5},{5,4},{6,7},{7,6},{8,9},{9,8},{10,11... | collective-permute-start | bytes 7688 | tf_op jit(solution)/shard_map/ppermute | solution.py:486
  3.2 0.0 collective-permute-start.1
  3.2 0.5 collective-permute-start.2
  3.8 1.4 shard_map.109
  5.1 13.8 %all-to-all-start = ((s32[128,1,128]{2,1,0:T(1,128)}), s32[128,1,128]{2,1,0:T(1,128)S(1)}, u32[]{:S(2)}, u32[]{:S(2)}) async-start(s32[128,1,128]{2,1,0:T(1,128)} %shard_map.109), calls=%async_computation | async-start | bytes 131072 | tf_op jit(solution)/shard_map/all_to_all | solution.py:483
  18.9 1.3 shift-left_or_fusion.1.mine_ref
  20.2 3.7 %shard_map.110.near_ref = bf16[64,128,32]{2,1,0:T(8,128)(2,1)} custom-call(f32[3,64,128]{2,1,0:T(8,128)} %positions_ref.3, f32[64,128]{1,0:T(8,128)} %area_ref.1, f32[64,128]{1,0:T(8,128)} %facing_ref.3), custom_call_target="tpu_custom_call" | custom-call | flops 10000000 | bytes 8000000 | tf_op jit(solution)/shard_map/pallas_call | solution.py:463
  23.9 0.0 collective-permute-done
  23.9 0.0 collective-permute-done.1
  23.9 0.0 collective-permute-done.2
  23.9 0.6 shift-left_or_fusion.other_ref
  24.6 4.6 %shard_map.111 = (s32[1296]{0:T(1024)}, s32[1]{0:T(128)}) custom-call(s32[640]{0:T(1024)} %shift-left_or_fusion.1.mine_ref, s32[640]{0:T(1024)} %shift-left_or_fusion.other_ref), custom_call_target="tpu_custom_call" | custom-call | flops 10000000 | bytes 10000000 | tf_op jit(solution)/shard_map/pallas_call | solution.py:62
  29.2 0.4 all-to-all-done
  29.6 3.6 %shard_map.112 = (bf16[64,32,128]{2,1,0:T(8,128)(2,1)S(1)}, f32[128,1,640]{2,1,0:T(1,128)S(1)}, bf16[128,32,128]{2,1,0:T(8,128)(2,1)}) custom-call(s32[128,128]{1,0:T(8,128)S(1)} %bitcast.4, f32[3,64,128]{2,1,0:T(8,128)S(1)} %copy-done.2, f32[64,1,128]{2,1,0:T(1,128)S(1)} %bitcast.11, f32[64,128]{1,0:T(8,128)S(1)} %copy-done.4, f32[64,32,128]{2,1,0:T(8,128)S(1)} %copy-done), custom_call_target="tpu_custom_call" | custom-call | tf_op jit(solution)/shard_map/pallas_call | solution.py:391
  33.2 27.6 %all_to_all.30.geometry_ref = f32[128,1,640]{2,1,0:T(1,128)} all-to-all(f32[128,1,640]{2,1,0:T(1,128)S(1)} %get-tuple-element.26), channel_id=1, replica_groups=mesh['blk'=128,'grp'=2] {'blk'}, dimensions={0} | all-to-all | bytes 655360 | tf_op jit(solution)/shard_map/all_to_all | solution.py:483
  60.8 6.4 %all-to-all-start.3 = ((bf16[128,32,128]{2,1,0:T(8,128)(2,1)}), bf16[128,32,128]{2,1,0:T(8,128)(2,1)S(1)}, u32[]{:S(2)}, u32[]{:S(2)}) async-start(bf16[128,32,128]{2,1,0:T(8,128)(2,1)} %get-tuple-element.36), calls=%async_computation.3 | async-start | bytes 2097152 | tf_op jit(solution)/shard_map/all_to_all | solution.py:483
  67.2 3.7 %shard_map.113.far_ref = bf16[128,32,128]{2,1,0:T(8,128)(2,1)} custom-call(f32[128,1,640]{2,1,0:T(1,128)} %all_to_all.30.geometry_ref), custom_call_target="tpu_custom_call" | custom-call | flops 10000000 | bytes 8000000 | tf_op jit(solution)/shard_map/pallas_call | solution.py:463
  70.9 25.2 %shard_map.114 = (bf16[1280,128,128]{2,1,0:T(8,128)(2,1)}, s16[128,32,128]{2,1,0:T(8,128)(2,1)}) custom-call(s32[1296]{0:T(1024)} %get-tuple-element.28.list_ref, s32[1]{0:T(128)} %get-tuple-element.29.steps_ref, s32[128,128]{1,0:T(8,128)} %constant.16.clone.pattern_ref, bf16[64,128,32]{2,1,0:T(8,128)(2,1)} %shard_map.110.near_ref, ...), custom_call_target="tpu_custom_call" | custom-call | flops 20000000000 | bytes 60000000 | tf_op jit(solution)/shard_map/pallas_call | solution.py:196
  96.1 0.0 all-to-all-done.3.ex_ref
  96.2 0.0 copy-start.8
  96.2 15.6 %all-to-all-start.2 = ((s16[128,32,128]{2,1,0:T(8,128)(2,1)}), s16[128,32,128]{2,1,0:T(8,128)(2,1)S(1)}, u32[]{:S(2)}, u32[]{:S(2)}) async-start(s16[128,32,128]{2,1,0:T(8,128)(2,1)} %get-tuple-element.34), calls=%async_computation.2 | async-start | bytes 2097152 | tf_op jit(solution)/shard_map/all_to_all | solution.py:483
  111.8 0.0 copy-start.10
  111.8 0.0 copy-start.11
  111.8 19.0 %shard_map.116 = f32[65,32,128]{2,1,0:T(8,128)} custom-call(s32[1296]{0:T(1024)} %get-tuple-element.28.list_ref, s32[1]{0:T(128)} %get-tuple-element.29.steps_ref, bf16[1280,128,128]{2,1,0:T(8,128)(2,1)} %get-tuple-element.33.tiles_ref, bf16[128,32,128]{2,1,0:T(8,128)(2,1)} %copy-done.8), custom_call_target="tpu_custom_call" | custom-call | flops 10000000000 | bytes 40000000 | tf_op jit(solution)/shard_map/pallas_call | solution.py:227
  130.8 3.7 %collective-permute-start.5 = (f32[65,32,128]{2,1,0:T(8,128)}, f32[65,32,128]{2,1,0:T(8,128)S(1)}, u32[]{:S(2)}, u32[]{:S(2)}) collective-permute-start(f32[65,32,128]{2,1,0:T(8,128)} %shard_map.116), channel_id=1, source_target_pairs={{0,1},{1,0},{2,3},{3,2},{4,5},{5,4},{6,7},{7,6},{8,9},{9,8},{10,11... | collective-permute-start | bytes 3194888 | tf_op jit(solution)/shard_map/ppermute | solution.py:486
  134.6 5.0 %all-to-all-done.2.got_ref = s16[128,32,128]{2,1,0:T(8,128)(2,1)S(1)} async-done(((s16[128,32,128]{2,1,0:T(8,128)(2,1)}), s16[128,32,128]{2,1,0:T(8,128)(2,1)S(1)}, u32[]{:S(2)}, u32[]{:S(2)}) %all-to-all-start.2) | async-done | bytes 1048608 | tf_op jit(solution)/shard_map/all_to_all | solution.py:483
  139.5 4.4 %collective-permute-start.4 = (s16[128,32,128]{2,1,0:T(8,128)(2,1)S(1)}, s16[128,32,128]{2,1,0:T(8,128)(2,1)S(1)}, u32[]{:S(2)}, u32[]{:S(2)}) collective-permute-start(s16[128,32,128]{2,1,0:T(8,128)(2,1)S(1)} %all-to-all-done.2.got_ref), channel_id=1, source_target_pairs={{0,1},{1,0},{2,3},{3,2},{4,5},{5,4},{6,7},{7,6},{8,9},{9,8},{10,11... | collective-permute-start | bytes 3145736 | tf_op jit(solution)/shard_map/ppermute | solution.py:486
  144.0 0.0 collective-permute-start.3
  144.0 0.1 select_reduce_fusion
  144.2 2.5 %shard_map.115.own_ref = f32[64,32,128]{2,1,0:T(8,128)S(1)} custom-call(s32[128,128]{1,0:T(8,128)S(1)} %bitcast.6, s16[128,32,128]{2,1,0:T(8,128)(2,1)S(1)} %all-to-all-done.2.got_ref), custom_call_target="tpu_custom_call" | custom-call | flops 10000000 | bytes 4000000 | tf_op jit(solution)/shard_map/pallas_call | solution.py:252
  146.7 0.0 collective-permute-done.5
  146.7 0.4 fusion.3.base_ref
  147.1 0.0 collective-permute-done.3.asked_other_ref
  147.1 0.0 collective-permute-done.4.got_ref
  147.1 4.8 %shard_map.117 = (bf16[64,32,128]{2,1,0:T(8,128)(2,1)S(1)}, bf16[128,32,128]{2,1,0:T(8,128)(2,1)}) custom-call(s32[128,128]{1,0:T(8,128)S(1)} %bitcast.7, s32[128,128]{1,0:T(8,128)S(1)} %collective-permute-done.3.asked_other_ref, f32[64,32,128]{2,1,0:T(8,128)S(1)} %shard_map.115.own_ref, s16[128,32,128]{2,1,0:T(8,128)(2,1)S(1)} %collective-permute-done.4.got_ref, ...), custom_call_target="tpu_custom_call" | custom-call | tf_op jit(solution)/shard_map/pallas_call | solution.py:281
  151.9 6.2 %all-to-all-start.5 = ((bf16[128,32,128]{2,1,0:T(8,128)(2,1)}), bf16[128,32,128]{2,1,0:T(8,128)(2,1)S(1)}, u32[]{:S(2)}, u32[]{:S(2)}) async-start(bf16[128,32,128]{2,1,0:T(8,128)(2,1)} %get-tuple-element.38), calls=%async_computation.5 | async-start | bytes 2097152 | tf_op jit(solution)/shard_map/all_to_all | solution.py:483
  158.2 15.1 %shard_map.118 = s16[128,32,128]{2,1,0:T(8,128)(2,1)} custom-call(s32[1296]{0:T(1024)} %get-tuple-element.28.list_ref, s32[1]{0:T(128)} %get-tuple-element.29.steps_ref, bf16[1280,128,128]{2,1,0:T(8,128)(2,1)} %get-tuple-element.33.tiles_ref, bf16[64,32,128]{2,1,0:T(8,128)(2,1)} %copy-done.1), custom_call_target="tpu_custom_call" | custom-call | flops 10000000000 | bytes 40000000 | tf_op jit(solution)/shard_map/pallas_call | solution.py:214
  173.3 14.4 %all-to-all-done.5.ex_ref = bf16[128,32,128]{2,1,0:T(8,128)(2,1)S(1)} async-done(((bf16[128,32,128]{2,1,0:T(8,128)(2,1)}), bf16[128,32,128]{2,1,0:T(8,128)(2,1)S(1)}, u32[]{:S(2)}, u32[]{:S(2)}) %all-to-all-start.5) | async-done | bytes 1048608 | tf_op jit(solution)/shard_map/all_to_all | solution.py:483
  187.7 7.2 %all-to-all-start.4 = ((s16[128,32,128]{2,1,0:T(8,128)(2,1)}), s16[128,32,128]{2,1,0:T(8,128)(2,1)S(1)}, u32[]{:S(2)}, u32[]{:S(2)}) async-start(s16[128,32,128]{2,1,0:T(8,128)(2,1)} %shard_map.118), calls=%async_computation.4 | async-start | bytes 2097152 | tf_op jit(solution)/shard_map/all_to_all | solution.py:483
  194.9 19.0 %shard_map.120 = f32[65,32,128]{2,1,0:T(8,128)} custom-call(s32[1296]{0:T(1024)} %get-tuple-element.28.list_ref, s32[1]{0:T(128)} %get-tuple-element.29.steps_ref, bf16[1280,128,128]{2,1,0:T(8,128)(2,1)} %get-tuple-element.33.tiles_ref, bf16[128,32,128]{2,1,0:T(8,128)(2,1)} %copy-done.9), custom_call_target="tpu_custom_call" | custom-call | flops 10000000000 | bytes 40000000 | tf_op jit(solution)/shard_map/pallas_call | solution.py:227
  214.0 3.8 %collective-permute-start.7 = (f32[65,32,128]{2,1,0:T(8,128)}, f32[65,32,128]{2,1,0:T(8,128)}, u32[]{:S(2)}, u32[]{:S(2)}) collective-permute-start(f32[65,32,128]{2,1,0:T(8,128)} %shard_map.120), channel_id=1, source_target_pairs={{0,1},{1,0},{2,3},{3,2},{4,5},{5,4},{6,7},{7,6},{8,9},{9,8},{10,11... | collective-permute-start | bytes 3194888 | tf_op jit(solution)/shard_map/ppermute | solution.py:486
  217.7 5.0 %all-to-all-done.4.got_ref = s16[128,32,128]{2,1,0:T(8,128)(2,1)S(1)} async-done(((s16[128,32,128]{2,1,0:T(8,128)(2,1)}), s16[128,32,128]{2,1,0:T(8,128)(2,1)S(1)}, u32[]{:S(2)}, u32[]{:S(2)}) %all-to-all-start.4) | async-done | bytes 1048608 | tf_op jit(solution)/shard_map/all_to_all | solution.py:483
  222.7 4.5 %collective-permute-start.6 = (s16[128,32,128]{2,1,0:T(8,128)(2,1)S(1)}, s16[128,32,128]{2,1,0:T(8,128)(2,1)S(1)}, u32[]{:S(2)}, u32[]{:S(2)}) collective-permute-start(s16[128,32,128]{2,1,0:T(8,128)(2,1)S(1)} %all-to-all-done.4.got_ref), channel_id=1, source_target_pairs={{0,1},{1,0},{2,3},{3,2},{4,5},{5,4},{6,7},{7,6},{8,9},{9,8},{10,11... | collective-permute-start | bytes 3145736 | tf_op jit(solution)/shard_map/ppermute | solution.py:486
  227.1 2.5 %shard_map.119.own_ref = f32[64,32,128]{2,1,0:T(8,128)S(1)} custom-call(s32[128,128]{1,0:T(8,128)S(1)} %bitcast.8, s16[128,32,128]{2,1,0:T(8,128)(2,1)S(1)} %all-to-all-done.4.got_ref), custom_call_target="tpu_custom_call" | custom-call | flops 10000000 | bytes 4000000 | tf_op jit(solution)/shard_map/pallas_call | solution.py:252
  229.6 0.0 collective-permute-done.7
  229.7 1.6 fusion.1.base_ref
  231.3 0.0 collective-permute-done.6.got_ref
  231.3 3.6 %shard_map.121 = f32[64,32,128]{2,1,0:T(8,128)} custom-call(s32[128,128]{1,0:T(8,128)S(1)} %collective-permute-done.3.asked_other_ref, f32[64,32,128]{2,1,0:T(8,128)S(1)} %shard_map.119.own_ref, s16[128,32,128]{2,1,0:T(8,128)(2,1)S(1)} %collective-permute-done.6.got_ref, f32[64,32,128]{2,1,0:T(8,128)S(1)} %fusion.1.base_ref, f32[64,1,128]{2,1,0:T(1,128)S(1)} %bitcast.10), custom_call_target="tpu_custom_call" | custom-call | tf_op jit(solution)/shard_map/pallas_call | solution.py:314
  (21 shorter events, 0.0 us)
Async XLA Ops:
  0.0 23.9 %collective-permute-start = (s32[640]{0:T(1024)}, s32[640]{0:T(1024)S(1)}, u32[]{:S(2)}, u32[]{:S(2)}) collective-permute-start(s32[640]{0:T(1024)} %param.18), channel_id=1, source_target_pairs={{0,1},{1,0},{2,3},{3,2},{4,5},{5,4},{6,7},{7,6},{8,9},{9,8},{10,11... | collective-permute-start | bytes 7688 | tf_op jit(solution)/shard_map/ppermute | solution.py:486
  3.2 20.7 %collective-permute-start.1 = (s32[640]{0:T(1024)}, s32[640]{0:T(1024)S(1)}, u32[]{:S(2)}, u32[]{:S(2)}) collective-permute-start(s32[640]{0:T(1024)} %param.19), channel_id=1, source_target_pairs={{0,1},{1,0},{2,3},{3,2},{4,5},{5,4},{6,7},{7,6},{8,9},{9,8},{10,11... | collective-permute-start | bytes 7688 | tf_op jit(solution)/shard_map/ppermute | solution.py:486
  3.2 20.7 %collective-permute-start.2 = (s32[640]{0:T(1024)}, s32[640]{0:T(1024)S(1)}, u32[]{:S(2)}, u32[]{:S(2)}) collective-permute-start(s32[640]{0:T(1024)} %param.20), channel_id=1, source_target_pairs={{0,1},{1,0},{2,3},{3,2},{4,5},{5,4},{6,7},{7,6},{8,9},{9,8},{10,11... | collective-permute-start | bytes 7688 | tf_op jit(solution)/shard_map/ppermute | solution.py:486
  5.1 24.5 %all-to-all-start = ((s32[128,1,128]{2,1,0:T(1,128)}), s32[128,1,128]{2,1,0:T(1,128)S(1)}, u32[]{:S(2)}, u32[]{:S(2)}) async-start(s32[128,1,128]{2,1,0:T(1,128)} %shard_map.109), calls=%async_computation | async-start | bytes 131072 | tf_op jit(solution)/shard_map/all_to_all | solution.py:483
  20.2 9.4 %copy-start = (f32[64,32,128]{2,1,0:T(8,128)S(1)}, f32[64,32,128]{2,1,0:T(8,128)}, u32[]{:S(2)}) copy-start(f32[64,32,128]{2,1,0:T(8,128)} %emission_ref.1) | copy-start | bytes 3145732
  20.2 9.4 %copy-start.2 = (f32[3,64,128]{2,1,0:T(8,128)S(1)}, f32[3,64,128]{2,1,0:T(8,128)}, u32[]{:S(2)}) copy-start(f32[3,64,128]{2,1,0:T(8,128)} %positions_ref.3) | copy-start | bytes 294916
  20.2 9.4 %copy-start.3 = (f32[64,128]{1,0:T(8,128)S(1)}, f32[64,128]{1,0:T(8,128)}, u32[]{:S(2)}) copy-start(f32[64,128]{1,0:T(8,128)} %area_ref.1) | copy-start | bytes 98308
  20.2 9.4 %copy-start.4 = (f32[64,128]{1,0:T(8,128)S(1)}, f32[64,128]{1,0:T(8,128)}, u32[]{:S(2)}) copy-start(f32[64,128]{1,0:T(8,128)} %facing_ref.3) | copy-start | bytes 98308
  33.2 27.6 %copy-start.5 = (bf16[64,32,128]{2,1,0:T(8,128)(2,1)}, bf16[64,32,128]{2,1,0:T(8,128)(2,1)S(1)}, u32[]{:S(2)}) copy-start(bf16[64,32,128]{2,1,0:T(8,128)(2,1)S(1)} %get-tuple-element.32.ex_ref) | copy-start | bytes 1572868
  60.8 35.3 %all-to-all-start.3 = ((bf16[128,32,128]{2,1,0:T(8,128)(2,1)}), bf16[128,32,128]{2,1,0:T(8,128)(2,1)S(1)}, u32[]{:S(2)}, u32[]{:S(2)}) async-start(bf16[128,32,128]{2,1,0:T(8,128)(2,1)} %get-tuple-element.36), calls=%async_computation.3 | async-start | bytes 2097152 | tf_op jit(solution)/shard_map/all_to_all | solution.py:483
  96.2 15.6 %copy-start.8 = (bf16[128,32,128]{2,1,0:T(8,128)(2,1)}, bf16[128,32,128]{2,1,0:T(8,128)(2,1)S(1)}, u32[]{:S(2)}) copy-start(bf16[128,32,128]{2,1,0:T(8,128)(2,1)S(1)} %all-to-all-done.3.ex_ref) | copy-start | bytes 3145732
  96.2 43.4 %all-to-all-start.2 = ((s16[128,32,128]{2,1,0:T(8,128)(2,1)}), s16[128,32,128]{2,1,0:T(8,128)(2,1)S(1)}, u32[]{:S(2)}, u32[]{:S(2)}) async-start(s16[128,32,128]{2,1,0:T(8,128)(2,1)} %get-tuple-element.34), calls=%async_computation.2 | async-start | bytes 2097152 | tf_op jit(solution)/shard_map/all_to_all | solution.py:483
  111.8 32.2 %copy-start.10 = (s32[64,128]{1,0:T(8,128)S(1)}, s32[64,128]{1,0:T(8,128)}, u32[]{:S(2)}) copy-start(s32[64,128]{1,0:T(8,128)} %param.15) | copy-start | bytes 98308
  111.8 32.2 %copy-start.11 = (f32[8]{0:T(128)S(1)}, f32[8]{0:T(128)}, u32[]{:S(2)}) copy-start(f32[8]{0:T(128)} %param.16) | copy-start | bytes 100
  130.8 15.8 %collective-permute-start.5 = (f32[65,32,128]{2,1,0:T(8,128)}, f32[65,32,128]{2,1,0:T(8,128)S(1)}, u32[]{:S(2)}, u32[]{:S(2)}) collective-permute-start(f32[65,32,128]{2,1,0:T(8,128)} %shard_map.116), channel_id=1, source_target_pairs={{0,1},{1,0},{2,3},{3,2},{4,5},{5,4},{6,7},{7,6},{8,9},{9,8},{10,11... | collective-permute-start | bytes 3194888 | tf_op jit(solution)/shard_map/ppermute | solution.py:486
  139.5 7.6 %collective-permute-start.4 = (s16[128,32,128]{2,1,0:T(8,128)(2,1)S(1)}, s16[128,32,128]{2,1,0:T(8,128)(2,1)S(1)}, u32[]{:S(2)}, u32[]{:S(2)}) collective-permute-start(s16[128,32,128]{2,1,0:T(8,128)(2,1)S(1)} %all-to-all-done.2.got_ref), channel_id=1, source_target_pairs={{0,1},{1,0},{2,3},{3,2},{4,5},{5,4},{6,7},{7,6},{8,9},{9,8},{10,11... | collective-permute-start | bytes 3145736 | tf_op jit(solution)/shard_map/ppermute | solution.py:486
  144.0 3.1 %collective-permute-start.3 = (s32[128,128]{1,0:T(8,128)S(1)}, s32[128,128]{1,0:T(8,128)S(1)}, u32[]{:S(2)}, u32[]{:S(2)}) collective-permute-start(s32[128,128]{1,0:T(8,128)S(1)} %bitcast.5), channel_id=1, source_target_pairs={{0,1},{1,0},{2,3},{3,2},{4,5},{5,4},{6,7},{7,6},{8,9},{9,8},{10,11... | collective-permute-start | bytes 196616 | tf_op jit(solution)/shard_map/ppermute | solution.py:486
  144.1 2.5 %copy-start.6 = (f32[65,32,128]{2,1,0:T(8,128)S(1)}, f32[65,32,128]{2,1,0:T(8,128)}, u32[]{:S(2)}) copy-start(f32[65,32,128]{2,1,0:T(8,128)} %shard_map.116) | copy-start | bytes 3194884
  151.9 6.2 %copy-start.1 = (bf16[64,32,128]{2,1,0:T(8,128)(2,1)}, bf16[64,32,128]{2,1,0:T(8,128)(2,1)S(1)}, u32[]{:S(2)}) copy-start(bf16[64,32,128]{2,1,0:T(8,128)(2,1)S(1)} %get-tuple-element.37.ex_ref) | copy-start | bytes 1572868
  151.9 35.7 %all-to-all-start.5 = ((bf16[128,32,128]{2,1,0:T(8,128)(2,1)}), bf16[128,32,128]{2,1,0:T(8,128)(2,1)S(1)}, u32[]{:S(2)}, u32[]{:S(2)}) async-start(bf16[128,32,128]{2,1,0:T(8,128)(2,1)} %get-tuple-element.38), calls=%async_computation.5 | async-start | bytes 2097152 | tf_op jit(solution)/shard_map/all_to_all | solution.py:483
  187.7 7.3 %copy-start.9 = (bf16[128,32,128]{2,1,0:T(8,128)(2,1)}, bf16[128,32,128]{2,1,0:T(8,128)(2,1)S(1)}, u32[]{:S(2)}) copy-start(bf16[128,32,128]{2,1,0:T(8,128)(2,1)S(1)} %all-to-all-done.5.ex_ref) | copy-start | bytes 3145732
  187.7 35.0 %all-to-all-start.4 = ((s16[128,32,128]{2,1,0:T(8,128)(2,1)}), s16[128,32,128]{2,1,0:T(8,128)(2,1)S(1)}, u32[]{:S(2)}, u32[]{:S(2)}) async-start(s16[128,32,128]{2,1,0:T(8,128)(2,1)} %shard_map.118), calls=%async_computation.4 | async-start | bytes 2097152 | tf_op jit(solution)/shard_map/all_to_all | solution.py:483
  214.0 15.7 %copy-start.7 = (f32[65,32,128]{2,1,0:T(8,128)S(1)}, f32[65,32,128]{2,1,0:T(8,128)}, u32[]{:S(2)}) copy-start(f32[65,32,128]{2,1,0:T(8,128)} %shard_map.120) | copy-start | bytes 3194884
  214.0 15.7 %collective-permute-start.7 = (f32[65,32,128]{2,1,0:T(8,128)}, f32[65,32,128]{2,1,0:T(8,128)}, u32[]{:S(2)}, u32[]{:S(2)}) collective-permute-start(f32[65,32,128]{2,1,0:T(8,128)} %shard_map.120), channel_id=1, source_target_pairs={{0,1},{1,0},{2,3},{3,2},{4,5},{5,4},{6,7},{7,6},{8,9},{9,8},{10,11... | collective-permute-start | bytes 3194888 | tf_op jit(solution)/shard_map/ppermute | solution.py:486
  222.7 8.6 %collective-permute-start.6 = (s16[128,32,128]{2,1,0:T(8,128)(2,1)S(1)}, s16[128,32,128]{2,1,0:T(8,128)(2,1)S(1)}, u32[]{:S(2)}, u32[]{:S(2)}) collective-permute-start(s16[128,32,128]{2,1,0:T(8,128)(2,1)S(1)} %all-to-all-done.4.got_ref), channel_id=1, source_target_pairs={{0,1},{1,0},{2,3},{3,2},{4,5},{5,4},{6,7},{7,6},{8,9},{9,8},{10,11... | collective-permute-start | bytes 3145736 | tf_op jit(solution)/shard_map/ppermute | solution.py:486

commit v4 on v3

--- a/solution.py
+++ b/solution.py
@@ -12,8 +12,8 @@
 NCLASS = 8
 HASH = 747796405
 FEATURES = 32
-UNROLL = 16
-DEPTH = 8
+UNROLL = 64
+DEPTH = 4
 VMEM = 60 * 1024 * 1024
 SMEM_SPEC = pl.BlockSpec(memory_space=pltpu.SMEM)
 VMEM_SPEC = pl.BlockSpec(memory_space=pltpu.VMEM)
@@ -105,9 +105,11 @@
 
 
 def build_kernel(
-    list_ref, steps_ref, pattern_ref, near_ref, far_ref, ex_ref, tiles_ref, out_ref, acc, held, sems
+    list_ref, steps_ref, pattern_ref, near_ref, geometry_ref, ex_ref, tiles_ref, out_ref,
+    acc, held, sems, far, turned,
 ):
     steps = steps_ref[0]
+    far_factors(geometry_ref, far, turned)
     acc[...] = jnp.zeros_like(acc)
 
     def turn(step, carry):
@@ -121,7 +123,7 @@
             word = list_ref[step * UNROLL + j]
             row, slot = row_of(word) & 63, slot_of(word)
             shift = jnp.left_shift(lax.shift_right_logical(word, jnp.int32(15)) * jnp.int32(HASH), 21)
-            scaled = jnp.dot(near_ref[row], far_ref[slot & 127], preferred_element_type=jnp.float32)
+            scaled = jnp.dot(near_ref[row], far[slot & 127], preferred_element_type=jnp.float32)
             mixed = pattern_ref[...] + shift
             mixed = mixed ^ jnp.left_shift(mixed, 5)
             tile = jnp.where(mixed < 0, pl.reciprocal(scaled, approx=True), 0.0).astype(jnp.bfloat16)
@@ -191,8 +193,8 @@
 SEMS = pltpu.SemaphoreType.DMA((DEPTH,))
 
 
-def build(pairs, steps, pattern, near, far, exitance, pair_max):
-    slots, hours = far.shape[0], exitance.shape[1]
+def build(pairs, steps, pattern, near, geometry, exitance, pair_max):
+    slots, hours = geometry.shape[0], exitance.shape[1]
     return pl.pallas_call(
         build_kernel,
         in_specs=[SMEM_SPEC] * 2 + [VMEM_SPEC] * 4,
@@ -201,12 +203,18 @@
             jax.ShapeDtypeStruct((pair_max, BLOCK, BLOCK), jnp.bfloat16),
             jax.ShapeDtypeStruct((slots, hours, BLOCK), jnp.int16),
         ],
-        scratch_shapes=[pltpu.VMEM((slots + 1, hours, BLOCK), jnp.float32), HELD, SEMS],
+        scratch_shapes=[
+            pltpu.VMEM((slots + 1, hours, BLOCK), jnp.float32),
+            HELD,
+            SEMS,
+            pltpu.VMEM((slots, FEATURES, BLOCK), jnp.bfloat16),
+            pltpu.VMEM((8 * FEATURES, BLOCK), jnp.float32),
+        ],
         compiler_params=pltpu.CompilerParams(vmem_limit_bytes=VMEM),
         cost_estimate=pl.CostEstimate(
             flops=20_000_000_000, bytes_accessed=60_000_000, transcendentals=10_000_000
         ),
-    )(pairs, steps, pattern, near, far, exitance)
+    )(pairs, steps, pattern, near, geometry, exitance)
 
 
 def columns(pairs, steps, tiles, exitance, slots):
@@ -361,50 +369,61 @@
         copy.start()
 
 
-def serve_kernel(
-    asked_ref, positions_ref, area_ref, facing_ref, emission_ref, ex_ref, place_ref, send_ref,
-    placed, send, place_sems, send_sems,
-):
+def place_kernel(asked_ref, geometry_ref, place_ref, placed, sems):
     def put(at, carry):
-        block = pl.ds(asked_ref[at, 0], 1)
-        for i in range(3):
-            placed[at, :, i * BLOCK : (i + 1) * BLOCK] = positions_ref[i, block, :]
-        placed[at, :, 3 * BLOCK : 4 * BLOCK] = area_ref[block, 0, :]
-        placed[at, :, 4 * BLOCK : 5 * BLOCK] = facing_ref[block, :]
-        return carry
-
-    place_copies = part_copies(placed, place_ref, place_sems)
-    send_copies = part_copies(send, send_ref, send_sems)
+        placed[at] = geometry_ref[pl.ds(asked_ref[at, 0], 1), :]
+        return carry
+
+    copies = part_copies(placed, place_ref, sems)
     size = placed.shape[0] // PARTS
-    for i, copy in enumerate(place_copies):
+    for i, copy in enumerate(copies):
         lax.fori_loop(i * size, (i + 1) * size, put, 0, unroll=8)
         copy.start()
+    for copy in copies:
+        copy.wait()
+
+
+def place(asked, geometry):
+    owners = asked.shape[0]
+    return pl.pallas_call(
+        place_kernel,
+        in_specs=[SMEM_SPEC, VMEM_SPEC],
+        out_specs=HBM_SPEC,
+        out_shape=jax.ShapeDtypeStruct((owners, 1, geometry.shape[1]), jnp.float32),
+        scratch_shapes=[
+            pltpu.VMEM((owners, 1, geometry.shape[1]), jnp.float32),
+            pltpu.SemaphoreType.DMA((PARTS,)),
+        ],
+        compiler_params=pltpu.CompilerParams(vmem_limit_bytes=VMEM // 4),
+    )(asked, geometry)
+
+
+def first_kernel(asked_ref, area_ref, emission_ref, ex_ref, send_ref, send, sems):
     ex_ref[...] = (area_ref[...] * emission_ref[...]).astype(jnp.bfloat16)
-    put_asked(asked_ref, ex_ref, send, send_copies)
-    for copy in place_copies + send_copies:
+    copies = part_copies(send, send_ref, sems)
+    put_asked(asked_ref, ex_ref, send, copies)
+    for copy in copies:
         copy.wait()
 
 
-def serve(asked, positions, area, facing, emission):
+def first(asked, area, emission):
     blocks, hours, block = emission.shape
     owners = asked.shape[0]
     return pl.pallas_call(
-        serve_kernel,
-        in_specs=[SMEM_SPEC] + [VMEM_SPEC] * 4,
-        out_specs=[VMEM_SPEC, HBM_SPEC, HBM_SPEC],
+        first_kernel,
+        in_specs=[SMEM_SPEC] + [VMEM_SPEC] * 2,
+        out_specs=[VMEM_SPEC, HBM_SPEC],
         out_shape=[
             jax.ShapeDtypeStruct((blocks, hours, block), jnp.bfloat16),
-            jax.ShapeDtypeStruct((owners, 1, 5 * block), jnp.float32),
             jax.ShapeDtypeStruct((owners, hours, block), jnp.bfloat16),
         ],
         scratch_shapes=[
-            pltpu.VMEM((owners, 1, 5 * block), jnp.float32),
             pltpu.VMEM((owners, hours, block), jnp.bfloat16),
             pltpu.SemaphoreType.DMA((PARTS,)),
-            pltpu.SemaphoreType.DMA((PARTS,)),
         ],
         compiler_params=pltpu.CompilerParams(vmem_limit_bytes=VMEM // 4),
-    )(asked, positions, area, facing, emission)
+        cost_estimate=pl.CostEstimate(flops=10_000_000, bytes_accessed=8_000_000, transcendentals=0),
+    )(asked, area, emission)
 
 
 def factor_rows(x, y, z, area, facing, near):
@@ -449,14 +468,14 @@
     factor_blocks(read, out_ref.shape[0], turned, True, put)
 
 
-def far_kernel(geometry_ref, out_ref, turned):
+def far_factors(geometry_ref, out, turned):
     def read(at):
         return [geometry_ref[at, 0, i * BLOCK : (i + 1) * BLOCK] for i in range(5)]
 
     def put(at, block):
-        out_ref[at] = block.astype(jnp.bfloat16)
-
-    factor_blocks(read, out_ref.shape[0], turned, False, put)
+        out[at] = block.astype(jnp.bfloat16)
+
+    factor_blocks(read, out.shape[0], turned, False, put)
 
 
 def factors(kernel, arrays, shape):
@@ -493,15 +512,14 @@
 
     lists = (pair_rows, pair_slots, pair_code)
     pairs, steps = pair_list(words(*lists), words(*map(swap, lists)))
+    geometry = exchange(place(asked, jnp.concatenate([*positions, patch_area, facing], axis=1)))
+    area = patch_area[:, None, :]
     near = factors(near_kernel, (positions, patch_area, facing), (blocks, BLOCK, FEATURES))
-    asked, near, pairs, steps = lax.optimization_barrier((asked, near, pairs, steps))
-
-    area = patch_area[:, None, :]
-    exitance, place, send = serve(asked, positions, area, facing, emission)
-    geometry = exchange(place)
-    send, geometry, asked, albedo_class = lax.optimization_barrier((send, geometry, asked, albedo_class))
-    far = factors(far_kernel, (geometry,), (owners, FEATURES, BLOCK))
+    exitance, send = first(asked, area, emission)
     asked_other = swap(asked)
+    send, geometry, near, pairs, steps, asked_other = lax.optimization_barrier(
+        (send, geometry, near, pairs, steps, asked_other)
+    )
 
     class_ids = jnp.arange(NCLASS, dtype=jnp.int32)
     albedo = jnp.sum(
@@ -510,13 +528,14 @@
 
     fetched = exchange(send)
     tiles, back = build(
-        pairs, steps, jnp.asarray(hash_pattern()), near, far, exitance, 2 * pair_rows.shape[0]
+        pairs, steps, jnp.asarray(hash_pattern()), near, geometry, exitance, 2 * pair_rows.shape[0]
     )
 
     def collect(back, fetched):
         got = exchange(back)
         to_rows = rows(pairs, steps, tiles, fetched, blocks)
         base = emission + albedo * (to_rows[:blocks] + swap(to_rows)[:blocks])
+        got, base = lax.optimization_barrier((got, base))
         return own(asked, got, blocks), swap(got), base
 
     exitance, send = middle(asked, asked_other, *collect(back, fetched), albedo, area)

time: 235 us -> 226 us (0.962)
  blocking collectives: 27.6 us -> 0 us
  waiting for transfers between devices: 24.7 us -> 46.2 us
  Pallas kernels: 109 us -> 98.8 us
  local copies, waits for them, and re-layouts: 0.05 us -> 5.39 us
    all_to_all x1 -> x0, blocking collectives: 27.6 us -> none  [exchange(): return lax.all_to_all(array, 'blk', split_axis=0, concat_axis=0, tiled=True)]
    all_to_all x5 -> x6, waiting for transfers between devices: 24.7 us -> 41.3 us  [exchange(): return lax.all_to_all(array, 'blk', split_axis=0, concat_axis=0, tiled=True)]
    all_to_all x5 -> x6, starting transfers between devices: 49.2 us -> 57 us  [exchange(): return lax.all_to_all(array, 'blk', split_axis=0, concat_axis=0, tiled=True)]
    ppermute x8, starting transfers between devices: 20.2 us -> 12.9 us  [swap(): return lax.ppermute(array, 'grp', [(0, 1), (1, 0)])]
    ppermute x8, waiting for transfers between devices: 0.02 us -> 4.9 us  [swap(): return lax.ppermute(array, 'grp', [(0, 1), (1, 0)])]
    unnamed x24 -> x28, local copies, waits for them, and re-layouts: 0.05 us -> 4.63 us
    pallas_call x2 -> x1, Pallas kernels: 7.43 us -> 3.69 us  [factors(): pl.pallas_call(kernel, in_specs=[VMEM_SPEC] * len(arrays), out_specs=VMEM...]
    pallas_call x1, Pallas kernels: 25.2 us -> 21.5 us  [build(): pl.pallas_call(build_kernel, in_specs=[SMEM_SPEC] * 2 + [VMEM_SPEC] * 4,...]
  transfers between devices with their start and end apart: 13 -> 14, of which waited for: 4 -> 7; matrix products, arithmetic and copies ran while one was open for 2% -> 4% of each run, Pallas kernels for 41% -> 38%
where the time goes in v4:
time: 226 us; the launch traced here: 225 us
  Pallas kernels  98.8 us (44%)
  starting transfers between devices  69.9 us (31%)
  waiting for transfers between devices  46.2 us (20%)
  local copies, waits for them, and re-layouts  5.39 us (2%)
  other arithmetic  4.6 us (2%)
    all_to_all x6, starting transfers between devices, exchange(): return lax.all_to_all(array, 'blk', split_axis=0, concat_axis=0, tiled=True)  57 us
    all_to_all x6, waiting for transfers between devices, exchange(): return lax.all_to_all(array, 'blk', split_axis=0, concat_axis=0, tiled=True)  41.3 us
    pallas_call x2, Pallas kernels, rows(): pl.pallas_call(rows_kernel, in_specs=[SMEM_SPEC] * 2 + [ANY_SPEC, VMEM_SP...  35.7 us
    pallas_call x1, Pallas kernels, build(): pl.pallas_call(build_kernel, in_specs=[SMEM_SPEC] * 2 + [VMEM_SPEC] * 4,...  21.5 us
    pallas_call x1, Pallas kernels, columns(): pl.pallas_call(columns_kernel, in_specs=[SMEM_SPEC] * 2 + [ANY_SPEC, VMEM...  13.1 us
    ppermute x8, starting transfers between devices, swap(): return lax.ppermute(array, 'grp', [(0, 1), (1, 0)])  12.9 us
    pallas_call x2, Pallas kernels, own(): pl.pallas_call(own_kernel, in_specs=[SMEM_SPEC, VMEM_SPEC], out_specs=VME...  4.99 us
    ppermute x8, waiting for transfers between devices, swap(): return lax.ppermute(array, 'grp', [(0, 1), (1, 0)])  4.9 us
  transfers between devices with their start and end apart: 14, of which 7 were waited for; matrix products, arithmetic and copies ran while one was open for 4% of the time, Pallas kernels for 38%

profile of v4, /device:TPU:1, one launch (start us, length us, event | category | flops | bytes accessed | tf_op | source)
XLA Modules:
  0.0 225.3 jit_solution(14818007846119192830)
XLA Ops:
  0.0 1.5 shard_map.109
  1.5 16.3 %all-to-all-start = ((s32[128,1,128]{2,1,0:T(1,128)}), s32[128,1,128]{2,1,0:T(1,128)S(1)}, u32[]{:S(2)}, u32[]{:S(2)}) async-start(s32[128,1,128]{2,1,0:T(1,128)} %shard_map.109), calls=%async_computation | async-start | bytes 131072 | tf_op jit(solution)/shard_map/all_to_all | solution.py:502
  17.9 0.8 bitcast_dynamic-update-slice_fusion.2
  18.6 0.8 bitcast_dynamic-update-slice_fusion.1
  19.4 0.8 bitcast_dynamic-update-slice_fusion
  20.2 0.8 constant_dynamic-update-slice_fusion.1
  20.9 0.8 constant_dynamic-update-slice_fusion.geometry_ref
  21.7 6.9 %all-to-all-done = s32[128,1,128]{2,1,0:T(1,128)S(1)} async-done(((s32[128,1,128]{2,1,0:T(1,128)}), s32[128,1,128]{2,1,0:T(1,128)S(1)}, u32[]{:S(2)}, u32[]{:S(2)}) %all-to-all-start) | async-done | bytes 65568 | tf_op jit(solution)/shard_map/all_to_all | solution.py:502
  28.5 2.6 %shard_map.111 = f32[128,1,640]{2,1,0:T(1,128)} custom-call(s32[128,128]{1,0:T(8,128)S(1)} %bitcast.10, f32[64,640]{1,0:T(8,128)S(1)} %constant_dynamic-update-slice_fusion.geometry_ref), custom_call_target="tpu_custom_call" | custom-call | tf_op jit(solution)/shard_map/pallas_call | solution.py:388
  31.2 6.3 %all-to-all-start.1 = ((f32[128,1,640]{2,1,0:T(1,128)}), f32[128,1,640]{2,1,0:T(1,128)S(1)}, u32[]{:S(2)}, u32[]{:S(2)}) async-start(f32[128,1,640]{2,1,0:T(1,128)} %shard_map.111), calls=%async_computation.1 | async-start | bytes 655360 | tf_op jit(solution)/shard_map/all_to_all | solution.py:502
  37.5 2.0 collective-permute-start
  39.6 0.1 collective-permute-start.1
  39.7 0.4 collective-permute-start.2
  40.1 0.6 shift-left_or_fusion.1.mine_ref
  40.7 3.7 %shard_map.112.near_ref = bf16[64,128,32]{2,1,0:T(8,128)(2,1)} custom-call(f32[3,64,128]{2,1,0:T(8,128)} %positions_ref.1, f32[64,128]{1,0:T(8,128)} %area_ref.1, f32[64,128]{1,0:T(8,128)} %facing_ref.1), custom_call_target="tpu_custom_call" | custom-call | flops 10000000 | bytes 8000000 | tf_op jit(solution)/shard_map/pallas_call | solution.py:482
  44.4 0.1 collective-permute-start.3
  44.5 0.6 shift-left_or_fusion.other_ref
  45.1 4.7 %shard_map.113 = (s32[1344]{0:T(1024)}, s32[1]{0:T(128)}) custom-call(s32[640]{0:T(1024)} %shift-left_or_fusion.1.mine_ref, s32[640]{0:T(1024)} %shift-left_or_fusion.other_ref), custom_call_target="tpu_custom_call" | custom-call | flops 10000000 | bytes 10000000 | tf_op jit(solution)/shard_map/pallas_call | solution.py:62
  49.8 2.7 %shard_map.110 = (bf16[64,32,128]{2,1,0:T(8,128)(2,1)S(1)}, bf16[128,32,128]{2,1,0:T(8,128)(2,1)}) custom-call(s32[128,128]{1,0:T(8,128)S(1)} %bitcast.12, f32[64,1,128]{2,1,0:T(1,128)S(1)} %bitcast.18, f32[64,32,128]{2,1,0:T(8,128)S(1)} %copy-done), custom_call_target="tpu_custom_call" | custom-call | flops 10000000 | bytes 8000000 | tf_op jit(solution)/shard_map/pallas_call | solution.py:412
  52.5 0.8 copy-done.3
  53.3 13.5 %all-to-all-start.3 = ((bf16[128,32,128]{2,1,0:T(8,128)(2,1)}), bf16[128,32,128]{2,1,0:T(8,128)(2,1)S(1)}, u32[]{:S(2)}, u32[]{:S(2)}) async-start(bf16[128,32,128]{2,1,0:T(8,128)(2,1)} %get-tuple-element.34), calls=%async_computation.3 | async-start | bytes 2097152 | tf_op jit(solution)/shard_map/all_to_all | solution.py:502
  66.8 21.5 %shard_map.114 = (bf16[1280,128,128]{2,1,0:T(8,128)(2,1)}, s16[128,32,128]{2,1,0:T(8,128)(2,1)}) custom-call(s32[1344]{0:T(1024)} %get-tuple-element.27.list_ref, s32[1]{0:T(128)} %get-tuple-element.28.steps_ref, s32[128,128]{1,0:T(8,128)} %constant.16.clone.pattern_ref, bf16[64,128,32]{2,1,0:T(8,128)(2,1)} %shard_map.112.near_ref, ...), custom_call_target="tpu_custom_call" | custom-call | flops 20000000000 | bytes 60000000 | tf_op jit(solution)/shard_map/pallas_call | solution.py:198
  88.3 7.6 %all-to-all-done.3.ex_ref = bf16[128,32,128]{2,1,0:T(8,128)(2,1)S(1)} async-done(((bf16[128,32,128]{2,1,0:T(8,128)(2,1)}), bf16[128,32,128]{2,1,0:T(8,128)(2,1)S(1)}, u32[]{:S(2)}, u32[]{:S(2)}) %all-to-all-start.3) | async-done | bytes 1048608 | tf_op jit(solution)/shard_map/all_to_all | solution.py:502
  95.9 7.6 %all-to-all-start.2 = ((s16[128,32,128]{2,1,0:T(8,128)(2,1)}), s16[128,32,128]{2,1,0:T(8,128)(2,1)S(1)}, u32[]{:S(2)}, u32[]{:S(2)}) async-start(s16[128,32,128]{2,1,0:T(8,128)(2,1)} %get-tuple-element.33), calls=%async_computation.2 | async-start | bytes 2097152 | tf_op jit(solution)/shard_map/all_to_all | solution.py:502
  103.5 0.0 copy-start.7
  103.5 0.0 copy-start.11
  103.5 17.8 %shard_map.115 = f32[65,32,128]{2,1,0:T(8,128)} custom-call(s32[1344]{0:T(1024)} %get-tuple-element.27.list_ref, s32[1]{0:T(128)} %get-tuple-element.28.steps_ref, bf16[1280,128,128]{2,1,0:T(8,128)(2,1)} %get-tuple-element.32.tiles_ref, bf16[128,32,128]{2,1,0:T(8,128)(2,1)} %copy-done.4), custom_call_target="tpu_custom_call" | custom-call | flops 10000000000 | bytes 40000000 | tf_op jit(solution)/shard_map/pallas_call | solution.py:235
  121.4 0.7 collective-permute-start.4
  122.0 0.1 select_reduce_fusion
  122.2 2.4 %collective-permute-done.4 = f32[65,32,128]{2,1,0:T(8,128)S(1)} collective-permute-done((f32[65,32,128]{2,1,0:T(8,128)}, f32[65,32,128]{2,1,0:T(8,128)S(1)}, u32[]{:S(2)}, u32[]{:S(2)}) %collective-permute-start.4) | collective-permute-done | bytes 1064992 | tf_op jit(solution)/shard_map/ppermute | solution.py:505
  124.6 1.6 fusion.3.base_ref
  126.2 5.0 %all-to-all-done.2.got_ref = s16[128,32,128]{2,1,0:T(8,128)(2,1)S(1)} async-done(((s16[128,32,128]{2,1,0:T(8,128)(2,1)}), s16[128,32,128]{2,1,0:T(8,128)(2,1)S(1)}, u32[]{:S(2)}, u32[]{:S(2)}) %all-to-all-start.2) | async-done | bytes 1048608 | tf_op jit(solution)/shard_map/all_to_all | solution.py:502
  131.2 4.6 %collective-permute-start.5 = (s16[128,32,128]{2,1,0:T(8,128)(2,1)S(1)}, s16[128,32,128]{2,1,0:T(8,128)(2,1)S(1)}, u32[]{:S(2)}, u32[]{:S(2)}) collective-permute-start(s16[128,32,128]{2,1,0:T(8,128)(2,1)S(1)} %all-to-all-done.2.got_ref), channel_id=1, source_target_pairs={{0,1},{1,0},{2,3},{3,2},{4,5},{5,4},{6,7},{7,6},{8,9},{9,8},{10,11... | collective-permute-start | bytes 3145736 | tf_op jit(solution)/shard_map/ppermute | solution.py:505
  135.7 2.5 %shard_map.116.own_ref = f32[64,32,128]{2,1,0:T(8,128)S(1)} custom-call(s32[128,128]{1,0:T(8,128)S(1)} %bitcast.13, s16[128,32,128]{2,1,0:T(8,128)(2,1)S(1)} %all-to-all-done.2.got_ref), custom_call_target="tpu_custom_call" | custom-call | flops 10000000 | bytes 4000000 | tf_op jit(solution)/shard_map/pallas_call | solution.py:260
  138.2 4.8 %shard_map.117 = (bf16[64,32,128]{2,1,0:T(8,128)(2,1)S(1)}, bf16[128,32,128]{2,1,0:T(8,128)(2,1)}) custom-call(s32[128,128]{1,0:T(8,128)S(1)} %bitcast.14, s32[128,128]{1,0:T(8,128)S(1)} %collective-permute-done.3.asked_other_ref, f32[64,32,128]{2,1,0:T(8,128)S(1)} %shard_map.116.own_ref, s16[128,32,128]{2,1,0:T(8,128)(2,1)S(1)} %collective-permute-done.5.got_ref, ...), custom_call_target="tpu_custom_call" | custom-call | tf_op jit(solution)/shard_map/pallas_call | solution.py:289
  143.0 0.8 copy-done.1
  143.8 6.2 %all-to-all-start.5 = ((bf16[128,32,128]{2,1,0:T(8,128)(2,1)}), bf16[128,32,128]{2,1,0:T(8,128)(2,1)S(1)}, u32[]{:S(2)}, u32[]{:S(2)}) async-start(bf16[128,32,128]{2,1,0:T(8,128)(2,1)} %get-tuple-element.38), calls=%async_computation.5 | async-start | bytes 2097152 | tf_op jit(solution)/shard_map/all_to_all | solution.py:502
  150.0 13.1 %shard_map.118 = s16[128,32,128]{2,1,0:T(8,128)(2,1)} custom-call(s32[1344]{0:T(1024)} %get-tuple-element.27.list_ref, s32[1]{0:T(128)} %get-tuple-element.28.steps_ref, bf16[1280,128,128]{2,1,0:T(8,128)(2,1)} %get-tuple-element.32.tiles_ref, bf16[64,32,128]{2,1,0:T(8,128)(2,1)} %copy-done.1), custom_call_target="tpu_custom_call" | custom-call | flops 10000000000 | bytes 40000000 | tf_op jit(solution)/shard_map/pallas_call | solution.py:222
  163.1 16.7 %all-to-all-done.5.ex_ref = bf16[128,32,128]{2,1,0:T(8,128)(2,1)S(1)} async-done(((bf16[128,32,128]{2,1,0:T(8,128)(2,1)}), bf16[128,32,128]{2,1,0:T(8,128)(2,1)S(1)}, u32[]{:S(2)}, u32[]{:S(2)}) %all-to-all-start.5) | async-done | bytes 1048608 | tf_op jit(solution)/shard_map/all_to_all | solution.py:502
  179.8 7.1 %all-to-all-start.4 = ((s16[128,32,128]{2,1,0:T(8,128)(2,1)}), s16[128,32,128]{2,1,0:T(8,128)(2,1)S(1)}, u32[]{:S(2)}, u32[]{:S(2)}) async-start(s16[128,32,128]{2,1,0:T(8,128)(2,1)} %shard_map.118), calls=%async_computation.4 | async-start | bytes 2097152 | tf_op jit(solution)/shard_map/all_to_all | solution.py:502
  186.9 17.8 %shard_map.119 = f32[65,32,128]{2,1,0:T(8,128)} custom-call(s32[1344]{0:T(1024)} %get-tuple-element.27.list_ref, s32[1]{0:T(128)} %get-tuple-element.28.steps_ref, bf16[1280,128,128]{2,1,0:T(8,128)(2,1)} %get-tuple-element.32.tiles_ref, bf16[128,32,128]{2,1,0:T(8,128)(2,1)} %copy-done.5), custom_call_target="tpu_custom_call" | custom-call | flops 10000000000 | bytes 40000000 | tf_op jit(solution)/shard_map/pallas_call | solution.py:235
  204.7 0.6 collective-permute-start.6
  205.3 2.5 %collective-permute-done.6 = f32[65,32,128]{2,1,0:T(8,128)S(1)} collective-permute-done((f32[65,32,128]{2,1,0:T(8,128)}, f32[65,32,128]{2,1,0:T(8,128)S(1)}, u32[]{:S(2)}, u32[]{:S(2)}) %collective-permute-start.6) | collective-permute-done | bytes 1064992 | tf_op jit(solution)/shard_map/ppermute | solution.py:505
  207.8 1.6 fusion.1.base_ref
  209.4 5.2 %all-to-all-done.4.got_ref = s16[128,32,128]{2,1,0:T(8,128)(2,1)S(1)} async-done(((s16[128,32,128]{2,1,0:T(8,128)(2,1)}), s16[128,32,128]{2,1,0:T(8,128)(2,1)S(1)}, u32[]{:S(2)}, u32[]{:S(2)}) %all-to-all-start.4) | async-done | bytes 1048608 | tf_op jit(solution)/shard_map/all_to_all | solution.py:502
  214.6 4.4 %collective-permute-start.7 = (s16[128,32,128]{2,1,0:T(8,128)(2,1)S(1)}, s16[128,32,128]{2,1,0:T(8,128)(2,1)S(1)}, u32[]{:S(2)}, u32[]{:S(2)}) collective-permute-start(s16[128,32,128]{2,1,0:T(8,128)(2,1)S(1)} %all-to-all-done.4.got_ref), channel_id=1, source_target_pairs={{0,1},{1,0},{2,3},{3,2},{4,5},{5,4},{6,7},{7,6},{8,9},{9,8},{10,11... | collective-permute-start | bytes 3145736 | tf_op jit(solution)/shard_map/ppermute | solution.py:505
  219.1 2.5 %shard_map.120.own_ref = f32[64,32,128]{2,1,0:T(8,128)S(1)} custom-call(s32[128,128]{1,0:T(8,128)S(1)} %bitcast.15, s16[128,32,128]{2,1,0:T(8,128)(2,1)S(1)} %all-to-all-done.4.got_ref), custom_call_target="tpu_custom_call" | custom-call | flops 10000000 | bytes 4000000 | tf_op jit(solution)/shard_map/pallas_call | solution.py:260
  221.6 3.5 %shard_map.121 = f32[64,32,128]{2,1,0:T(8,128)} custom-call(s32[128,128]{1,0:T(8,128)S(1)} %collective-permute-done.3.asked_other_ref, f32[64,32,128]{2,1,0:T(8,128)S(1)} %shard_map.120.own_ref, s16[128,32,128]{2,1,0:T(8,128)(2,1)S(1)} %collective-permute-done.7.got_ref, f32[64,32,128]{2,1,0:T(8,128)S(1)} %fusion.1.base_ref, f32[64,1,128]{2,1,0:T(1,128)S(1)} %bitcast.17), custom_call_target="tpu_custom_call" | custom-call | tf_op jit(solution)/shard_map/pallas_call | solution.py:322
  (27 shorter events, 0.1 us)
Async XLA Ops:
  0.0 37.5 %copy-start.8 = (s32[640]{0:T(1024)S(1)}, s32[640]{0:T(1024)}, u32[]{:S(2)}) copy-start(s32[640]{0:T(1024)} %param.18) | copy-start | bytes 7684
  0.0 39.6 %copy-start.9 = (s32[640]{0:T(1024)S(1)}, s32[640]{0:T(1024)}, u32[]{:S(2)}) copy-start(s32[640]{0:T(1024)} %param.19) | copy-start | bytes 7684
  0.0 39.7 %copy-start.10 = (s32[640]{0:T(1024)S(1)}, s32[640]{0:T(1024)}, u32[]{:S(2)}) copy-start(s32[640]{0:T(1024)} %param.20) | copy-start | bytes 7684
  1.5 27.0 %all-to-all-start = ((s32[128,1,128]{2,1,0:T(1,128)}), s32[128,1,128]{2,1,0:T(1,128)S(1)}, u32[]{:S(2)}, u32[]{:S(2)}) async-start(s32[128,1,128]{2,1,0:T(1,128)} %shard_map.109), calls=%async_computation | async-start | bytes 131072 | tf_op jit(solution)/shard_map/all_to_all | solution.py:502
  31.2 22.1 %all-to-all-start.1 = ((f32[128,1,640]{2,1,0:T(1,128)}), f32[128,1,640]{2,1,0:T(1,128)S(1)}, u32[]{:S(2)}, u32[]{:S(2)}) async-start(f32[128,1,640]{2,1,0:T(1,128)} %shard_map.111), calls=%async_computation.1 | async-start | bytes 655360 | tf_op jit(solution)/shard_map/all_to_all | solution.py:502
  37.5 7.0 %collective-permute-start = (s32[640]{0:T(1024)S(1)}, s32[640]{0:T(1024)S(1)}, u32[]{:S(2)}, u32[]{:S(2)}) collective-permute-start(s32[640]{0:T(1024)S(1)} %copy-done.8), channel_id=1, source_target_pairs={{0,1},{1,0},{2,3},{3,2},{4,5},{5,4},{6,7},{7,6},{8,9},{9,8},{10,11... | collective-permute-start | bytes 7688 | tf_op jit(solution)/shard_map/ppermute | solution.py:505
  39.6 4.9 %collective-permute-start.1 = (s32[640]{0:T(1024)S(1)}, s32[640]{0:T(1024)S(1)}, u32[]{:S(2)}, u32[]{:S(2)}) collective-permute-start(s32[640]{0:T(1024)S(1)} %copy-done.9), channel_id=1, source_target_pairs={{0,1},{1,0},{2,3},{3,2},{4,5},{5,4},{6,7},{7,6},{8,9},{9,8},{10,11... | collective-permute-start | bytes 7688 | tf_op jit(solution)/shard_map/ppermute | solution.py:505
  39.7 4.8 %collective-permute-start.2 = (s32[640]{0:T(1024)S(1)}, s32[640]{0:T(1024)S(1)}, u32[]{:S(2)}, u32[]{:S(2)}) collective-permute-start(s32[640]{0:T(1024)S(1)} %copy-done.10), channel_id=1, source_target_pairs={{0,1},{1,0},{2,3},{3,2},{4,5},{5,4},{6,7},{7,6},{8,9},{9,8},{10,11... | collective-permute-start | bytes 7688 | tf_op jit(solution)/shard_map/ppermute | solution.py:505
  40.7 9.1 %copy-start = (f32[64,32,128]{2,1,0:T(8,128)S(1)}, f32[64,32,128]{2,1,0:T(8,128)}, u32[]{:S(2)}) copy-start(f32[64,32,128]{2,1,0:T(8,128)} %emission_ref.1) | copy-start | bytes 3145732
  40.7 9.1 %copy-start.2 = (f32[64,128]{1,0:T(8,128)S(1)}, f32[64,128]{1,0:T(8,128)}, u32[]{:S(2)}) copy-start(f32[64,128]{1,0:T(8,128)} %area_ref.1) | copy-start | bytes 98308
  44.4 8.9 %collective-permute-start.3 = (s32[128,128]{1,0:T(8,128)S(1)}, s32[128,128]{1,0:T(8,128)S(1)}, u32[]{:S(2)}, u32[]{:S(2)}) collective-permute-start(s32[128,128]{1,0:T(8,128)S(1)} %bitcast.11), channel_id=1, source_target_pairs={{0,1},{1,0},{2,3},{3,2},{4,5},{5,4},{6,7},{7,6},{8,9},{9,8},{10,11... | collective-permute-start | bytes 196616 | tf_op jit(solution)/shard_map/ppermute | solution.py:505
  52.5 0.8 copy-start.3
  53.3 13.5 %copy-start.6 = (f32[128,1,640]{2,1,0:T(1,128)}, f32[128,1,640]{2,1,0:T(1,128)S(1)}, u32[]{:S(2)}) copy-start(f32[128,1,640]{2,1,0:T(1,128)S(1)} %all-to-all-done.1.geometry_ref) | copy-start | bytes 983044
  53.3 42.6 %all-to-all-start.3 = ((bf16[128,32,128]{2,1,0:T(8,128)(2,1)}), bf16[128,32,128]{2,1,0:T(8,128)(2,1)S(1)}, u32[]{:S(2)}, u32[]{:S(2)}) async-start(bf16[128,32,128]{2,1,0:T(8,128)(2,1)} %get-tuple-element.34), calls=%async_computation.3 | async-start | bytes 2097152 | tf_op jit(solution)/shard_map/all_to_all | solution.py:502
  95.9 7.6 %copy-start.4 = (bf16[128,32,128]{2,1,0:T(8,128)(2,1)}, bf16[128,32,128]{2,1,0:T(8,128)(2,1)S(1)}, u32[]{:S(2)}) copy-start(bf16[128,32,128]{2,1,0:T(8,128)(2,1)S(1)} %all-to-all-done.3.ex_ref) | copy-start | bytes 3145732
  95.9 35.3 %all-to-all-start.2 = ((s16[128,32,128]{2,1,0:T(8,128)(2,1)}), s16[128,32,128]{2,1,0:T(8,128)(2,1)S(1)}, u32[]{:S(2)}, u32[]{:S(2)}) async-start(s16[128,32,128]{2,1,0:T(8,128)(2,1)} %get-tuple-element.33), calls=%async_computation.2 | async-start | bytes 2097152 | tf_op jit(solution)/shard_map/all_to_all | solution.py:502
  103.5 18.5 %copy-start.7 = (s32[64,128]{1,0:T(8,128)S(1)}, s32[64,128]{1,0:T(8,128)}, u32[]{:S(2)}) copy-start(s32[64,128]{1,0:T(8,128)} %param.15) | copy-start | bytes 98308
  103.5 18.5 %copy-start.11 = (f32[8]{0:T(128)S(1)}, f32[8]{0:T(128)}, u32[]{:S(2)}) copy-start(f32[8]{0:T(128)} %param.16) | copy-start | bytes 100
  121.4 3.2 %collective-permute-start.4 = (f32[65,32,128]{2,1,0:T(8,128)}, f32[65,32,128]{2,1,0:T(8,128)S(1)}, u32[]{:S(2)}, u32[]{:S(2)}) collective-permute-start(f32[65,32,128]{2,1,0:T(8,128)} %shard_map.115), channel_id=1, source_target_pairs={{0,1},{1,0},{2,3},{3,2},{4,5},{5,4},{6,7},{7,6},{8,9},{9,8},{10,11... | collective-permute-start | bytes 3194888 | tf_op jit(solution)/shard_map/ppermute | solution.py:505
  131.2 7.1 %collective-permute-start.5 = (s16[128,32,128]{2,1,0:T(8,128)(2,1)S(1)}, s16[128,32,128]{2,1,0:T(8,128)(2,1)S(1)}, u32[]{:S(2)}, u32[]{:S(2)}) collective-permute-start(s16[128,32,128]{2,1,0:T(8,128)(2,1)S(1)} %all-to-all-done.2.got_ref), channel_id=1, source_target_pairs={{0,1},{1,0},{2,3},{3,2},{4,5},{5,4},{6,7},{7,6},{8,9},{9,8},{10,11... | collective-permute-start | bytes 3145736 | tf_op jit(solution)/shard_map/ppermute | solution.py:505
  143.0 0.8 copy-start.1
  143.8 36.0 %all-to-all-start.5 = ((bf16[128,32,128]{2,1,0:T(8,128)(2,1)}), bf16[128,32,128]{2,1,0:T(8,128)(2,1)S(1)}, u32[]{:S(2)}, u32[]{:S(2)}) async-start(bf16[128,32,128]{2,1,0:T(8,128)(2,1)} %get-tuple-element.38), calls=%async_computation.5 | async-start | bytes 2097152 | tf_op jit(solution)/shard_map/all_to_all | solution.py:502
  179.8 7.1 %copy-start.5 = (bf16[128,32,128]{2,1,0:T(8,128)(2,1)}, bf16[128,32,128]{2,1,0:T(8,128)(2,1)S(1)}, u32[]{:S(2)}) copy-start(bf16[128,32,128]{2,1,0:T(8,128)(2,1)S(1)} %all-to-all-done.5.ex_ref) | copy-start | bytes 3145732
  179.8 34.9 %all-to-all-start.4 = ((s16[128,32,128]{2,1,0:T(8,128)(2,1)}), s16[128,32,128]{2,1,0:T(8,128)(2,1)S(1)}, u32[]{:S(2)}, u32[]{:S(2)}) async-start(s16[128,32,128]{2,1,0:T(8,128)(2,1)} %shard_map.118), calls=%async_computation.4 | async-start | bytes 2097152 | tf_op jit(solution)/shard_map/all_to_all | solution.py:502
  204.7 3.1 %collective-permute-start.6 = (f32[65,32,128]{2,1,0:T(8,128)}, f32[65,32,128]{2,1,0:T(8,128)S(1)}, u32[]{:S(2)}, u32[]{:S(2)}) collective-permute-start(f32[65,32,128]{2,1,0:T(8,128)} %shard_map.119), channel_id=1, source_target_pairs={{0,1},{1,0},{2,3},{3,2},{4,5},{5,4},{6,7},{7,6},{8,9},{9,8},{10,11... | collective-permute-start | bytes 3194888 | tf_op jit(solution)/shard_map/ppermute | solution.py:505
  214.6 7.0 %collective-permute-start.7 = (s16[128,32,128]{2,1,0:T(8,128)(2,1)S(1)}, s16[128,32,128]{2,1,0:T(8,128)(2,1)S(1)}, u32[]{:S(2)}, u32[]{:S(2)}) collective-permute-start(s16[128,32,128]{2,1,0:T(8,128)(2,1)S(1)} %all-to-all-done.4.got_ref), channel_id=1, source_target_pairs={{0,1},{1,0},{2,3},{3,2},{4,5},{5,4},{6,7},{7,6},{8,9},{9,8},{10,11... | collective-permute-start | bytes 3145736 | tf_op jit(solution)/shard_map/ppermute | solution.py:505

commit v5 on v4

--- a/solution.py
+++ b/solution.py
@@ -39,7 +39,10 @@
     return lax.shift_right_logical(word, jnp.int32(7)) & 255
 
 
-def list_kernel(mine_ref, other_ref, list_ref, steps_ref):
+def list_kernel(mine_ref, other_ref, asked_ref, list_ref, steps_ref, short_ref):
+    for owner in range(asked_ref.shape[0]):
+        short_ref[owner] = asked_ref[owner, 0]
+
     def take_from(words_ref):
         def take(turn, count):
             for j in range(8):
@@ -58,17 +61,18 @@
     steps_ref[0] = jnp.maximum((count + UNROLL - 1) // UNROLL, 1)
 
 
-def pair_list(mine, other):
+def pair_list(mine, other, asked):
     return pl.pallas_call(
         list_kernel,
         out_shape=(
             jax.ShapeDtypeStruct((2 * mine.shape[0] + UNROLL,), jnp.int32),
             jax.ShapeDtypeStruct((1,), jnp.int32),
+            jax.ShapeDtypeStruct((asked.shape[0],), jnp.int32),
         ),
-        in_specs=[SMEM_SPEC] * 2,
-        out_specs=(SMEM_SPEC, SMEM_SPEC),
+        in_specs=[SMEM_SPEC] * 3,
+        out_specs=(SMEM_SPEC,) * 3,
         cost_estimate=pl.CostEstimate(flops=10_000_000, bytes_accessed=10_000_000, transcendentals=0),
-    )(mine, other)
+    )(mine, other, asked)
 
 
 def encode(acc, out_ref):
@@ -245,7 +249,7 @@
 
 def add_asked(acc, asked_ref, got_ref):
     def add(at, carry):
-        acc[asked_ref[at, 0]] += decode(got_ref[at])
+        acc[asked_ref[at]] += decode(got_ref[at])
         return carry
 
     lax.fori_loop(0, got_ref.shape[0], add, 0, unroll=8)
@@ -291,8 +295,8 @@
         in_specs=[SMEM_SPEC] * 2 + [VMEM_SPEC] * 5,
         out_specs=[HBM_SPEC] * 2,
         out_shape=[
-            jax.ShapeDtypeStruct((blocks, hours, block), jnp.bfloat16),
-            jax.ShapeDtypeStruct((owners, hours, block), jnp.bfloat16),
+            pltpu.HBM((blocks, hours, block), jnp.bfloat16),
+            pltpu.HBM((owners, hours, block), jnp.bfloat16),
         ],
         scratch_shapes=[
             pltpu.VMEM((blocks, hours, block), jnp.float32),
@@ -361,7 +365,7 @@
     size = send.shape[0] // PARTS
 
     def put(at, carry):
-        send[at] = ex_ref[asked_ref[at, 0]]
+        send[at] = ex_ref[asked_ref[at]]
         return carry
 
     for i, copy in enumerate(copies):
@@ -398,11 +402,14 @@
     )(asked, geometry)
 
 
-def first_kernel(asked_ref, area_ref, emission_ref, ex_ref, send_ref, send, sems):
-    ex_ref[...] = (area_ref[...] * emission_ref[...]).astype(jnp.bfloat16)
-    copies = part_copies(send, send_ref, sems)
-    put_asked(asked_ref, ex_ref, send, copies)
-    for copy in copies:
+def first_kernel(asked_ref, area_ref, emission_ref, ex_out_ref, send_ref, ex, send, ex_sems, send_sems):
+    ex[...] = (area_ref[...] * emission_ref[...]).astype(jnp.bfloat16)
+    ex_copies = part_copies(ex, ex_out_ref, ex_sems)
+    send_copies = part_copies(send, send_ref, send_sems)
+    put_asked(asked_ref, ex, send, send_copies)
+    for copy in ex_copies:
+        copy.start()
+    for copy in ex_copies + send_copies:
         copy.wait()
 
 
@@ -412,13 +419,15 @@
     return pl.pallas_call(
         first_kernel,
         in_specs=[SMEM_SPEC] + [VMEM_SPEC] * 2,
-        out_specs=[VMEM_SPEC, HBM_SPEC],
+        out_specs=[HBM_SPEC] * 2,
         out_shape=[
-            jax.ShapeDtypeStruct((blocks, hours, block), jnp.bfloat16),
-            jax.ShapeDtypeStruct((owners, hours, block), jnp.bfloat16),
+            pltpu.HBM((blocks, hours, block), jnp.bfloat16),
+            pltpu.HBM((owners, hours, block), jnp.bfloat16),
         ],
         scratch_shapes=[
+            pltpu.VMEM((blocks, hours, block), jnp.bfloat16),
             pltpu.VMEM((owners, hours, block), jnp.bfloat16),
+            pltpu.SemaphoreType.DMA((PARTS,)),
             pltpu.SemaphoreType.DMA((PARTS,)),
         ],
         compiler_params=pltpu.CompilerParams(vmem_limit_bytes=VMEM // 4),
@@ -458,7 +467,11 @@
     lax.fori_loop(0, count // 8, group, 0)
 
 
-def near_kernel(positions_ref, area_ref, facing_ref, out_ref, turned):
+def near_kernel(positions_ref, area_ref, facing_ref, out_ref, geometry_ref, turned):
+    parts = [positions_ref[i] for i in range(3)] + [area_ref[...], facing_ref[...]]
+    for i, part in enumerate(parts):
+        geometry_ref[:, i * BLOCK : (i + 1) * BLOCK] = part
+
     def read(at):
         return [positions_ref[i, at, :] for i in range(3)] + [area_ref[at, :], facing_ref[at, :]]
 
@@ -478,16 +491,20 @@
     factor_blocks(read, out.shape[0], turned, False, put)
 
 
-def factors(kernel, arrays, shape):
-    return pl.pallas_call(
-        kernel,
-        in_specs=[VMEM_SPEC] * len(arrays),
-        out_specs=VMEM_SPEC,
-        out_shape=jax.ShapeDtypeStruct(shape, jnp.bfloat16),
+def near_factors(positions, patch_area, facing):
+    blocks = patch_area.shape[0]
+    return pl.pallas_call(
+        near_kernel,
+        in_specs=[VMEM_SPEC] * 3,
+        out_specs=[VMEM_SPEC] * 2,
+        out_shape=[
+            jax.ShapeDtypeStruct((blocks, BLOCK, FEATURES), jnp.bfloat16),
+            jax.ShapeDtypeStruct((blocks, 5 * BLOCK), jnp.float32),
+        ],
         scratch_shapes=[pltpu.VMEM((8 * FEATURES, BLOCK), jnp.float32)],
-        compiler_params=pltpu.CompilerParams(vmem_limit_bytes=VMEM),
+        compiler_params=pltpu.CompilerParams(vmem_limit_bytes=VMEM // 4),
         cost_estimate=pl.CostEstimate(flops=10_000_000, bytes_accessed=8_000_000, transcendentals=0),
-    )(*arrays)
+    )(positions, patch_area, facing)
 
 
 def local(
@@ -504,19 +521,19 @@
     def swap(array):
         return lax.ppermute(array, "grp", [(0, 1), (1, 0)])
 
-    asked = exchange(ask(core, fetch_block, owners)).reshape(owners, BLOCK)
+    asked_rows = exchange(ask(core, fetch_block, owners)).reshape(owners, BLOCK)
+    near, own_geometry = near_factors(positions, patch_area, facing)
+    geometry = exchange(place(asked_rows, own_geometry))
 
     def words(pair_row, pair_slot, code):
         skip = (pair_slot & 1) ^ core
         return pair_row | (skip << 6) | ((pair_slot >> 1) << 7) | jnp.left_shift(code, 15)
 
     lists = (pair_rows, pair_slots, pair_code)
-    pairs, steps = pair_list(words(*lists), words(*map(swap, lists)))
-    geometry = exchange(place(asked, jnp.concatenate([*positions, patch_area, facing], axis=1)))
+    pairs, steps, asked = pair_list(words(*lists), words(*map(swap, lists)), asked_rows)
+    asked_other = swap(asked)
     area = patch_area[:, None, :]
-    near = factors(near_kernel, (positions, patch_area, facing), (blocks, BLOCK, FEATURES))
     exitance, send = first(asked, area, emission)
-    asked_other = swap(asked)
     send, geometry, near, pairs, steps, asked_other = lax.optimization_barrier(
         (send, geometry, near, pairs, steps, asked_other)
     )

time: 226 us -> 220 us (0.973)
  Pallas kernels: 98.8 us -> 87.9 us
  starting transfers between devices: 69.9 us -> 74.1 us
    ppermute x8, starting transfers between devices: 12.9 us -> 17.7 us  [swap(): return lax.ppermute(array, 'grp', [(0, 1), (1, 0)])]
    pallas_call x1, Pallas kernels: 3.69 us -> 1.33 us  [near_factors(): pl.pallas_call(near_kernel, in_specs=[VMEM_SPEC] * 3, out_specs=[VMEM_SPE...]
    unnamed x28 -> x34, local copies, waits for them, and re-layouts: 4.63 us -> 4.43 us
  transfers between devices with their start and end apart: 14 -> 14, of which waited for: 7 -> 12; matrix products, arithmetic and copies ran while one was open for 4% -> 2% of each run, Pallas kernels for 38% -> 36%
where the time goes in v5:
time: 220 us; the launch traced here: 219 us
  Pallas kernels  87.9 us (40%)
  starting transfers between devices  74.1 us (34%)
  waiting for transfers between devices  47.7 us (22%)
  local copies, waits for them, and re-layouts  4.43 us (2%)
  other arithmetic  4.38 us (2%)
    all_to_all x6, starting transfers between devices, exchange(): return lax.all_to_all(array, 'blk', split_axis=0, concat_axis=0, tiled=True)  56.5 us
    all_to_all x6, waiting for transfers between devices, exchange(): return lax.all_to_all(array, 'blk', split_axis=0, concat_axis=0, tiled=True)  40.9 us
    pallas_call x2, Pallas kernels, rows(): pl.pallas_call(rows_kernel, in_specs=[SMEM_SPEC] * 2 + [ANY_SPEC, VMEM_SP...  33.5 us
    pallas_call x1, Pallas kernels, build(): pl.pallas_call(build_kernel, in_specs=[SMEM_SPEC] * 2 + [VMEM_SPEC] * 4,...  20.5 us
    ppermute x8, starting transfers between devices, swap(): return lax.ppermute(array, 'grp', [(0, 1), (1, 0)])  17.7 us
    pallas_call x1, Pallas kernels, columns(): pl.pallas_call(columns_kernel, in_specs=[SMEM_SPEC] * 2 + [ANY_SPEC, VMEM...  12.5 us
    ppermute x8, waiting for transfers between devices, swap(): return lax.ppermute(array, 'grp', [(0, 1), (1, 0)])  6.79 us
    pallas_call x1, Pallas kernels, pair_list(): pl.pallas_call(list_kernel, out_shape=(jax.ShapeDtypeStruct((2 * mine.sha...  5.83 us
  transfers between devices with their start and end apart: 14, of which 12 were waited for; matrix products, arithmetic and copies ran while one was open for 2% of the time, Pallas kernels for 36%

profile of v5, /device:TPU:1, one launch (start us, length us, event | category | flops | bytes accessed | tf_op | source)
XLA Modules:
  0.0 218.9 jit_solution(9957599408871561464)
XLA Ops:
  0.0 1.5 shard_map.109
  1.5 16.3 %all-to-all-start = ((s32[128,1,128]{2,1,0:T(1,128)}), s32[128,1,128]{2,1,0:T(1,128)S(1)}, u32[]{:S(2)}, u32[]{:S(2)}) async-start(s32[128,1,128]{2,1,0:T(1,128)} %shard_map.109), calls=%async_computation | async-start | bytes 131072 | tf_op jit(solution)/shard_map/all_to_all | solution.py:519
  17.9 0.7 copy-done.2
  18.6 0.9 copy-done.4
  19.5 0.8 copy-done.5
  20.3 1.3 shard_map.112
  21.6 1.4 copy-done.8
  23.0 5.5 %all-to-all-done = s32[128,1,128]{2,1,0:T(1,128)S(1)} async-done(((s32[128,1,128]{2,1,0:T(1,128)}), s32[128,1,128]{2,1,0:T(1,128)S(1)}, u32[]{:S(2)}, u32[]{:S(2)}) %all-to-all-start) | async-done | bytes 65568 | tf_op jit(solution)/shard_map/all_to_all | solution.py:519
  28.5 2.6 %shard_map.113 = f32[128,1,640]{2,1,0:T(1,128)} custom-call(s32[128,128]{1,0:T(8,128)S(1)} %bitcast.6, f32[64,640]{1,0:T(8,128)S(1)} %get-tuple-element.28.geometry_ref), custom_call_target="tpu_custom_call" | custom-call | tf_op jit(solution)/shard_map/pallas_call | solution.py:392
  31.2 7.7 %all-to-all-start.1 = ((f32[128,1,640]{2,1,0:T(1,128)}), f32[128,1,640]{2,1,0:T(1,128)S(1)}, u32[]{:S(2)}, u32[]{:S(2)}) async-start(f32[128,1,640]{2,1,0:T(1,128)} %shard_map.113), calls=%async_computation.1 | async-start | bytes 655360 | tf_op jit(solution)/shard_map/all_to_all | solution.py:519
  38.8 1.6 collective-permute-start
  40.4 0.1 collective-permute-start.1
  40.6 0.4 collective-permute-start.2
  41.0 0.6 shift-left_or_fusion.1.mine_ref
  41.6 0.2 collective-permute-done.2
  41.8 0.6 shift-left_or_fusion.other_ref
  42.4 5.8 %shard_map.110 = (s32[1344]{0:T(1024)}, s32[1]{0:T(128)}, s32[128]{0:T(128)}) custom-call(s32[640]{0:T(1024)} %shift-left_or_fusion.1.mine_ref, s32[640]{0:T(1024)} %shift-left_or_fusion.other_ref, s32[128,128]{1,0:T(8,128)} %bitcast.7), custom_call_target="tpu_custom_call" | custom-call | flops 10000000 | bytes 10000000 | tf_op jit(solution)/shard_map/pallas_call | solution.py:65
  48.2 0.4 collective-permute-start.3
  48.7 0.6 copy-done.6
  49.3 1.9 shard_map.111
  51.1 1.7 all-to-all-done.1.geometry_ref
  52.9 11.8 %all-to-all-start.3 = ((bf16[128,32,128]{2,1,0:T(8,128)(2,1)}), bf16[128,32,128]{2,1,0:T(8,128)(2,1)S(1)}, u32[]{:S(2)}, u32[]{:S(2)}) async-start(bf16[128,32,128]{2,1,0:T(8,128)(2,1)} %get-tuple-element.40), calls=%async_computation.3 | async-start | bytes 2097152 | tf_op jit(solution)/shard_map/all_to_all | solution.py:519
  64.7 20.5 %shard_map.114 = (bf16[1280,128,128]{2,1,0:T(8,128)(2,1)}, s16[128,32,128]{2,1,0:T(8,128)(2,1)}) custom-call(s32[1344]{0:T(1024)} %get-tuple-element.33.list_ref, s32[1]{0:T(128)} %get-tuple-element.34.steps_ref, s32[128,128]{1,0:T(8,128)} %constant.16.clone.pattern_ref, bf16[64,128,32]{2,1,0:T(8,128)(2,1)} %copy-done.8, f32[128,1,640]{2,1,0:T(1,128)} %copy-done.11, ...), custom_call_target="tpu_custom_call" | custom-call | flops 20000000000 | bytes 60000000 | tf_op jit(solution)/shard_map/pallas_call | solution.py:202
  85.2 8.9 %all-to-all-done.3.ex_ref = bf16[128,32,128]{2,1,0:T(8,128)(2,1)S(1)} async-done(((bf16[128,32,128]{2,1,0:T(8,128)(2,1)}), bf16[128,32,128]{2,1,0:T(8,128)(2,1)S(1)}, u32[]{:S(2)}, u32[]{:S(2)}) %all-to-all-start.3) | async-done | bytes 1048608 | tf_op jit(solution)/shard_map/all_to_all | solution.py:519
  94.1 7.3 %all-to-all-start.2 = ((s16[128,32,128]{2,1,0:T(8,128)(2,1)}), s16[128,32,128]{2,1,0:T(8,128)(2,1)S(1)}, u32[]{:S(2)}, u32[]{:S(2)}) async-start(s16[128,32,128]{2,1,0:T(8,128)(2,1)} %get-tuple-element.39), calls=%async_computation.2 | async-start | bytes 2097152 | tf_op jit(solution)/shard_map/all_to_all | solution.py:519
  101.5 16.8 %shard_map.115 = f32[65,32,128]{2,1,0:T(8,128)} custom-call(s32[1344]{0:T(1024)} %get-tuple-element.33.list_ref, s32[1]{0:T(128)} %get-tuple-element.34.steps_ref, bf16[1280,128,128]{2,1,0:T(8,128)(2,1)} %get-tuple-element.38.tiles_ref, bf16[128,32,128]{2,1,0:T(8,128)(2,1)} %copy-done.9), custom_call_target="tpu_custom_call" | custom-call | flops 10000000000 | bytes 40000000 | tf_op jit(solution)/shard_map/pallas_call | solution.py:239
  118.2 3.2 %collective-permute-start.4 = (f32[65,32,128]{2,1,0:T(8,128)}, f32[65,32,128]{2,1,0:T(8,128)S(1)}, u32[]{:S(2)}, u32[]{:S(2)}) collective-permute-start(f32[65,32,128]{2,1,0:T(8,128)} %shard_map.115), channel_id=1, source_target_pairs={{0,1},{1,0},{2,3},{3,2},{4,5},{5,4},{6,7},{7,6},{8,9},{9,8},{10,11... | collective-permute-start | bytes 3194888 | tf_op jit(solution)/shard_map/ppermute | solution.py:522
  121.4 0.1 select_reduce_fusion
  121.6 2.4 %collective-permute-done.4 = f32[65,32,128]{2,1,0:T(8,128)S(1)} collective-permute-done((f32[65,32,128]{2,1,0:T(8,128)}, f32[65,32,128]{2,1,0:T(8,128)S(1)}, u32[]{:S(2)}, u32[]{:S(2)}) %collective-permute-start.4) | collective-permute-done | bytes 1064992 | tf_op jit(solution)/shard_map/ppermute | solution.py:522
  123.9 1.5 fusion.3.base_ref
  125.5 3.7 %all-to-all-done.2.got_ref = s16[128,32,128]{2,1,0:T(8,128)(2,1)S(1)} async-done(((s16[128,32,128]{2,1,0:T(8,128)(2,1)}), s16[128,32,128]{2,1,0:T(8,128)(2,1)S(1)}, u32[]{:S(2)}, u32[]{:S(2)}) %all-to-all-start.2) | async-done | bytes 1048608 | tf_op jit(solution)/shard_map/all_to_all | solution.py:519
  129.2 4.5 %collective-permute-start.5 = (s16[128,32,128]{2,1,0:T(8,128)(2,1)S(1)}, s16[128,32,128]{2,1,0:T(8,128)(2,1)S(1)}, u32[]{:S(2)}, u32[]{:S(2)}) collective-permute-start(s16[128,32,128]{2,1,0:T(8,128)(2,1)S(1)} %all-to-all-done.2.got_ref), channel_id=1, source_target_pairs={{0,1},{1,0},{2,3},{3,2},{4,5},{5,4},{6,7},{7,6},{8,9},{9,8},{10,11... | collective-permute-start | bytes 3145736 | tf_op jit(solution)/shard_map/ppermute | solution.py:522
  133.7 1.4 shard_map.116.own_ref
  135.1 0.8 collective-permute-done.5.got_ref
  136.0 2.9 %shard_map.117 = (bf16[64,32,128]{2,1,0:T(8,128)(2,1)}, bf16[128,32,128]{2,1,0:T(8,128)(2,1)}) custom-call(s32[128]{0:T(128)S(1)} %copy-done.7, s32[128]{0:T(128)S(1)} %collective-permute-done.3.asked_other_ref, f32[64,32,128]{2,1,0:T(8,128)S(1)} %shard_map.116.own_ref, s16[128,32,128]{2,1,0:T(8,128)(2,1)S(1)} %collective-permute-done.5.got_ref, ...), custom_call_target="tpu_custom_call" | custom-call | tf_op jit(solution)/shard_map/pallas_call | solution.py:293
  138.8 6.2 %all-to-all-start.5 = ((bf16[128,32,128]{2,1,0:T(8,128)(2,1)}), bf16[128,32,128]{2,1,0:T(8,128)(2,1)S(1)}, u32[]{:S(2)}, u32[]{:S(2)}) async-start(bf16[128,32,128]{2,1,0:T(8,128)(2,1)} %get-tuple-element.44), calls=%async_computation.5 | async-start | bytes 2097152 | tf_op jit(solution)/shard_map/all_to_all | solution.py:519
  145.0 12.5 %shard_map.118 = s16[128,32,128]{2,1,0:T(8,128)(2,1)} custom-call(s32[1344]{0:T(1024)} %get-tuple-element.33.list_ref, s32[1]{0:T(128)} %get-tuple-element.34.steps_ref, bf16[1280,128,128]{2,1,0:T(8,128)(2,1)} %get-tuple-element.38.tiles_ref, bf16[64,32,128]{2,1,0:T(8,128)(2,1)} %get-tuple-element.43.ex_ref), custom_call_target="tpu_custom_call" | custom-call | flops 10000000000 | bytes 40000000 | tf_op jit(solution)/shard_map/pallas_call | solution.py:226
  157.6 17.1 %all-to-all-done.5.ex_ref = bf16[128,32,128]{2,1,0:T(8,128)(2,1)S(1)} async-done(((bf16[128,32,128]{2,1,0:T(8,128)(2,1)}), bf16[128,32,128]{2,1,0:T(8,128)(2,1)S(1)}, u32[]{:S(2)}, u32[]{:S(2)}) %all-to-all-start.5) | async-done | bytes 1048608 | tf_op jit(solution)/shard_map/all_to_all | solution.py:519
  174.6 7.2 %all-to-all-start.4 = ((s16[128,32,128]{2,1,0:T(8,128)(2,1)}), s16[128,32,128]{2,1,0:T(8,128)(2,1)S(1)}, u32[]{:S(2)}, u32[]{:S(2)}) async-start(s16[128,32,128]{2,1,0:T(8,128)(2,1)} %shard_map.118), calls=%async_computation.4 | async-start | bytes 2097152 | tf_op jit(solution)/shard_map/all_to_all | solution.py:519
  181.8 16.7 %shard_map.119 = f32[65,32,128]{2,1,0:T(8,128)} custom-call(s32[1344]{0:T(1024)} %get-tuple-element.33.list_ref, s32[1]{0:T(128)} %get-tuple-element.34.steps_ref, bf16[1280,128,128]{2,1,0:T(8,128)(2,1)} %get-tuple-element.38.tiles_ref, bf16[128,32,128]{2,1,0:T(8,128)(2,1)} %copy-done.10), custom_call_target="tpu_custom_call" | custom-call | flops 10000000000 | bytes 40000000 | tf_op jit(solution)/shard_map/pallas_call | solution.py:239
  198.6 3.0 %collective-permute-start.6 = (f32[65,32,128]{2,1,0:T(8,128)}, f32[65,32,128]{2,1,0:T(8,128)S(1)}, u32[]{:S(2)}, u32[]{:S(2)}) collective-permute-start(f32[65,32,128]{2,1,0:T(8,128)} %shard_map.119), channel_id=1, source_target_pairs={{0,1},{1,0},{2,3},{3,2},{4,5},{5,4},{6,7},{7,6},{8,9},{9,8},{10,11... | collective-permute-start | bytes 3194888 | tf_op jit(solution)/shard_map/ppermute | solution.py:522
  201.6 2.5 %collective-permute-done.6 = f32[65,32,128]{2,1,0:T(8,128)S(1)} collective-permute-done((f32[65,32,128]{2,1,0:T(8,128)}, f32[65,32,128]{2,1,0:T(8,128)S(1)}, u32[]{:S(2)}, u32[]{:S(2)}) %collective-permute-start.6) | collective-permute-done | bytes 1064992 | tf_op jit(solution)/shard_map/ppermute | solution.py:522
  204.1 1.5 fusion.1.base_ref
  205.6 4.0 %all-to-all-done.4.got_ref = s16[128,32,128]{2,1,0:T(8,128)(2,1)S(1)} async-done(((s16[128,32,128]{2,1,0:T(8,128)(2,1)}), s16[128,32,128]{2,1,0:T(8,128)(2,1)S(1)}, u32[]{:S(2)}, u32[]{:S(2)}) %all-to-all-start.4) | async-done | bytes 1048608 | tf_op jit(solution)/shard_map/all_to_all | solution.py:519
  209.6 4.4 %collective-permute-start.7 = (s16[128,32,128]{2,1,0:T(8,128)(2,1)S(1)}, s16[128,32,128]{2,1,0:T(8,128)(2,1)S(1)}, u32[]{:S(2)}, u32[]{:S(2)}) collective-permute-start(s16[128,32,128]{2,1,0:T(8,128)(2,1)S(1)} %all-to-all-done.4.got_ref), channel_id=1, source_target_pairs={{0,1},{1,0},{2,3},{3,2},{4,5},{5,4},{6,7},{7,6},{8,9},{9,8},{10,11... | collective-permute-start | bytes 3145736 | tf_op jit(solution)/shard_map/ppermute | solution.py:522
  214.0 1.4 shard_map.120.own_ref
  215.5 0.8 collective-permute-done.7.got_ref
  216.3 2.5 %shard_map.121 = f32[64,32,128]{2,1,0:T(8,128)} custom-call(s32[128]{0:T(128)S(1)} %collective-permute-done.3.asked_other_ref, f32[64,32,128]{2,1,0:T(8,128)S(1)} %shard_map.120.own_ref, s16[128,32,128]{2,1,0:T(8,128)(2,1)S(1)} %collective-permute-done.7.got_ref, f32[64,32,128]{2,1,0:T(8,128)S(1)} %fusion.1.base_ref, f32[64,1,128]{2,1,0:T(1,128)S(1)} %bitcast.5), custom_call_target="tpu_custom_call" | custom-call | tf_op jit(solution)/shard_map/pallas_call | solution.py:326
  (32 shorter events, 0.1 us)
Async XLA Ops:
  0.0 48.7 %copy-start = (f32[64,32,128]{2,1,0:T(8,128)S(1)}, f32[64,32,128]{2,1,0:T(8,128)}, u32[]{:S(2)}) copy-start(f32[64,32,128]{2,1,0:T(8,128)} %emission_ref.1) | copy-start | bytes 3145732
  1.5 27.0 %all-to-all-start = ((s32[128,1,128]{2,1,0:T(1,128)}), s32[128,1,128]{2,1,0:T(1,128)S(1)}, u32[]{:S(2)}, u32[]{:S(2)}) async-start(s32[128,1,128]{2,1,0:T(1,128)} %shard_map.109), calls=%async_computation | async-start | bytes 131072 | tf_op jit(solution)/shard_map/all_to_all | solution.py:519
  17.9 0.8 copy-start.2
  18.6 0.9 copy-start.4
  19.5 0.8 copy-start.5
  20.3 18.6 %copy-start.13 = (s32[640]{0:T(1024)S(1)}, s32[640]{0:T(1024)}, u32[]{:S(2)}) copy-start(s32[640]{0:T(1024)} %param.18) | copy-start | bytes 7684
  20.3 20.2 %copy-start.14 = (s32[640]{0:T(1024)S(1)}, s32[640]{0:T(1024)}, u32[]{:S(2)}) copy-start(s32[640]{0:T(1024)} %param.19) | copy-start | bytes 7684
  20.3 20.3 %copy-start.15 = (s32[640]{0:T(1024)S(1)}, s32[640]{0:T(1024)}, u32[]{:S(2)}) copy-start(s32[640]{0:T(1024)} %param.20) | copy-start | bytes 7684
  20.3 28.4 %copy-start.3 = (f32[64,128]{1,0:T(8,128)S(1)}, f32[64,128]{1,0:T(8,128)}, u32[]{:S(2)}) copy-start(f32[64,128]{1,0:T(8,128)} %area_ref.1) | copy-start | bytes 98308
  21.6 1.4 copy-start.8
  28.5 13.9 %copy-start.1 = (s32[128,1,128]{2,1,0:T(1,128)}, s32[128,1,128]{2,1,0:T(1,128)S(1)}, u32[]{:S(2)}) copy-start(s32[128,1,128]{2,1,0:T(1,128)S(1)} %all-to-all-done) | copy-start | bytes 196612
  31.2 21.7 %all-to-all-start.1 = ((f32[128,1,640]{2,1,0:T(1,128)}), f32[128,1,640]{2,1,0:T(1,128)S(1)}, u32[]{:S(2)}, u32[]{:S(2)}) async-start(f32[128,1,640]{2,1,0:T(1,128)} %shard_map.113), calls=%async_computation.1 | async-start | bytes 655360 | tf_op jit(solution)/shard_map/all_to_all | solution.py:519
  38.8 2.7 %collective-permute-start = (s32[640]{0:T(1024)S(1)}, s32[640]{0:T(1024)S(1)}, u32[]{:S(2)}, u32[]{:S(2)}) collective-permute-start(s32[640]{0:T(1024)S(1)} %copy-done.13), channel_id=1, source_target_pairs={{0,1},{1,0},{2,3},{3,2},{4,5},{5,4},{6,7},{7,6},{8,9},{9,8},{10,11... | collective-permute-start | bytes 7688 | tf_op jit(solution)/shard_map/ppermute | solution.py:522
  40.4 1.2 collective-permute-start.1
  40.6 1.2 collective-permute-start.2
  48.2 2.9 %collective-permute-start.3 = (s32[128]{0:T(128)}, s32[128]{0:T(128)S(1)}, u32[]{:S(2)}, u32[]{:S(2)}) collective-permute-start(s32[128]{0:T(128)} %get-tuple-element.26.asked_ref), channel_id=1, source_target_pairs={{0,1},{1,0},{2,3},{3,2},{4,5},{5,4},{6,7},{7,6},{8,9},{9,8},{10,11... | collective-permute-start | bytes 1544 | tf_op jit(solution)/shard_map/ppermute | solution.py:522
  48.7 0.6 copy-start.6
  52.9 11.8 %copy-start.11 = (f32[128,1,640]{2,1,0:T(1,128)}, f32[128,1,640]{2,1,0:T(1,128)S(1)}, u32[]{:S(2)}) copy-start(f32[128,1,640]{2,1,0:T(1,128)S(1)} %all-to-all-done.1.geometry_ref) | copy-start | bytes 983044
  52.9 41.3 %all-to-all-start.3 = ((bf16[128,32,128]{2,1,0:T(8,128)(2,1)}), bf16[128,32,128]{2,1,0:T(8,128)(2,1)S(1)}, u32[]{:S(2)}, u32[]{:S(2)}) async-start(bf16[128,32,128]{2,1,0:T(8,128)(2,1)} %get-tuple-element.40), calls=%async_computation.3 | async-start | bytes 2097152 | tf_op jit(solution)/shard_map/all_to_all | solution.py:519
  94.1 7.3 %copy-start.9 = (bf16[128,32,128]{2,1,0:T(8,128)(2,1)}, bf16[128,32,128]{2,1,0:T(8,128)(2,1)S(1)}, u32[]{:S(2)}) copy-start(bf16[128,32,128]{2,1,0:T(8,128)(2,1)S(1)} %all-to-all-done.3.ex_ref) | copy-start | bytes 3145732
  94.1 35.0 %all-to-all-start.2 = ((s16[128,32,128]{2,1,0:T(8,128)(2,1)}), s16[128,32,128]{2,1,0:T(8,128)(2,1)S(1)}, u32[]{:S(2)}, u32[]{:S(2)}) async-start(s16[128,32,128]{2,1,0:T(8,128)(2,1)} %get-tuple-element.39), calls=%async_computation.2 | async-start | bytes 2097152 | tf_op jit(solution)/shard_map/all_to_all | solution.py:519
  101.5 20.0 %copy-start.12 = (s32[64,128]{1,0:T(8,128)S(1)}, s32[64,128]{1,0:T(8,128)}, u32[]{:S(2)}) copy-start(s32[64,128]{1,0:T(8,128)} %param.15) | copy-start | bytes 98308
  101.5 20.0 %copy-start.16 = (f32[8]{0:T(128)S(1)}, f32[8]{0:T(128)}, u32[]{:S(2)}) copy-start(f32[8]{0:T(128)} %param.16) | copy-start | bytes 100
  118.2 5.7 %collective-permute-start.4 = (f32[65,32,128]{2,1,0:T(8,128)}, f32[65,32,128]{2,1,0:T(8,128)S(1)}, u32[]{:S(2)}, u32[]{:S(2)}) collective-permute-start(f32[65,32,128]{2,1,0:T(8,128)} %shard_map.115), channel_id=1, source_target_pairs={{0,1},{1,0},{2,3},{3,2},{4,5},{5,4},{6,7},{7,6},{8,9},{9,8},{10,11... | collective-permute-start | bytes 3194888 | tf_op jit(solution)/shard_map/ppermute | solution.py:522
  121.6 12.1 %copy-start.7 = (s32[128]{0:T(128)S(1)}, s32[128]{0:T(128)}, u32[]{:S(2)}) copy-start(s32[128]{0:T(128)} %get-tuple-element.26.asked_ref) | copy-start | bytes 1540
  129.2 6.8 %collective-permute-start.5 = (s16[128,32,128]{2,1,0:T(8,128)(2,1)S(1)}, s16[128,32,128]{2,1,0:T(8,128)(2,1)S(1)}, u32[]{:S(2)}, u32[]{:S(2)}) collective-permute-start(s16[128,32,128]{2,1,0:T(8,128)(2,1)S(1)} %all-to-all-done.2.got_ref), channel_id=1, source_target_pairs={{0,1},{1,0},{2,3},{3,2},{4,5},{5,4},{6,7},{7,6},{8,9},{9,8},{10,11... | collective-permute-start | bytes 3145736 | tf_op jit(solution)/shard_map/ppermute | solution.py:522
  138.8 35.8 %all-to-all-start.5 = ((bf16[128,32,128]{2,1,0:T(8,128)(2,1)}), bf16[128,32,128]{2,1,0:T(8,128)(2,1)S(1)}, u32[]{:S(2)}, u32[]{:S(2)}) async-start(bf16[128,32,128]{2,1,0:T(8,128)(2,1)} %get-tuple-element.44), calls=%async_computation.5 | async-start | bytes 2097152 | tf_op jit(solution)/shard_map/all_to_all | solution.py:519
  174.6 7.2 %copy-start.10 = (bf16[128,32,128]{2,1,0:T(8,128)(2,1)}, bf16[128,32,128]{2,1,0:T(8,128)(2,1)S(1)}, u32[]{:S(2)}) copy-start(bf16[128,32,128]{2,1,0:T(8,128)(2,1)S(1)} %all-to-all-done.5.ex_ref) | copy-start | bytes 3145732
  174.6 35.0 %all-to-all-start.4 = ((s16[128,32,128]{2,1,0:T(8,128)(2,1)}), s16[128,32,128]{2,1,0:T(8,128)(2,1)S(1)}, u32[]{:S(2)}, u32[]{:S(2)}) async-start(s16[128,32,128]{2,1,0:T(8,128)(2,1)} %shard_map.118), calls=%async_computation.4 | async-start | bytes 2097152 | tf_op jit(solution)/shard_map/all_to_all | solution.py:519
  198.6 5.5 %collective-permute-start.6 = (f32[65,32,128]{2,1,0:T(8,128)}, f32[65,32,128]{2,1,0:T(8,128)S(1)}, u32[]{:S(2)}, u32[]{:S(2)}) collective-permute-start(f32[65,32,128]{2,1,0:T(8,128)} %shard_map.119), channel_id=1, source_target_pairs={{0,1},{1,0},{2,3},{3,2},{4,5},{5,4},{6,7},{7,6},{8,9},{9,8},{10,11... | collective-permute-start | bytes 3194888 | tf_op jit(solution)/shard_map/ppermute | solution.py:522
  209.6 6.7 %collective-permute-start.7 = (s16[128,32,128]{2,1,0:T(8,128)(2,1)S(1)}, s16[128,32,128]{2,1,0:T(8,128)(2,1)S(1)}, u32[]{:S(2)}, u32[]{:S(2)}) collective-permute-start(s16[128,32,128]{2,1,0:T(8,128)(2,1)S(1)} %all-to-all-done.4.got_ref), channel_id=1, source_target_pairs={{0,1},{1,0},{2,3},{3,2},{4,5},{5,4},{6,7},{7,6},{8,9},{9,8},{10,11... | collective-permute-start | bytes 3145736 | tf_op jit(solution)/shard_map/ppermute | solution.py:522

commit v6 on v5

--- a/solution.py
+++ b/solution.py
@@ -39,10 +39,7 @@
     return lax.shift_right_logical(word, jnp.int32(7)) & 255
 
 
-def list_kernel(mine_ref, other_ref, asked_ref, list_ref, steps_ref, short_ref):
-    for owner in range(asked_ref.shape[0]):
-        short_ref[owner] = asked_ref[owner, 0]
-
+def list_kernel(mine_ref, other_ref, list_ref, steps_ref):
     def take_from(words_ref):
         def take(turn, count):
             for j in range(8):
@@ -61,18 +58,17 @@
     steps_ref[0] = jnp.maximum((count + UNROLL - 1) // UNROLL, 1)
 
 
-def pair_list(mine, other, asked):
+def pair_list(mine, other):
     return pl.pallas_call(
         list_kernel,
         out_shape=(
             jax.ShapeDtypeStruct((2 * mine.shape[0] + UNROLL,), jnp.int32),
             jax.ShapeDtypeStruct((1,), jnp.int32),
-            jax.ShapeDtypeStruct((asked.shape[0],), jnp.int32),
         ),
-        in_specs=[SMEM_SPEC] * 3,
-        out_specs=(SMEM_SPEC,) * 3,
+        in_specs=[SMEM_SPEC] * 2,
+        out_specs=(SMEM_SPEC,) * 2,
         cost_estimate=pl.CostEstimate(flops=10_000_000, bytes_accessed=10_000_000, transcendentals=0),
-    )(mine, other, asked)
+    )(mine, other)
 
 
 def encode(acc, out_ref):
@@ -373,9 +369,22 @@
         copy.start()
 
 
-def place_kernel(asked_ref, geometry_ref, place_ref, placed, sems):
+def place_kernel(
+    asked_ref, geometry_ref, place_ref, short_ref, placed, sems, short, short_sem, geometry, geometry_sem
+):
+    to_rows = pltpu.make_async_copy(geometry_ref, geometry, geometry_sem)
+    to_rows.start()
+    asked = asked_ref[...]
+    row = lax.broadcasted_iota(jnp.int32, asked.shape, 0)
+    column = lax.broadcasted_iota(jnp.int32, asked.shape, 1)
+    short_ref[...] = jnp.sum(jnp.where(row == column, asked, 0), axis=0, keepdims=True)
+    to_scalars = pltpu.make_async_copy(short_ref, short, short_sem)
+    to_scalars.start()
+    to_scalars.wait()
+    to_rows.wait()
+
     def put(at, carry):
-        placed[at] = geometry_ref[pl.ds(asked_ref[at, 0], 1), :]
+        placed[at] = geometry[pl.ds(short[0, at], 1), :]
         return carry
 
     copies = part_copies(placed, place_ref, sems)
@@ -391,12 +400,19 @@
     owners = asked.shape[0]
     return pl.pallas_call(
         place_kernel,
-        in_specs=[SMEM_SPEC, VMEM_SPEC],
-        out_specs=HBM_SPEC,
-        out_shape=jax.ShapeDtypeStruct((owners, 1, geometry.shape[1]), jnp.float32),
+        in_specs=[VMEM_SPEC, HBM_SPEC],
+        out_specs=[HBM_SPEC, VMEM_SPEC],
+        out_shape=[
+            jax.ShapeDtypeStruct((owners, 1, geometry.shape[1]), jnp.float32),
+            jax.ShapeDtypeStruct((1, owners), jnp.int32),
+        ],
         scratch_shapes=[
             pltpu.VMEM((owners, 1, geometry.shape[1]), jnp.float32),
             pltpu.SemaphoreType.DMA((PARTS,)),
+            pltpu.SMEM((1, owners), jnp.int32),
+            pltpu.SemaphoreType.DMA,
+            pltpu.VMEM(geometry.shape, jnp.float32),
+            pltpu.SemaphoreType.DMA,
         ],
         compiler_params=pltpu.CompilerParams(vmem_limit_bytes=VMEM // 4),
     )(asked, geometry)
@@ -502,7 +518,7 @@
             jax.ShapeDtypeStruct((blocks, 5 * BLOCK), jnp.float32),
         ],
         scratch_shapes=[pltpu.VMEM((8 * FEATURES, BLOCK), jnp.float32)],
-        compiler_params=pltpu.CompilerParams(vmem_limit_bytes=VMEM // 4),
+        compiler_params=pltpu.CompilerParams(vmem_limit_bytes=VMEM),
         cost_estimate=pl.CostEstimate(flops=10_000_000, bytes_accessed=8_000_000, transcendentals=0),
     )(positions, patch_area, facing)
 
@@ -523,20 +539,19 @@
 
     asked_rows = exchange(ask(core, fetch_block, owners)).reshape(owners, BLOCK)
     near, own_geometry = near_factors(positions, patch_area, facing)
-    geometry = exchange(place(asked_rows, own_geometry))
+    placed, asked = place(asked_rows, own_geometry)
+    asked = asked.reshape(owners)
+    geometry = exchange(placed)
 
     def words(pair_row, pair_slot, code):
         skip = (pair_slot & 1) ^ core
         return pair_row | (skip << 6) | ((pair_slot >> 1) << 7) | jnp.left_shift(code, 15)
 
     lists = (pair_rows, pair_slots, pair_code)
-    pairs, steps, asked = pair_list(words(*lists), words(*map(swap, lists)), asked_rows)
-    asked_other = swap(asked)
+    pairs, steps = pair_list(words(*lists), words(*map(swap, lists)))
     area = patch_area[:, None, :]
     exitance, send = first(asked, area, emission)
-    send, geometry, near, pairs, steps, asked_other = lax.optimization_barrier(
-        (send, geometry, near, pairs, steps, asked_other)
-    )
+    send, geometry, near, pairs, steps = lax.optimization_barrier((send, geometry, near, pairs, steps))
 
     class_ids = jnp.arange(NCLASS, dtype=jnp.int32)
     albedo = jnp.sum(
@@ -544,6 +559,7 @@
     )[:, None, :]
 
     fetched = exchange(send)
+    asked_other, geometry = lax.optimization_barrier((swap(asked), geometry))
     tiles, back = build(
         pairs, steps, jnp.asarray(hash_pattern()), near, geometry, exitance, 2 * pair_rows.shape[0]
     )

time: 220 us -> 217 us (0.986)
  starting transfers between devices: 74.1 us -> 68.1 us
  Pallas kernels: 87.9 us -> 92.1 us
  local copies, waits for them, and re-layouts: 4.43 us -> 0.95 us
  waiting for transfers between devices: 47.7 us -> 50 us
    ppermute x8, starting transfers between devices: 17.7 us -> 13.4 us  [swap(): return lax.ppermute(array, 'grp', [(0, 1), (1, 0)])]
    unnamed x34 -> x16, local copies, waits for them, and re-layouts: 4.43 us -> 0.95 us
    pallas_call x1, Pallas kernels: 1.33 us -> 3.61 us  [near_factors(): pl.pallas_call(near_kernel, in_specs=[VMEM_SPEC] * 3, out_specs=[VMEM_SPE...]
  transfers between devices with their start and end apart: 14 -> 14, of which waited for: 12 -> 11; matrix products, arithmetic and copies ran while one was open for 2% -> 2% of each run, Pallas kernels for 36% -> 39%
where the time goes in v6:
time: 217 us
  Pallas kernels  92.1 us (42%)
  starting transfers between devices  68.1 us (31%)
  waiting for transfers between devices  50 us (23%)
  other arithmetic  5.09 us (2%)
    all_to_all x6, starting transfers between devices, exchange(): return lax.all_to_all(array, 'blk', split_axis=0, concat_axis=0, tiled=True)  54.7 us
    all_to_all x6, waiting for transfers between devices, exchange(): return lax.all_to_all(array, 'blk', split_axis=0, concat_axis=0, tiled=True)  42.6 us
    pallas_call x2, Pallas kernels, rows(): pl.pallas_call(rows_kernel, in_specs=[SMEM_SPEC] * 2 + [ANY_SPEC, VMEM_SP...  35.7 us
    pallas_call x1, Pallas kernels, build(): pl.pallas_call(build_kernel, in_specs=[SMEM_SPEC] * 2 + [VMEM_SPEC] * 4,...  21.7 us
    ppermute x8, starting transfers between devices, swap(): return lax.ppermute(array, 'grp', [(0, 1), (1, 0)])  13.4 us
    pallas_call x1, Pallas kernels, columns(): pl.pallas_call(columns_kernel, in_specs=[SMEM_SPEC] * 2 + [ANY_SPEC, VMEM...  13.1 us
    ppermute x8, waiting for transfers between devices, swap(): return lax.ppermute(array, 'grp', [(0, 1), (1, 0)])  7.39 us
    pallas_call x1, Pallas kernels, pair_list(): pl.pallas_call(list_kernel, out_shape=(jax.ShapeDtypeStruct((2 * mine.sha...  4.67 us
  transfers between devices with their start and end apart: 14, of which 11 were waited for; matrix products, arithmetic and copies ran while one was open for 2% of the time, Pallas kernels for 39%

profile of v6, /device:TPU:1, one launch (start us, length us, event | category | flops | bytes accessed | tf_op | source)
XLA Modules:
  0.0 216.5 jit_solution(12509347426206297124)
XLA Ops:
  0.0 1.5 shard_map.109
  1.5 16.3 %all-to-all-start = ((s32[128,1,128]{2,1,0:T(1,128)}), s32[128,1,128]{2,1,0:T(1,128)S(1)}, u32[]{:S(2)}, u32[]{:S(2)}) async-start(s32[128,1,128]{2,1,0:T(1,128)} %shard_map.109), calls=%async_computation | async-start | bytes 131072 | tf_op jit(solution)/shard_map/all_to_all | solution.py:535
  17.9 3.6 %shard_map.110 = (bf16[64,128,32]{2,1,0:T(8,128)(2,1)}, f32[64,640]{1,0:T(8,128)}) custom-call(f32[3,64,128]{2,1,0:T(8,128)} %positions_ref.1, f32[64,128]{1,0:T(8,128)} %area_ref.1, f32[64,128]{1,0:T(8,128)} %facing_ref.1), custom_call_target="tpu_custom_call" | custom-call | flops 10000000 | bytes 8000000 | tf_op jit(solution)/shard_map/pallas_call | solution.py:512
  21.5 7.1 %all-to-all-done = s32[128,1,128]{2,1,0:T(1,128)S(1)} async-done(((s32[128,1,128]{2,1,0:T(1,128)}), s32[128,1,128]{2,1,0:T(1,128)S(1)}, u32[]{:S(2)}, u32[]{:S(2)}) %all-to-all-start) | async-done | bytes 65568 | tf_op jit(solution)/shard_map/all_to_all | solution.py:535
  28.6 0.9 copy-done.2
  29.5 1.8 shard_map.111
  31.3 6.2 %all-to-all-start.1 = ((f32[128,1,640]{2,1,0:T(1,128)}), f32[128,1,640]{2,1,0:T(1,128)S(1)}, u32[]{:S(2)}, u32[]{:S(2)}) async-start(f32[128,1,640]{2,1,0:T(1,128)} %get-tuple-element.31), calls=%async_computation.1 | async-start | bytes 655360 | tf_op jit(solution)/shard_map/all_to_all | solution.py:535
  37.5 2.2 %collective-permute-start.3 = (s32[640]{0:T(1024)}, s32[640]{0:T(1024)S(1)}, u32[]{:S(2)}, u32[]{:S(2)}) collective-permute-start(s32[640]{0:T(1024)} %param.20), channel_id=1, source_target_pairs={{0,1},{1,0},{2,3},{3,2},{4,5},{5,4},{6,7},{7,6},{8,9},{9,8},{10,11... | collective-permute-start | bytes 7688 | tf_op jit(solution)/shard_map/ppermute | solution.py:538
  39.6 0.1 collective-permute-start.2
  39.7 0.4 collective-permute-start.1
  40.1 1.3 shift-left_or_fusion.1.mine_ref
  41.5 0.0 collective-permute-done.3
  41.5 0.0 collective-permute-done.2
  41.5 0.6 shift-left_or_fusion.other_ref
  42.1 4.7 %shard_map.113 = (s32[1344]{0:T(1024)}, s32[1]{0:T(128)}) custom-call(s32[640]{0:T(1024)} %shift-left_or_fusion.1.mine_ref, s32[640]{0:T(1024)} %shift-left_or_fusion.other_ref), custom_call_target="tpu_custom_call" | custom-call | flops 10000000 | bytes 10000000 | tf_op jit(solution)/shard_map/pallas_call | solution.py:62
  46.8 1.8 shard_map.112
  48.6 2.0 all-to-all-done.1.geometry_ref
  50.6 11.5 %all-to-all-start.3 = ((bf16[128,32,128]{2,1,0:T(8,128)(2,1)}), bf16[128,32,128]{2,1,0:T(8,128)(2,1)S(1)}, u32[]{:S(2)}, u32[]{:S(2)}) async-start(bf16[128,32,128]{2,1,0:T(8,128)(2,1)} %get-tuple-element.44), calls=%async_computation.3 | async-start | bytes 2097152 | tf_op jit(solution)/shard_map/all_to_all | solution.py:535
  62.1 0.4 collective-permute-start
  62.6 0.8 collective-permute-done.asked_other_ref
  63.4 21.7 %shard_map.114 = (bf16[1280,128,128]{2,1,0:T(8,128)(2,1)}, s16[128,32,128]{2,1,0:T(8,128)(2,1)}) custom-call(s32[1344]{0:T(1024)} %get-tuple-element.37.list_ref, s32[1]{0:T(128)} %get-tuple-element.38.steps_ref, s32[128,128]{1,0:T(8,128)} %constant.16.clone.pattern_ref, bf16[64,128,32]{2,1,0:T(8,128)(2,1)} %get-tuple-element.39.near_ref, ...), custom_call_target="tpu_custom_call" | custom-call | flops 20000000000 | bytes 60000000 | tf_op jit(solution)/shard_map/pallas_call | solution.py:198
  85.2 6.5 %all-to-all-done.3.ex_ref = bf16[128,32,128]{2,1,0:T(8,128)(2,1)S(1)} async-done(((bf16[128,32,128]{2,1,0:T(8,128)(2,1)}), bf16[128,32,128]{2,1,0:T(8,128)(2,1)S(1)}, u32[]{:S(2)}, u32[]{:S(2)}) %all-to-all-start.3) | async-done | bytes 1048608 | tf_op jit(solution)/shard_map/all_to_all | solution.py:535
  91.7 7.3 %all-to-all-start.2 = ((s16[128,32,128]{2,1,0:T(8,128)(2,1)}), s16[128,32,128]{2,1,0:T(8,128)(2,1)S(1)}, u32[]{:S(2)}, u32[]{:S(2)}) async-start(s16[128,32,128]{2,1,0:T(8,128)(2,1)} %get-tuple-element.43), calls=%async_computation.2 | async-start | bytes 2097152 | tf_op jit(solution)/shard_map/all_to_all | solution.py:535
  99.0 0.0 copy-start.6
  99.1 0.0 copy-start.7
  99.1 17.8 %shard_map.115 = f32[65,32,128]{2,1,0:T(8,128)} custom-call(s32[1344]{0:T(1024)} %get-tuple-element.37.list_ref, s32[1]{0:T(128)} %get-tuple-element.38.steps_ref, bf16[1280,128,128]{2,1,0:T(8,128)(2,1)} %get-tuple-element.42.tiles_ref, bf16[128,32,128]{2,1,0:T(8,128)(2,1)} %copy-done.3), custom_call_target="tpu_custom_call" | custom-call | flops 10000000000 | bytes 40000000 | tf_op jit(solution)/shard_map/pallas_call | solution.py:235
  116.9 0.7 collective-permute-start.4
  117.6 0.1 select_reduce_fusion
  117.7 2.4 %collective-permute-done.4 = f32[65,32,128]{2,1,0:T(8,128)S(1)} collective-permute-done((f32[65,32,128]{2,1,0:T(8,128)}, f32[65,32,128]{2,1,0:T(8,128)S(1)}, u32[]{:S(2)}, u32[]{:S(2)}) %collective-permute-start.4) | collective-permute-done | bytes 1064992 | tf_op jit(solution)/shard_map/ppermute | solution.py:538
  120.1 1.5 fusion.3.base_ref
  121.6 5.1 %all-to-all-done.2.got_ref = s16[128,32,128]{2,1,0:T(8,128)(2,1)S(1)} async-done(((s16[128,32,128]{2,1,0:T(8,128)(2,1)}), s16[128,32,128]{2,1,0:T(8,128)(2,1)S(1)}, u32[]{:S(2)}, u32[]{:S(2)}) %all-to-all-start.2) | async-done | bytes 1048608 | tf_op jit(solution)/shard_map/all_to_all | solution.py:535
  126.7 4.6 %collective-permute-start.5 = (s16[128,32,128]{2,1,0:T(8,128)(2,1)S(1)}, s16[128,32,128]{2,1,0:T(8,128)(2,1)S(1)}, u32[]{:S(2)}, u32[]{:S(2)}) collective-permute-start(s16[128,32,128]{2,1,0:T(8,128)(2,1)S(1)} %all-to-all-done.2.got_ref), channel_id=1, source_target_pairs={{0,1},{1,0},{2,3},{3,2},{4,5},{5,4},{6,7},{7,6},{8,9},{9,8},{10,11... | collective-permute-start | bytes 3145736 | tf_op jit(solution)/shard_map/ppermute | solution.py:538
  131.3 1.4 shard_map.116.own_ref
  132.7 0.8 collective-permute-done.5.got_ref
  133.6 2.9 %shard_map.117 = (bf16[64,32,128]{2,1,0:T(8,128)(2,1)}, bf16[128,32,128]{2,1,0:T(8,128)(2,1)}) custom-call(s32[128]{0:T(128)S(1)} %bitcast.13, s32[128]{0:T(128)S(1)} %collective-permute-done.asked_other_ref, f32[64,32,128]{2,1,0:T(8,128)S(1)} %shard_map.116.own_ref, s16[128,32,128]{2,1,0:T(8,128)(2,1)S(1)} %collective-permute-done.5.got_ref, ...), custom_call_target="tpu_custom_call" | custom-call | tf_op jit(solution)/shard_map/pallas_call | solution.py:289
  136.4 6.2 %all-to-all-start.5 = ((bf16[128,32,128]{2,1,0:T(8,128)(2,1)}), bf16[128,32,128]{2,1,0:T(8,128)(2,1)S(1)}, u32[]{:S(2)}, u32[]{:S(2)}) async-start(bf16[128,32,128]{2,1,0:T(8,128)(2,1)} %get-tuple-element.48), calls=%async_computation.5 | async-start | bytes 2097152 | tf_op jit(solution)/shard_map/all_to_all | solution.py:535
  142.6 13.1 %shard_map.118 = s16[128,32,128]{2,1,0:T(8,128)(2,1)} custom-call(s32[1344]{0:T(1024)} %get-tuple-element.37.list_ref, s32[1]{0:T(128)} %get-tuple-element.38.steps_ref, bf16[1280,128,128]{2,1,0:T(8,128)(2,1)} %get-tuple-element.42.tiles_ref, bf16[64,32,128]{2,1,0:T(8,128)(2,1)} %get-tuple-element.47.ex_ref), custom_call_target="tpu_custom_call" | custom-call | flops 10000000000 | bytes 40000000 | tf_op jit(solution)/shard_map/pallas_call | solution.py:222
  155.7 16.5 %all-to-all-done.5.ex_ref = bf16[128,32,128]{2,1,0:T(8,128)(2,1)S(1)} async-done(((bf16[128,32,128]{2,1,0:T(8,128)(2,1)}), bf16[128,32,128]{2,1,0:T(8,128)(2,1)S(1)}, u32[]{:S(2)}, u32[]{:S(2)}) %all-to-all-start.5) | async-done | bytes 1048608 | tf_op jit(solution)/shard_map/all_to_all | solution.py:535
  172.2 7.2 %all-to-all-start.4 = ((s16[128,32,128]{2,1,0:T(8,128)(2,1)}), s16[128,32,128]{2,1,0:T(8,128)(2,1)S(1)}, u32[]{:S(2)}, u32[]{:S(2)}) async-start(s16[128,32,128]{2,1,0:T(8,128)(2,1)} %shard_map.118), calls=%async_computation.4 | async-start | bytes 2097152 | tf_op jit(solution)/shard_map/all_to_all | solution.py:535
  179.4 17.8 %shard_map.119 = f32[65,32,128]{2,1,0:T(8,128)} custom-call(s32[1344]{0:T(1024)} %get-tuple-element.37.list_ref, s32[1]{0:T(128)} %get-tuple-element.38.steps_ref, bf16[1280,128,128]{2,1,0:T(8,128)(2,1)} %get-tuple-element.42.tiles_ref, bf16[128,32,128]{2,1,0:T(8,128)(2,1)} %copy-done.4), custom_call_target="tpu_custom_call" | custom-call | flops 10000000000 | bytes 40000000 | tf_op jit(solution)/shard_map/pallas_call | solution.py:235
  197.2 0.6 collective-permute-start.6
  197.8 2.5 %collective-permute-done.6 = f32[65,32,128]{2,1,0:T(8,128)S(1)} collective-permute-done((f32[65,32,128]{2,1,0:T(8,128)}, f32[65,32,128]{2,1,0:T(8,128)S(1)}, u32[]{:S(2)}, u32[]{:S(2)}) %collective-permute-start.6) | collective-permute-done | bytes 1064992 | tf_op jit(solution)/shard_map/ppermute | solution.py:538
  200.3 1.5 fusion.1.base_ref
  201.8 5.3 %all-to-all-done.4.got_ref = s16[128,32,128]{2,1,0:T(8,128)(2,1)S(1)} async-done(((s16[128,32,128]{2,1,0:T(8,128)(2,1)}), s16[128,32,128]{2,1,0:T(8,128)(2,1)S(1)}, u32[]{:S(2)}, u32[]{:S(2)}) %all-to-all-start.4) | async-done | bytes 1048608 | tf_op jit(solution)/shard_map/all_to_all | solution.py:535
  207.2 4.4 %collective-permute-start.7 = (s16[128,32,128]{2,1,0:T(8,128)(2,1)S(1)}, s16[128,32,128]{2,1,0:T(8,128)(2,1)S(1)}, u32[]{:S(2)}, u32[]{:S(2)}) collective-permute-start(s16[128,32,128]{2,1,0:T(8,128)(2,1)S(1)} %all-to-all-done.4.got_ref), channel_id=1, source_target_pairs={{0,1},{1,0},{2,3},{3,2},{4,5},{5,4},{6,7},{7,6},{8,9},{9,8},{10,11... | collective-permute-start | bytes 3145736 | tf_op jit(solution)/shard_map/ppermute | solution.py:538
  211.6 1.4 shard_map.120.own_ref
  213.1 0.8 collective-permute-done.7.got_ref
  213.9 2.5 %shard_map.121 = f32[64,32,128]{2,1,0:T(8,128)} custom-call(s32[128]{0:T(128)S(1)} %collective-permute-done.asked_other_ref, f32[64,32,128]{2,1,0:T(8,128)S(1)} %shard_map.120.own_ref, s16[128,32,128]{2,1,0:T(8,128)(2,1)S(1)} %collective-permute-done.7.got_ref, f32[64,32,128]{2,1,0:T(8,128)S(1)} %fusion.1.base_ref, f32[64,1,128]{2,1,0:T(1,128)S(1)} %bitcast.6), custom_call_target="tpu_custom_call" | custom-call | tf_op jit(solution)/shard_map/pallas_call | solution.py:322
  (14 shorter events, 0.0 us)
Async XLA Ops:
  0.0 46.7 %copy-start.1 = (f32[64,128]{1,0:T(8,128)S(1)}, f32[64,128]{1,0:T(8,128)}, u32[]{:S(2)}) copy-start(f32[64,128]{1,0:T(8,128)} %area_ref.1) | copy-start | bytes 98308
  0.0 46.8 %copy-start = (f32[64,32,128]{2,1,0:T(8,128)S(1)}, f32[64,32,128]{2,1,0:T(8,128)}, u32[]{:S(2)}) copy-start(f32[64,32,128]{2,1,0:T(8,128)} %emission_ref.1) | copy-start | bytes 3145732
  1.5 27.1 %all-to-all-start = ((s32[128,1,128]{2,1,0:T(1,128)}), s32[128,1,128]{2,1,0:T(1,128)S(1)}, u32[]{:S(2)}, u32[]{:S(2)}) async-start(s32[128,1,128]{2,1,0:T(1,128)} %shard_map.109), calls=%async_computation | async-start | bytes 131072 | tf_op jit(solution)/shard_map/all_to_all | solution.py:535
  28.6 0.9 copy-start.2
  31.3 19.4 %all-to-all-start.1 = ((f32[128,1,640]{2,1,0:T(1,128)}), f32[128,1,640]{2,1,0:T(1,128)S(1)}, u32[]{:S(2)}, u32[]{:S(2)}) async-start(f32[128,1,640]{2,1,0:T(1,128)} %get-tuple-element.31), calls=%async_computation.1 | async-start | bytes 655360 | tf_op jit(solution)/shard_map/all_to_all | solution.py:535
  37.5 4.0 %collective-permute-start.3 = (s32[640]{0:T(1024)}, s32[640]{0:T(1024)S(1)}, u32[]{:S(2)}, u32[]{:S(2)}) collective-permute-start(s32[640]{0:T(1024)} %param.20), channel_id=1, source_target_pairs={{0,1},{1,0},{2,3},{3,2},{4,5},{5,4},{6,7},{7,6},{8,9},{9,8},{10,11... | collective-permute-start | bytes 7688 | tf_op jit(solution)/shard_map/ppermute | solution.py:538
  39.6 1.8 collective-permute-start.2
  39.7 1.7 collective-permute-start.1
  50.6 12.8 %copy-start.5 = (f32[128,1,640]{2,1,0:T(1,128)}, f32[128,1,640]{2,1,0:T(1,128)S(1)}, u32[]{:S(2)}) copy-start(f32[128,1,640]{2,1,0:T(1,128)S(1)} %all-to-all-done.1.geometry_ref) | copy-start | bytes 983044
  50.6 41.0 %all-to-all-start.3 = ((bf16[128,32,128]{2,1,0:T(8,128)(2,1)}), bf16[128,32,128]{2,1,0:T(8,128)(2,1)S(1)}, u32[]{:S(2)}, u32[]{:S(2)}) async-start(bf16[128,32,128]{2,1,0:T(8,128)(2,1)} %get-tuple-element.44), calls=%async_computation.3 | async-start | bytes 2097152 | tf_op jit(solution)/shard_map/all_to_all | solution.py:535
  62.1 1.3 collective-permute-start
  91.7 7.4 %copy-start.3 = (bf16[128,32,128]{2,1,0:T(8,128)(2,1)}, bf16[128,32,128]{2,1,0:T(8,128)(2,1)S(1)}, u32[]{:S(2)}) copy-start(bf16[128,32,128]{2,1,0:T(8,128)(2,1)S(1)} %all-to-all-done.3.ex_ref) | copy-start | bytes 3145732
  91.7 35.0 %all-to-all-start.2 = ((s16[128,32,128]{2,1,0:T(8,128)(2,1)}), s16[128,32,128]{2,1,0:T(8,128)(2,1)S(1)}, u32[]{:S(2)}, u32[]{:S(2)}) async-start(s16[128,32,128]{2,1,0:T(8,128)(2,1)} %get-tuple-element.43), calls=%async_computation.2 | async-start | bytes 2097152 | tf_op jit(solution)/shard_map/all_to_all | solution.py:535
  99.0 18.5 %copy-start.6 = (s32[64,128]{1,0:T(8,128)S(1)}, s32[64,128]{1,0:T(8,128)}, u32[]{:S(2)}) copy-start(s32[64,128]{1,0:T(8,128)} %param.15) | copy-start | bytes 98308
  99.1 18.5 %copy-start.7 = (f32[8]{0:T(128)S(1)}, f32[8]{0:T(128)}, u32[]{:S(2)}) copy-start(f32[8]{0:T(128)} %param.16) | copy-start | bytes 100
  116.9 3.2 %collective-permute-start.4 = (f32[65,32,128]{2,1,0:T(8,128)}, f32[65,32,128]{2,1,0:T(8,128)S(1)}, u32[]{:S(2)}, u32[]{:S(2)}) collective-permute-start(f32[65,32,128]{2,1,0:T(8,128)} %shard_map.115), channel_id=1, source_target_pairs={{0,1},{1,0},{2,3},{3,2},{4,5},{5,4},{6,7},{7,6},{8,9},{9,8},{10,11... | collective-permute-start | bytes 3194888 | tf_op jit(solution)/shard_map/ppermute | solution.py:538
  126.7 6.8 %collective-permute-start.5 = (s16[128,32,128]{2,1,0:T(8,128)(2,1)S(1)}, s16[128,32,128]{2,1,0:T(8,128)(2,1)S(1)}, u32[]{:S(2)}, u32[]{:S(2)}) collective-permute-start(s16[128,32,128]{2,1,0:T(8,128)(2,1)S(1)} %all-to-all-done.2.got_ref), channel_id=1, source_target_pairs={{0,1},{1,0},{2,3},{3,2},{4,5},{5,4},{6,7},{7,6},{8,9},{9,8},{10,11... | collective-permute-start | bytes 3145736 | tf_op jit(solution)/shard_map/ppermute | solution.py:538
  136.4 35.8 %all-to-all-start.5 = ((bf16[128,32,128]{2,1,0:T(8,128)(2,1)}), bf16[128,32,128]{2,1,0:T(8,128)(2,1)S(1)}, u32[]{:S(2)}, u32[]{:S(2)}) async-start(bf16[128,32,128]{2,1,0:T(8,128)(2,1)} %get-tuple-element.48), calls=%async_computation.5 | async-start | bytes 2097152 | tf_op jit(solution)/shard_map/all_to_all | solution.py:535
  172.2 7.2 %copy-start.4 = (bf16[128,32,128]{2,1,0:T(8,128)(2,1)}, bf16[128,32,128]{2,1,0:T(8,128)(2,1)S(1)}, u32[]{:S(2)}) copy-start(bf16[128,32,128]{2,1,0:T(8,128)(2,1)S(1)} %all-to-all-done.5.ex_ref) | copy-start | bytes 3145732
  172.2 34.9 %all-to-all-start.4 = ((s16[128,32,128]{2,1,0:T(8,128)(2,1)}), s16[128,32,128]{2,1,0:T(8,128)(2,1)S(1)}, u32[]{:S(2)}, u32[]{:S(2)}) async-start(s16[128,32,128]{2,1,0:T(8,128)(2,1)} %shard_map.118), calls=%async_computation.4 | async-start | bytes 2097152 | tf_op jit(solution)/shard_map/all_to_all | solution.py:535
  197.2 3.1 %collective-permute-start.6 = (f32[65,32,128]{2,1,0:T(8,128)}, f32[65,32,128]{2,1,0:T(8,128)S(1)}, u32[]{:S(2)}, u32[]{:S(2)}) collective-permute-start(f32[65,32,128]{2,1,0:T(8,128)} %shard_map.119), channel_id=1, source_target_pairs={{0,1},{1,0},{2,3},{3,2},{4,5},{5,4},{6,7},{7,6},{8,9},{9,8},{10,11... | collective-permute-start | bytes 3194888 | tf_op jit(solution)/shard_map/ppermute | solution.py:538
  207.2 6.7 %collective-permute-start.7 = (s16[128,32,128]{2,1,0:T(8,128)(2,1)S(1)}, s16[128,32,128]{2,1,0:T(8,128)(2,1)S(1)}, u32[]{:S(2)}, u32[]{:S(2)}) collective-permute-start(s16[128,32,128]{2,1,0:T(8,128)(2,1)S(1)} %all-to-all-done.4.got_ref), channel_id=1, source_target_pairs={{0,1},{1,0},{2,3},{3,2},{4,5},{5,4},{6,7},{7,6},{8,9},{9,8},{10,11... | collective-permute-start | bytes 3145736 | tf_op jit(solution)/shard_map/ppermute | solution.py:538

commit v7 on v6

--- a/solution.py
+++ b/solution.py
@@ -369,11 +369,7 @@
         copy.start()
 
 
-def place_kernel(
-    asked_ref, geometry_ref, place_ref, short_ref, placed, sems, short, short_sem, geometry, geometry_sem
-):
-    to_rows = pltpu.make_async_copy(geometry_ref, geometry, geometry_sem)
-    to_rows.start()
+def place_kernel(asked_ref, geometry_ref, place_ref, short_ref, placed, sems, short, short_sem):
     asked = asked_ref[...]
     row = lax.broadcasted_iota(jnp.int32, asked.shape, 0)
     column = lax.broadcasted_iota(jnp.int32, asked.shape, 1)
@@ -381,10 +377,9 @@
     to_scalars = pltpu.make_async_copy(short_ref, short, short_sem)
     to_scalars.start()
     to_scalars.wait()
-    to_rows.wait()
 
     def put(at, carry):
-        placed[at] = geometry[pl.ds(short[0, at], 1), :]
+        placed[at] = geometry_ref[pl.ds(short[0, at], 1), :]
         return carry
 
     copies = part_copies(placed, place_ref, sems)
@@ -400,7 +395,7 @@
     owners = asked.shape[0]
     return pl.pallas_call(
         place_kernel,
-        in_specs=[VMEM_SPEC, HBM_SPEC],
+        in_specs=[VMEM_SPEC] * 2,
         out_specs=[HBM_SPEC, VMEM_SPEC],
         out_shape=[
             jax.ShapeDtypeStruct((owners, 1, geometry.shape[1]), jnp.float32),
@@ -410,8 +405,6 @@
             pltpu.VMEM((owners, 1, geometry.shape[1]), jnp.float32),
             pltpu.SemaphoreType.DMA((PARTS,)),
             pltpu.SMEM((1, owners), jnp.int32),
-            pltpu.SemaphoreType.DMA,
-            pltpu.VMEM(geometry.shape, jnp.float32),
             pltpu.SemaphoreType.DMA,
         ],
         compiler_params=pltpu.CompilerParams(vmem_limit_bytes=VMEM // 4),
@@ -483,7 +476,7 @@
     lax.fori_loop(0, count // 8, group, 0)
 
 
-def near_kernel(positions_ref, area_ref, facing_ref, out_ref, geometry_ref, turned):
+def near_kernel(positions_ref, area_ref, facing_ref, out_ref, geometry_ref, turned, made, sems):
     parts = [positions_ref[i] for i in range(3)] + [area_ref[...], facing_ref[...]]
     for i, part in enumerate(parts):
         geometry_ref[:, i * BLOCK : (i + 1) * BLOCK] = part
@@ -492,9 +485,14 @@
         return [positions_ref[i, at, :] for i in range(3)] + [area_ref[at, :], facing_ref[at, :]]
 
     def put(at, block):
-        out_ref[at] = block.T.astype(jnp.bfloat16)
-
-    factor_blocks(read, out_ref.shape[0], turned, True, put)
+        made[at] = block.T.astype(jnp.bfloat16)
+
+    factor_blocks(read, made.shape[0], turned, True, put)
+    copies = part_copies(made, out_ref, sems)
+    for copy in copies:
+        copy.start()
+    for copy in copies:
+        copy.wait()
 
 
 def far_factors(geometry_ref, out, turned):
@@ -512,13 +510,17 @@
     return pl.pallas_call(
         near_kernel,
         in_specs=[VMEM_SPEC] * 3,
-        out_specs=[VMEM_SPEC] * 2,
+        out_specs=[HBM_SPEC, VMEM_SPEC],
         out_shape=[
-            jax.ShapeDtypeStruct((blocks, BLOCK, FEATURES), jnp.bfloat16),
+            pltpu.HBM((blocks, BLOCK, FEATURES), jnp.bfloat16),
             jax.ShapeDtypeStruct((blocks, 5 * BLOCK), jnp.float32),
         ],
-        scratch_shapes=[pltpu.VMEM((8 * FEATURES, BLOCK), jnp.float32)],
-        compiler_params=pltpu.CompilerParams(vmem_limit_bytes=VMEM),
+        scratch_shapes=[
+            pltpu.VMEM((8 * FEATURES, BLOCK), jnp.float32),
+            pltpu.VMEM((blocks, BLOCK, FEATURES), jnp.bfloat16),
+            pltpu.SemaphoreType.DMA((PARTS,)),
+        ],
+        compiler_params=pltpu.CompilerParams(vmem_limit_bytes=VMEM // 4),
         cost_estimate=pl.CostEstimate(flops=10_000_000, bytes_accessed=8_000_000, transcendentals=0),
     )(positions, patch_area, facing)
 
@@ -559,10 +561,11 @@
     )[:, None, :]
 
     fetched = exchange(send)
-    asked_other, geometry = lax.optimization_barrier((swap(asked), geometry))
     tiles, back = build(
         pairs, steps, jnp.asarray(hash_pattern()), near, geometry, exitance, 2 * pair_rows.shape[0]
     )
+
+    asked_other, back = lax.optimization_barrier((swap(asked), back))
 
     def collect(back, fetched):
         got = exchange(back)

time: 217 us -> 217 us (level)
  Pallas kernels: 92.1 us -> 86.5 us
  starting transfers between devices: 68.1 us -> 72.5 us
    ppermute x8, starting transfers between devices: 13.4 us -> 17.7 us  [swap(): return lax.ppermute(array, 'grp', [(0, 1), (1, 0)])]
    pallas_call x2, Pallas kernels: 35.7 us -> 33.2 us  [rows(): pl.pallas_call(rows_kernel, in_specs=[SMEM_SPEC] * 2 + [ANY_SPEC, VMEM_SP...]
  transfers between devices with their start and end apart: 14 -> 14, of which waited for: 11 -> 10; matrix products, arithmetic and copies ran while one was open for 2% -> 2% of each run, Pallas kernels for 39% -> 36%
where the time goes in v7:
time: 217 us; the launch traced here: 216 us
  Pallas kernels  86.5 us (40%)
  starting transfers between devices  72.5 us (33%)
  waiting for transfers between devices  49.4 us (23%)
  other arithmetic  5.1 us (2%)
  local copies, waits for them, and re-layouts  2.43 us (1%)
    all_to_all x6, starting transfers between devices, exchange(): return lax.all_to_all(array, 'blk', split_axis=0, concat_axis=0, tiled=True)  54.8 us
    all_to_all x6, waiting for transfers between devices, exchange(): return lax.all_to_all(array, 'blk', split_axis=0, concat_axis=0, tiled=True)  42.8 us
    pallas_call x2, Pallas kernels, rows(): pl.pallas_call(rows_kernel, in_specs=[SMEM_SPEC] * 2 + [ANY_SPEC, VMEM_SP...  33.2 us
    pallas_call x1, Pallas kernels, build(): pl.pallas_call(build_kernel, in_specs=[SMEM_SPEC] * 2 + [VMEM_SPEC] * 4,...  20.4 us
    ppermute x8, starting transfers between devices, swap(): return lax.ppermute(array, 'grp', [(0, 1), (1, 0)])  17.7 us
    pallas_call x1, Pallas kernels, columns(): pl.pallas_call(columns_kernel, in_specs=[SMEM_SPEC] * 2 + [ANY_SPEC, VMEM...  12.4 us
    ppermute x8, waiting for transfers between devices, swap(): return lax.ppermute(array, 'grp', [(0, 1), (1, 0)])  6.59 us
    pallas_call x1, Pallas kernels, pair_list(): pl.pallas_call(list_kernel, out_shape=(jax.ShapeDtypeStruct((2 * mine.sha...  4.67 us
  transfers between devices with their start and end apart: 14, of which 10 were waited for; matrix products, arithmetic and copies ran while one was open for 2% of the time, Pallas kernels for 36%

profile of v7, /device:TPU:1, one launch (start us, length us, event | category | flops | bytes accessed | tf_op | source)
XLA Modules:
  0.0 216.3 jit_solution(10255304289145270301)
XLA Ops:
  0.0 1.5 shard_map.109
  1.5 16.3 %all-to-all-start = ((s32[128,1,128]{2,1,0:T(1,128)}), s32[128,1,128]{2,1,0:T(1,128)S(1)}, u32[]{:S(2)}, u32[]{:S(2)}) async-start(s32[128,1,128]{2,1,0:T(1,128)} %shard_map.109), calls=%async_computation | async-start | bytes 131072 | tf_op jit(solution)/shard_map/all_to_all | solution.py:537
  17.9 0.0 copy-start.1
  17.9 0.7 copy-done.1
  18.6 0.9 copy-done.3
  19.5 0.8 copy-done.4
  20.3 2.7 %shard_map.110 = (bf16[64,128,32]{2,1,0:T(8,128)(2,1)}, f32[64,640]{1,0:T(8,128)S(1)}) custom-call(f32[3,64,128]{2,1,0:T(8,128)S(1)} %copy-done.3, f32[64,128]{1,0:T(8,128)S(1)} %copy-done.1, f32[64,128]{1,0:T(8,128)S(1)} %copy-done.4), custom_call_target="tpu_custom_call" | custom-call | flops 10000000 | bytes 8000000 | tf_op jit(solution)/shard_map/pallas_call | solution.py:510
  23.0 5.5 %all-to-all-done = s32[128,1,128]{2,1,0:T(1,128)S(1)} async-done(((s32[128,1,128]{2,1,0:T(1,128)}), s32[128,1,128]{2,1,0:T(1,128)S(1)}, u32[]{:S(2)}, u32[]{:S(2)}) %all-to-all-start) | async-done | bytes 65568 | tf_op jit(solution)/shard_map/all_to_all | solution.py:537
  28.5 1.6 shard_map.111
  30.1 7.7 %all-to-all-start.1 = ((f32[128,1,640]{2,1,0:T(1,128)}), f32[128,1,640]{2,1,0:T(1,128)S(1)}, u32[]{:S(2)}, u32[]{:S(2)}) async-start(f32[128,1,640]{2,1,0:T(1,128)} %get-tuple-element.31), calls=%async_computation.1 | async-start | bytes 655360 | tf_op jit(solution)/shard_map/all_to_all | solution.py:537
  37.8 1.6 collective-permute-start.1
  39.4 0.1 collective-permute-start.2
  39.5 0.4 collective-permute-start.3
  39.9 1.3 shift-left_or_fusion.1.mine_ref
  41.3 0.6 shift-left_or_fusion.other_ref
  41.9 4.7 %shard_map.113 = (s32[1344]{0:T(1024)}, s32[1]{0:T(128)}) custom-call(s32[640]{0:T(1024)} %shift-left_or_fusion.1.mine_ref, s32[640]{0:T(1024)} %shift-left_or_fusion.other_ref), custom_call_target="tpu_custom_call" | custom-call | flops 10000000 | bytes 10000000 | tf_op jit(solution)/shard_map/pallas_call | solution.py:62
  46.6 1.9 shard_map.112
  48.4 3.4 %all-to-all-done.1.geometry_ref = f32[128,1,640]{2,1,0:T(1,128)S(1)} async-done(((f32[128,1,640]{2,1,0:T(1,128)}), f32[128,1,640]{2,1,0:T(1,128)S(1)}, u32[]{:S(2)}, u32[]{:S(2)}) %all-to-all-start.1) | async-done | bytes 327712 | tf_op jit(solution)/shard_map/all_to_all | solution.py:537
  51.8 10.1 %all-to-all-start.3 = ((bf16[128,32,128]{2,1,0:T(8,128)(2,1)}), bf16[128,32,128]{2,1,0:T(8,128)(2,1)S(1)}, u32[]{:S(2)}, u32[]{:S(2)}) async-start(bf16[128,32,128]{2,1,0:T(8,128)(2,1)} %get-tuple-element.44), calls=%async_computation.3 | async-start | bytes 2097152 | tf_op jit(solution)/shard_map/all_to_all | solution.py:537
  61.9 0.4 collective-permute-start
  62.4 20.4 %shard_map.114 = (bf16[1280,128,128]{2,1,0:T(8,128)(2,1)}, s16[128,32,128]{2,1,0:T(8,128)(2,1)}) custom-call(s32[1344]{0:T(1024)} %get-tuple-element.35.list_ref, s32[1]{0:T(128)} %get-tuple-element.36.steps_ref, s32[128,128]{1,0:T(8,128)} %constant.16.clone.pattern_ref, bf16[64,128,32]{2,1,0:T(8,128)(2,1)} %get-tuple-element.37.near_ref, ...), custom_call_target="tpu_custom_call" | custom-call | flops 20000000000 | bytes 60000000 | tf_op jit(solution)/shard_map/pallas_call | solution.py:198
  82.8 8.7 %all-to-all-done.3.ex_ref = bf16[128,32,128]{2,1,0:T(8,128)(2,1)S(1)} async-done(((bf16[128,32,128]{2,1,0:T(8,128)(2,1)}), bf16[128,32,128]{2,1,0:T(8,128)(2,1)S(1)}, u32[]{:S(2)}, u32[]{:S(2)}) %all-to-all-start.3) | async-done | bytes 1048608 | tf_op jit(solution)/shard_map/all_to_all | solution.py:537
  91.5 7.3 %all-to-all-start.2 = ((s16[128,32,128]{2,1,0:T(8,128)(2,1)}), s16[128,32,128]{2,1,0:T(8,128)(2,1)S(1)}, u32[]{:S(2)}, u32[]{:S(2)}) async-start(s16[128,32,128]{2,1,0:T(8,128)(2,1)} %get-tuple-element.43), calls=%async_computation.2 | async-start | bytes 2097152 | tf_op jit(solution)/shard_map/all_to_all | solution.py:537
  98.8 0.0 copy-start.8
  98.9 0.0 copy-start.9
  98.9 16.6 %shard_map.115 = f32[65,32,128]{2,1,0:T(8,128)} custom-call(s32[1344]{0:T(1024)} %get-tuple-element.35.list_ref, s32[1]{0:T(128)} %get-tuple-element.36.steps_ref, bf16[1280,128,128]{2,1,0:T(8,128)(2,1)} %get-tuple-element.42.tiles_ref, bf16[128,32,128]{2,1,0:T(8,128)(2,1)} %copy-done.5), custom_call_target="tpu_custom_call" | custom-call | flops 10000000000 | bytes 40000000 | tf_op jit(solution)/shard_map/pallas_call | solution.py:235
  115.5 3.1 %collective-permute-start.4 = (f32[65,32,128]{2,1,0:T(8,128)}, f32[65,32,128]{2,1,0:T(8,128)S(1)}, u32[]{:S(2)}, u32[]{:S(2)}) collective-permute-start(f32[65,32,128]{2,1,0:T(8,128)} %shard_map.115), channel_id=1, source_target_pairs={{0,1},{1,0},{2,3},{3,2},{4,5},{5,4},{6,7},{7,6},{8,9},{9,8},{10,11... | collective-permute-start | bytes 3194888 | tf_op jit(solution)/shard_map/ppermute | solution.py:540
  118.6 0.1 select_reduce_fusion
  118.7 2.4 %collective-permute-done.4 = f32[65,32,128]{2,1,0:T(8,128)S(1)} collective-permute-done((f32[65,32,128]{2,1,0:T(8,128)}, f32[65,32,128]{2,1,0:T(8,128)S(1)}, u32[]{:S(2)}, u32[]{:S(2)}) %collective-permute-start.4) | collective-permute-done | bytes 1064992 | tf_op jit(solution)/shard_map/ppermute | solution.py:540
  121.1 1.5 fusion.3.base_ref
  122.6 3.9 %all-to-all-done.2.got_ref = s16[128,32,128]{2,1,0:T(8,128)(2,1)S(1)} async-done(((s16[128,32,128]{2,1,0:T(8,128)(2,1)}), s16[128,32,128]{2,1,0:T(8,128)(2,1)S(1)}, u32[]{:S(2)}, u32[]{:S(2)}) %all-to-all-start.2) | async-done | bytes 1048608 | tf_op jit(solution)/shard_map/all_to_all | solution.py:537
  126.5 4.6 %collective-permute-start.5 = (s16[128,32,128]{2,1,0:T(8,128)(2,1)S(1)}, s16[128,32,128]{2,1,0:T(8,128)(2,1)S(1)}, u32[]{:S(2)}, u32[]{:S(2)}) collective-permute-start(s16[128,32,128]{2,1,0:T(8,128)(2,1)S(1)} %all-to-all-done.2.got_ref), channel_id=1, source_target_pairs={{0,1},{1,0},{2,3},{3,2},{4,5},{5,4},{6,7},{7,6},{8,9},{9,8},{10,11... | collective-permute-start | bytes 3145736 | tf_op jit(solution)/shard_map/ppermute | solution.py:540
  131.1 1.4 shard_map.116.own_ref
  132.5 0.8 collective-permute-done.5.got_ref
  133.3 2.9 %shard_map.117 = (bf16[64,32,128]{2,1,0:T(8,128)(2,1)}, bf16[128,32,128]{2,1,0:T(8,128)(2,1)}) custom-call(s32[128]{0:T(128)S(1)} %bitcast.13, s32[128]{0:T(128)S(1)} %collective-permute-done.asked_other_ref, f32[64,32,128]{2,1,0:T(8,128)S(1)} %shard_map.116.own_ref, s16[128,32,128]{2,1,0:T(8,128)(2,1)S(1)} %collective-permute-done.5.got_ref, ...), custom_call_target="tpu_custom_call" | custom-call | tf_op jit(solution)/shard_map/pallas_call | solution.py:289
  136.2 6.2 %all-to-all-start.5 = ((bf16[128,32,128]{2,1,0:T(8,128)(2,1)}), bf16[128,32,128]{2,1,0:T(8,128)(2,1)S(1)}, u32[]{:S(2)}, u32[]{:S(2)}) async-start(bf16[128,32,128]{2,1,0:T(8,128)(2,1)} %get-tuple-element.48), calls=%async_computation.5 | async-start | bytes 2097152 | tf_op jit(solution)/shard_map/all_to_all | solution.py:537
  142.4 12.4 %shard_map.118 = s16[128,32,128]{2,1,0:T(8,128)(2,1)} custom-call(s32[1344]{0:T(1024)} %get-tuple-element.35.list_ref, s32[1]{0:T(128)} %get-tuple-element.36.steps_ref, bf16[1280,128,128]{2,1,0:T(8,128)(2,1)} %get-tuple-element.42.tiles_ref, bf16[64,32,128]{2,1,0:T(8,128)(2,1)} %get-tuple-element.47.ex_ref), custom_call_target="tpu_custom_call" | custom-call | flops 10000000000 | bytes 40000000 | tf_op jit(solution)/shard_map/pallas_call | solution.py:222
  154.8 17.2 %all-to-all-done.5.ex_ref = bf16[128,32,128]{2,1,0:T(8,128)(2,1)S(1)} async-done(((bf16[128,32,128]{2,1,0:T(8,128)(2,1)}), bf16[128,32,128]{2,1,0:T(8,128)(2,1)S(1)}, u32[]{:S(2)}, u32[]{:S(2)}) %all-to-all-start.5) | async-done | bytes 1048608 | tf_op jit(solution)/shard_map/all_to_all | solution.py:537
  172.0 7.2 %all-to-all-start.4 = ((s16[128,32,128]{2,1,0:T(8,128)(2,1)}), s16[128,32,128]{2,1,0:T(8,128)(2,1)S(1)}, u32[]{:S(2)}, u32[]{:S(2)}) async-start(s16[128,32,128]{2,1,0:T(8,128)(2,1)} %shard_map.118), calls=%async_computation.4 | async-start | bytes 2097152 | tf_op jit(solution)/shard_map/all_to_all | solution.py:537
  179.2 16.6 %shard_map.119 = f32[65,32,128]{2,1,0:T(8,128)} custom-call(s32[1344]{0:T(1024)} %get-tuple-element.35.list_ref, s32[1]{0:T(128)} %get-tuple-element.36.steps_ref, bf16[1280,128,128]{2,1,0:T(8,128)(2,1)} %get-tuple-element.42.tiles_ref, bf16[128,32,128]{2,1,0:T(8,128)(2,1)} %copy-done.6), custom_call_target="tpu_custom_call" | custom-call | flops 10000000000 | bytes 40000000 | tf_op jit(solution)/shard_map/pallas_call | solution.py:235
  195.8 3.0 %collective-permute-start.6 = (f32[65,32,128]{2,1,0:T(8,128)}, f32[65,32,128]{2,1,0:T(8,128)S(1)}, u32[]{:S(2)}, u32[]{:S(2)}) collective-permute-start(f32[65,32,128]{2,1,0:T(8,128)} %shard_map.119), channel_id=1, source_target_pairs={{0,1},{1,0},{2,3},{3,2},{4,5},{5,4},{6,7},{7,6},{8,9},{9,8},{10,11... | collective-permute-start | bytes 3194888 | tf_op jit(solution)/shard_map/ppermute | solution.py:540
  198.8 2.5 %collective-permute-done.6 = f32[65,32,128]{2,1,0:T(8,128)S(1)} collective-permute-done((f32[65,32,128]{2,1,0:T(8,128)}, f32[65,32,128]{2,1,0:T(8,128)S(1)}, u32[]{:S(2)}, u32[]{:S(2)}) %collective-permute-start.6) | collective-permute-done | bytes 1064992 | tf_op jit(solution)/shard_map/ppermute | solution.py:540
  201.3 1.5 fusion.1.base_ref
  202.8 4.1 %all-to-all-done.4.got_ref = s16[128,32,128]{2,1,0:T(8,128)(2,1)S(1)} async-done(((s16[128,32,128]{2,1,0:T(8,128)(2,1)}), s16[128,32,128]{2,1,0:T(8,128)(2,1)S(1)}, u32[]{:S(2)}, u32[]{:S(2)}) %all-to-all-start.4) | async-done | bytes 1048608 | tf_op jit(solution)/shard_map/all_to_all | solution.py:537
  207.0 4.4 %collective-permute-start.7 = (s16[128,32,128]{2,1,0:T(8,128)(2,1)S(1)}, s16[128,32,128]{2,1,0:T(8,128)(2,1)S(1)}, u32[]{:S(2)}, u32[]{:S(2)}) collective-permute-start(s16[128,32,128]{2,1,0:T(8,128)(2,1)S(1)} %all-to-all-done.4.got_ref), channel_id=1, source_target_pairs={{0,1},{1,0},{2,3},{3,2},{4,5},{5,4},{6,7},{7,6},{8,9},{9,8},{10,11... | collective-permute-start | bytes 3145736 | tf_op jit(solution)/shard_map/ppermute | solution.py:540
  211.4 1.4 shard_map.120.own_ref
  212.8 0.8 collective-permute-done.7.got_ref
  213.7 2.5 %shard_map.121 = f32[64,32,128]{2,1,0:T(8,128)} custom-call(s32[128]{0:T(128)S(1)} %collective-permute-done.asked_other_ref, f32[64,32,128]{2,1,0:T(8,128)S(1)} %shard_map.120.own_ref, s16[128,32,128]{2,1,0:T(8,128)(2,1)S(1)} %collective-permute-done.7.got_ref, f32[64,32,128]{2,1,0:T(8,128)S(1)} %fusion.1.base_ref, f32[64,1,128]{2,1,0:T(1,128)S(1)} %bitcast.6), custom_call_target="tpu_custom_call" | custom-call | tf_op jit(solution)/shard_map/pallas_call | solution.py:322
  (18 shorter events, 0.0 us)
Async XLA Ops:
  0.0 46.5 %copy-start = (f32[64,32,128]{2,1,0:T(8,128)S(1)}, f32[64,32,128]{2,1,0:T(8,128)}, u32[]{:S(2)}) copy-start(f32[64,32,128]{2,1,0:T(8,128)} %emission_ref.1) | copy-start | bytes 3145732
  1.5 27.0 %all-to-all-start = ((s32[128,1,128]{2,1,0:T(1,128)}), s32[128,1,128]{2,1,0:T(1,128)S(1)}, u32[]{:S(2)}, u32[]{:S(2)}) async-start(s32[128,1,128]{2,1,0:T(1,128)} %shard_map.109), calls=%async_computation | async-start | bytes 131072 | tf_op jit(solution)/shard_map/all_to_all | solution.py:537
  17.9 0.8 copy-start.1
  18.6 0.9 copy-start.3
  19.5 0.8 copy-start.4
  20.3 26.3 %copy-start.2 = (f32[64,128]{1,0:T(8,128)S(1)}, f32[64,128]{1,0:T(8,128)}, u32[]{:S(2)}) copy-start(f32[64,128]{1,0:T(8,128)} %area_ref.1) | copy-start | bytes 98308
  30.1 21.7 %all-to-all-start.1 = ((f32[128,1,640]{2,1,0:T(1,128)}), f32[128,1,640]{2,1,0:T(1,128)S(1)}, u32[]{:S(2)}, u32[]{:S(2)}) async-start(f32[128,1,640]{2,1,0:T(1,128)} %get-tuple-element.31), calls=%async_computation.1 | async-start | bytes 655360 | tf_op jit(solution)/shard_map/all_to_all | solution.py:537
  37.8 3.4 %collective-permute-start.1 = (s32[640]{0:T(1024)}, s32[640]{0:T(1024)S(1)}, u32[]{:S(2)}, u32[]{:S(2)}) collective-permute-start(s32[640]{0:T(1024)} %param.18), channel_id=1, source_target_pairs={{0,1},{1,0},{2,3},{3,2},{4,5},{5,4},{6,7},{7,6},{8,9},{9,8},{10,11... | collective-permute-start | bytes 7688 | tf_op jit(solution)/shard_map/ppermute | solution.py:540
  39.4 1.8 collective-permute-start.2
  39.5 1.7 collective-permute-start.3
  51.8 10.5 %copy-start.7 = (f32[128,1,640]{2,1,0:T(1,128)}, f32[128,1,640]{2,1,0:T(1,128)S(1)}, u32[]{:S(2)}) copy-start(f32[128,1,640]{2,1,0:T(1,128)S(1)} %all-to-all-done.1.geometry_ref) | copy-start | bytes 983044
  51.8 39.6 %all-to-all-start.3 = ((bf16[128,32,128]{2,1,0:T(8,128)(2,1)}), bf16[128,32,128]{2,1,0:T(8,128)(2,1)S(1)}, u32[]{:S(2)}, u32[]{:S(2)}) async-start(bf16[128,32,128]{2,1,0:T(8,128)(2,1)} %get-tuple-element.44), calls=%async_computation.3 | async-start | bytes 2097152 | tf_op jit(solution)/shard_map/all_to_all | solution.py:537
  61.9 20.8 %collective-permute-start = (s32[128]{0:T(128)S(1)}, s32[128]{0:T(128)S(1)}, u32[]{:S(2)}, u32[]{:S(2)}) collective-permute-start(s32[128]{0:T(128)S(1)} %bitcast.11), channel_id=1, source_target_pairs={{0,1},{1,0},{2,3},{3,2},{4,5},{5,4},{6,7},{7,6},{8,9},{9,8},{10,11... | collective-permute-start | bytes 1544 | tf_op jit(solution)/shard_map/ppermute | solution.py:540
  91.5 7.4 %copy-start.5 = (bf16[128,32,128]{2,1,0:T(8,128)(2,1)}, bf16[128,32,128]{2,1,0:T(8,128)(2,1)S(1)}, u32[]{:S(2)}) copy-start(bf16[128,32,128]{2,1,0:T(8,128)(2,1)S(1)} %all-to-all-done.3.ex_ref) | copy-start | bytes 3145732
  91.5 35.0 %all-to-all-start.2 = ((s16[128,32,128]{2,1,0:T(8,128)(2,1)}), s16[128,32,128]{2,1,0:T(8,128)(2,1)S(1)}, u32[]{:S(2)}, u32[]{:S(2)}) async-start(s16[128,32,128]{2,1,0:T(8,128)(2,1)} %get-tuple-element.43), calls=%async_computation.2 | async-start | bytes 2097152 | tf_op jit(solution)/shard_map/all_to_all | solution.py:537
  98.8 19.7 %copy-start.8 = (s32[64,128]{1,0:T(8,128)S(1)}, s32[64,128]{1,0:T(8,128)}, u32[]{:S(2)}) copy-start(s32[64,128]{1,0:T(8,128)} %param.15) | copy-start | bytes 98308
  98.9 19.7 %copy-start.9 = (f32[8]{0:T(128)S(1)}, f32[8]{0:T(128)}, u32[]{:S(2)}) copy-start(f32[8]{0:T(128)} %param.16) | copy-start | bytes 100
  115.5 5.6 %collective-permute-start.4 = (f32[65,32,128]{2,1,0:T(8,128)}, f32[65,32,128]{2,1,0:T(8,128)S(1)}, u32[]{:S(2)}, u32[]{:S(2)}) collective-permute-start(f32[65,32,128]{2,1,0:T(8,128)} %shard_map.115), channel_id=1, source_target_pairs={{0,1},{1,0},{2,3},{3,2},{4,5},{5,4},{6,7},{7,6},{8,9},{9,8},{10,11... | collective-permute-start | bytes 3194888 | tf_op jit(solution)/shard_map/ppermute | solution.py:540
  126.5 6.8 %collective-permute-start.5 = (s16[128,32,128]{2,1,0:T(8,128)(2,1)S(1)}, s16[128,32,128]{2,1,0:T(8,128)(2,1)S(1)}, u32[]{:S(2)}, u32[]{:S(2)}) collective-permute-start(s16[128,32,128]{2,1,0:T(8,128)(2,1)S(1)} %all-to-all-done.2.got_ref), channel_id=1, source_target_pairs={{0,1},{1,0},{2,3},{3,2},{4,5},{5,4},{6,7},{7,6},{8,9},{9,8},{10,11... | collective-permute-start | bytes 3145736 | tf_op jit(solution)/shard_map/ppermute | solution.py:540
  136.2 35.8 %all-to-all-start.5 = ((bf16[128,32,128]{2,1,0:T(8,128)(2,1)}), bf16[128,32,128]{2,1,0:T(8,128)(2,1)S(1)}, u32[]{:S(2)}, u32[]{:S(2)}) async-start(bf16[128,32,128]{2,1,0:T(8,128)(2,1)} %get-tuple-element.48), calls=%async_computation.5 | async-start | bytes 2097152 | tf_op jit(solution)/shard_map/all_to_all | solution.py:537
  172.0 7.2 %copy-start.6 = (bf16[128,32,128]{2,1,0:T(8,128)(2,1)}, bf16[128,32,128]{2,1,0:T(8,128)(2,1)S(1)}, u32[]{:S(2)}) copy-start(bf16[128,32,128]{2,1,0:T(8,128)(2,1)S(1)} %all-to-all-done.5.ex_ref) | copy-start | bytes 3145732
  172.0 35.0 %all-to-all-start.4 = ((s16[128,32,128]{2,1,0:T(8,128)(2,1)}), s16[128,32,128]{2,1,0:T(8,128)(2,1)S(1)}, u32[]{:S(2)}, u32[]{:S(2)}) async-start(s16[128,32,128]{2,1,0:T(8,128)(2,1)} %shard_map.118), calls=%async_computation.4 | async-start | bytes 2097152 | tf_op jit(solution)/shard_map/all_to_all | solution.py:537
  195.8 5.5 %collective-permute-start.6 = (f32[65,32,128]{2,1,0:T(8,128)}, f32[65,32,128]{2,1,0:T(8,128)S(1)}, u32[]{:S(2)}, u32[]{:S(2)}) collective-permute-start(f32[65,32,128]{2,1,0:T(8,128)} %shard_map.119), channel_id=1, source_target_pairs={{0,1},{1,0},{2,3},{3,2},{4,5},{5,4},{6,7},{7,6},{8,9},{9,8},{10,11... | collective-permute-start | bytes 3194888 | tf_op jit(solution)/shard_map/ppermute | solution.py:540
  207.0 6.7 %collective-permute-start.7 = (s16[128,32,128]{2,1,0:T(8,128)(2,1)S(1)}, s16[128,32,128]{2,1,0:T(8,128)(2,1)S(1)}, u32[]{:S(2)}, u32[]{:S(2)}) collective-permute-start(s16[128,32,128]{2,1,0:T(8,128)(2,1)S(1)} %all-to-all-done.4.got_ref), channel_id=1, source_target_pairs={{0,1},{1,0},{2,3},{3,2},{4,5},{5,4},{6,7},{7,6},{8,9},{9,8},{10,11... | collective-permute-start | bytes 3145736 | tf_op jit(solution)/shard_map/ppermute | solution.py:540

commit v8 on v7

--- a/solution.py
+++ b/solution.py
@@ -142,12 +142,14 @@
     lax.fori_loop(jnp.maximum(steps - DEPTH, 0), steps, drain, 0)
 
 
-def stream(steps, tiles_ref, held, sems, use):
+def stream(steps, tiles_ref, held, sems, prepare, use):
     def fetch(step, carry):
         tile_copy(tiles_ref, held, sems, step, False).start()
         return carry
 
-    lax.fori_loop(0, jnp.minimum(steps, DEPTH - 1), fetch, 0)
+    fetch(0, 0)
+    prepare()
+    lax.fori_loop(1, jnp.minimum(steps, DEPTH - 1), fetch, 0)
 
     def turn(step, carry):
         @pl.when(step + DEPTH - 1 < steps)
@@ -162,7 +164,8 @@
 
 
 def columns_kernel(list_ref, steps_ref, tiles_ref, ex_ref, out_ref, acc, held, sems):
-    acc[...] = jnp.zeros_like(acc)
+    def prepare():
+        acc[...] = jnp.zeros_like(acc)
 
     def use(step, buffer):
         for j in range(UNROLL):
@@ -170,23 +173,26 @@
             row, slot = row_of(word) & 63, slot_of(word)
             acc[slot] += jnp.dot(ex_ref[row], held[buffer, j], preferred_element_type=jnp.float32)
 
-    stream(steps_ref[0], tiles_ref, held, sems, use)
+    stream(steps_ref[0], tiles_ref, held, sems, prepare, use)
     encode(acc, out_ref)
 
 
-def rows_kernel(list_ref, steps_ref, tiles_ref, ex_ref, out_ref, held, sems):
-    out_ref[...] = jnp.zeros_like(out_ref)
+def rows_kernel(list_ref, steps_ref, tiles_ref, fetched_ref, out_ref, held, sems, ex, ex_sem):
+    def prepare():
+        copy = pltpu.make_async_copy(fetched_ref, ex, ex_sem)
+        copy.start()
+        out_ref[...] = jnp.zeros_like(out_ref)
+        copy.wait()
 
     def use(step, buffer):
         for j in range(UNROLL):
             word = list_ref[step * UNROLL + j]
             row, slot = row_of(word), slot_of(word) & 127
             out_ref[row] += lax.dot_general(
-                ex_ref[slot], held[buffer, j], (((1,), (1,)), ((), ())),
-                preferred_element_type=jnp.float32,
+                ex[slot], held[buffer, j], (((1,), (1,)), ((), ())), preferred_element_type=jnp.float32
             )
 
-    stream(steps_ref[0], tiles_ref, held, sems, use)
+    stream(steps_ref[0], tiles_ref, held, sems, prepare, use)
 
 
 HELD = pltpu.VMEM((DEPTH, UNROLL, BLOCK, BLOCK), jnp.bfloat16)
@@ -234,10 +240,10 @@
     hours = fetched.shape[1]
     return pl.pallas_call(
         rows_kernel,
-        in_specs=[SMEM_SPEC] * 2 + [ANY_SPEC, VMEM_SPEC],
+        in_specs=[SMEM_SPEC] * 2 + [ANY_SPEC, ANY_SPEC],
         out_specs=VMEM_SPEC,
         out_shape=jax.ShapeDtypeStruct((row_blocks + 1, hours, BLOCK), jnp.float32),
-        scratch_shapes=[HELD, SEMS],
+        scratch_shapes=[HELD, SEMS, pltpu.VMEM(fetched.shape, jnp.bfloat16), pltpu.SemaphoreType.DMA],
         compiler_params=pltpu.CompilerParams(vmem_limit_bytes=VMEM),
         cost_estimate=pl.CostEstimate(flops=10_000_000_000, bytes_accessed=40_000_000, transcendentals=0),
     )(pairs, steps, tiles, fetched)

time: 217 us -> 217 us (level)
  starting transfers between devices: 72.5 us -> 67.6 us
  Pallas kernels: 86.5 us -> 91.1 us
    ppermute x8, starting transfers between devices: 17.7 us -> 12.7 us  [swap(): return lax.ppermute(array, 'grp', [(0, 1), (1, 0)])]
    pallas_call x2, Pallas kernels: 33.2 us -> 35.8 us  [rows(): pl.pallas_call(rows_kernel, in_specs=[SMEM_SPEC] * 2 + [ANY_SPEC, ANY_SPE...]
  transfers between devices with their start and end apart: 14 -> 14, of which waited for: 10 -> 10; matrix products, arithmetic and copies ran while one was open for 2% -> 2% of each run, Pallas kernels for 36% -> 38%
where the time goes in v8:
time: 217 us; the launch traced here: 216 us
  Pallas kernels  91.1 us (42%)
  starting transfers between devices  67.6 us (31%)
  waiting for transfers between devices  49.8 us (23%)
  other arithmetic  5.1 us (2%)
  local copies, waits for them, and re-layouts  2.43 us (1%)
    all_to_all x6, starting transfers between devices, exchange(): return lax.all_to_all(array, 'blk', split_axis=0, concat_axis=0, tiled=True)  54.8 us
    all_to_all x6, waiting for transfers between devices, exchange(): return lax.all_to_all(array, 'blk', split_axis=0, concat_axis=0, tiled=True)  43.2 us
    pallas_call x2, Pallas kernels, rows(): pl.pallas_call(rows_kernel, in_specs=[SMEM_SPEC] * 2 + [ANY_SPEC, ANY_SPE...  35.8 us
    pallas_call x1, Pallas kernels, build(): pl.pallas_call(build_kernel, in_specs=[SMEM_SPEC] * 2 + [VMEM_SPEC] * 4,...  21.7 us
    pallas_call x1, Pallas kernels, columns(): pl.pallas_call(columns_kernel, in_specs=[SMEM_SPEC] * 2 + [ANY_SPEC, VMEM...  12.9 us
    ppermute x8, starting transfers between devices, swap(): return lax.ppermute(array, 'grp', [(0, 1), (1, 0)])  12.7 us
    ppermute x8, waiting for transfers between devices, swap(): return lax.ppermute(array, 'grp', [(0, 1), (1, 0)])  6.58 us
    pallas_call x1, Pallas kernels, pair_list(): pl.pallas_call(list_kernel, out_shape=(jax.ShapeDtypeStruct((2 * mine.sha...  4.67 us
  transfers between devices with their start and end apart: 14, of which 10 were waited for; matrix products, arithmetic and copies ran while one was open for 2% of the time, Pallas kernels for 38%

profile of v8, /device:TPU:1, one launch (start us, length us, event | category | flops | bytes accessed | tf_op | source)
XLA Modules:
  0.0 216.3 jit_solution(11400602213669583906)
XLA Ops:
  0.0 1.5 shard_map.109
  1.5 16.3 %all-to-all-start = ((s32[128,1,128]{2,1,0:T(1,128)}), s32[128,1,128]{2,1,0:T(1,128)S(1)}, u32[]{:S(2)}, u32[]{:S(2)}) async-start(s32[128,1,128]{2,1,0:T(1,128)} %shard_map.109), calls=%async_computation | async-start | bytes 131072 | tf_op jit(solution)/shard_map/all_to_all | solution.py:543
  17.9 0.0 copy-start.1
  17.9 0.7 copy-done.1
  18.6 0.9 copy-done.3
  19.5 0.8 copy-done.4
  20.3 2.7 %shard_map.110 = (bf16[64,128,32]{2,1,0:T(8,128)(2,1)}, f32[64,640]{1,0:T(8,128)S(1)}) custom-call(f32[3,64,128]{2,1,0:T(8,128)S(1)} %copy-done.3, f32[64,128]{1,0:T(8,128)S(1)} %copy-done.1, f32[64,128]{1,0:T(8,128)S(1)} %copy-done.4), custom_call_target="tpu_custom_call" | custom-call | flops 10000000 | bytes 8000000 | tf_op jit(solution)/shard_map/pallas_call | solution.py:516
  23.0 5.5 %all-to-all-done = s32[128,1,128]{2,1,0:T(1,128)S(1)} async-done(((s32[128,1,128]{2,1,0:T(1,128)}), s32[128,1,128]{2,1,0:T(1,128)S(1)}, u32[]{:S(2)}, u32[]{:S(2)}) %all-to-all-start) | async-done | bytes 65568 | tf_op jit(solution)/shard_map/all_to_all | solution.py:543
  28.5 1.6 shard_map.111
  30.1 7.7 %all-to-all-start.1 = ((f32[128,1,640]{2,1,0:T(1,128)}), f32[128,1,640]{2,1,0:T(1,128)S(1)}, u32[]{:S(2)}, u32[]{:S(2)}) async-start(f32[128,1,640]{2,1,0:T(1,128)} %get-tuple-element.31), calls=%async_computation.1 | async-start | bytes 655360 | tf_op jit(solution)/shard_map/all_to_all | solution.py:543
  37.8 1.6 collective-permute-start.1
  39.4 0.1 collective-permute-start.2
  39.5 0.4 collective-permute-start.3
  39.9 1.3 shift-left_or_fusion.1.mine_ref
  41.3 0.6 shift-left_or_fusion.other_ref
  41.9 4.7 %shard_map.113 = (s32[1344]{0:T(1024)}, s32[1]{0:T(128)}) custom-call(s32[640]{0:T(1024)} %shift-left_or_fusion.1.mine_ref, s32[640]{0:T(1024)} %shift-left_or_fusion.other_ref), custom_call_target="tpu_custom_call" | custom-call | flops 10000000 | bytes 10000000 | tf_op jit(solution)/shard_map/pallas_call | solution.py:62
  46.6 1.9 shard_map.112
  48.4 3.4 %all-to-all-done.1.geometry_ref = f32[128,1,640]{2,1,0:T(1,128)S(1)} async-done(((f32[128,1,640]{2,1,0:T(1,128)}), f32[128,1,640]{2,1,0:T(1,128)S(1)}, u32[]{:S(2)}, u32[]{:S(2)}) %all-to-all-start.1) | async-done | bytes 327712 | tf_op jit(solution)/shard_map/all_to_all | solution.py:543
  51.8 10.1 %all-to-all-start.3 = ((bf16[128,32,128]{2,1,0:T(8,128)(2,1)}), bf16[128,32,128]{2,1,0:T(8,128)(2,1)S(1)}, u32[]{:S(2)}, u32[]{:S(2)}) async-start(bf16[128,32,128]{2,1,0:T(8,128)(2,1)} %get-tuple-element.44), calls=%async_computation.3 | async-start | bytes 2097152 | tf_op jit(solution)/shard_map/all_to_all | solution.py:543
  61.9 0.4 collective-permute-start
  62.4 21.7 %shard_map.114 = (bf16[1280,128,128]{2,1,0:T(8,128)(2,1)}, s16[128,32,128]{2,1,0:T(8,128)(2,1)}) custom-call(s32[1344]{0:T(1024)} %get-tuple-element.35.list_ref, s32[1]{0:T(128)} %get-tuple-element.36.steps_ref, s32[128,128]{1,0:T(8,128)} %constant.16.clone.pattern_ref, bf16[64,128,32]{2,1,0:T(8,128)(2,1)} %get-tuple-element.37.near_ref, ...), custom_call_target="tpu_custom_call" | custom-call | flops 20000000000 | bytes 60000000 | tf_op jit(solution)/shard_map/pallas_call | solution.py:204
  84.1 7.3 %all-to-all-done.3.fetched_ref = bf16[128,32,128]{2,1,0:T(8,128)(2,1)S(1)} async-done(((bf16[128,32,128]{2,1,0:T(8,128)(2,1)}), bf16[128,32,128]{2,1,0:T(8,128)(2,1)S(1)}, u32[]{:S(2)}, u32[]{:S(2)}) %all-to-all-start.3) | async-done | bytes 1048608 | tf_op jit(solution)/shard_map/all_to_all | solution.py:543
  91.5 7.3 %all-to-all-start.2 = ((s16[128,32,128]{2,1,0:T(8,128)(2,1)}), s16[128,32,128]{2,1,0:T(8,128)(2,1)S(1)}, u32[]{:S(2)}, u32[]{:S(2)}) async-start(s16[128,32,128]{2,1,0:T(8,128)(2,1)} %get-tuple-element.43), calls=%async_computation.2 | async-start | bytes 2097152 | tf_op jit(solution)/shard_map/all_to_all | solution.py:543
  98.8 0.0 copy-start.8
  98.9 0.0 copy-start.9
  98.9 17.9 %shard_map.115 = f32[65,32,128]{2,1,0:T(8,128)} custom-call(s32[1344]{0:T(1024)} %get-tuple-element.35.list_ref, s32[1]{0:T(128)} %get-tuple-element.36.steps_ref, bf16[1280,128,128]{2,1,0:T(8,128)(2,1)} %get-tuple-element.42.tiles_ref, bf16[128,32,128]{2,1,0:T(8,128)(2,1)} %copy-done.5), custom_call_target="tpu_custom_call" | custom-call | flops 10000000000 | bytes 40000000 | tf_op jit(solution)/shard_map/pallas_call | solution.py:241
  116.8 0.6 collective-permute-start.4
  117.4 0.1 select_reduce_fusion
  117.6 2.4 %collective-permute-done.4 = f32[65,32,128]{2,1,0:T(8,128)S(1)} collective-permute-done((f32[65,32,128]{2,1,0:T(8,128)}, f32[65,32,128]{2,1,0:T(8,128)S(1)}, u32[]{:S(2)}, u32[]{:S(2)}) %collective-permute-start.4) | collective-permute-done | bytes 1064992 | tf_op jit(solution)/shard_map/ppermute | solution.py:546
  120.0 1.5 fusion.3.base_ref
  121.5 5.0 %all-to-all-done.2.got_ref = s16[128,32,128]{2,1,0:T(8,128)(2,1)S(1)} async-done(((s16[128,32,128]{2,1,0:T(8,128)(2,1)}), s16[128,32,128]{2,1,0:T(8,128)(2,1)S(1)}, u32[]{:S(2)}, u32[]{:S(2)}) %all-to-all-start.2) | async-done | bytes 1048608 | tf_op jit(solution)/shard_map/all_to_all | solution.py:543
  126.5 4.6 %collective-permute-start.5 = (s16[128,32,128]{2,1,0:T(8,128)(2,1)S(1)}, s16[128,32,128]{2,1,0:T(8,128)(2,1)S(1)}, u32[]{:S(2)}, u32[]{:S(2)}) collective-permute-start(s16[128,32,128]{2,1,0:T(8,128)(2,1)S(1)} %all-to-all-done.2.got_ref), channel_id=1, source_target_pairs={{0,1},{1,0},{2,3},{3,2},{4,5},{5,4},{6,7},{7,6},{8,9},{9,8},{10,11... | collective-permute-start | bytes 3145736 | tf_op jit(solution)/shard_map/ppermute | solution.py:546
  131.1 1.4 shard_map.116.own_ref
  132.5 0.8 collective-permute-done.5.got_ref
  133.3 2.9 %shard_map.117 = (bf16[64,32,128]{2,1,0:T(8,128)(2,1)}, bf16[128,32,128]{2,1,0:T(8,128)(2,1)}) custom-call(s32[128]{0:T(128)S(1)} %bitcast.13, s32[128]{0:T(128)S(1)} %collective-permute-done.asked_other_ref, f32[64,32,128]{2,1,0:T(8,128)S(1)} %shard_map.116.own_ref, s16[128,32,128]{2,1,0:T(8,128)(2,1)S(1)} %collective-permute-done.5.got_ref, ...), custom_call_target="tpu_custom_call" | custom-call | tf_op jit(solution)/shard_map/pallas_call | solution.py:295
  136.2 6.2 %all-to-all-start.5 = ((bf16[128,32,128]{2,1,0:T(8,128)(2,1)}), bf16[128,32,128]{2,1,0:T(8,128)(2,1)S(1)}, u32[]{:S(2)}, u32[]{:S(2)}) async-start(bf16[128,32,128]{2,1,0:T(8,128)(2,1)} %get-tuple-element.48), calls=%async_computation.5 | async-start | bytes 2097152 | tf_op jit(solution)/shard_map/all_to_all | solution.py:543
  142.4 12.9 %shard_map.118 = s16[128,32,128]{2,1,0:T(8,128)(2,1)} custom-call(s32[1344]{0:T(1024)} %get-tuple-element.35.list_ref, s32[1]{0:T(128)} %get-tuple-element.36.steps_ref, bf16[1280,128,128]{2,1,0:T(8,128)(2,1)} %get-tuple-element.42.tiles_ref, bf16[64,32,128]{2,1,0:T(8,128)(2,1)} %get-tuple-element.47.ex_ref), custom_call_target="tpu_custom_call" | custom-call | flops 10000000000 | bytes 40000000 | tf_op jit(solution)/shard_map/pallas_call | solution.py:228
  155.4 16.6 %all-to-all-done.5.fetched_ref = bf16[128,32,128]{2,1,0:T(8,128)(2,1)S(1)} async-done(((bf16[128,32,128]{2,1,0:T(8,128)(2,1)}), bf16[128,32,128]{2,1,0:T(8,128)(2,1)S(1)}, u32[]{:S(2)}, u32[]{:S(2)}) %all-to-all-start.5) | async-done | bytes 1048608 | tf_op jit(solution)/shard_map/all_to_all | solution.py:543
  172.0 7.2 %all-to-all-start.4 = ((s16[128,32,128]{2,1,0:T(8,128)(2,1)}), s16[128,32,128]{2,1,0:T(8,128)(2,1)S(1)}, u32[]{:S(2)}, u32[]{:S(2)}) async-start(s16[128,32,128]{2,1,0:T(8,128)(2,1)} %shard_map.118), calls=%async_computation.4 | async-start | bytes 2097152 | tf_op jit(solution)/shard_map/all_to_all | solution.py:543
  179.2 17.9 %shard_map.119 = f32[65,32,128]{2,1,0:T(8,128)} custom-call(s32[1344]{0:T(1024)} %get-tuple-element.35.list_ref, s32[1]{0:T(128)} %get-tuple-element.36.steps_ref, bf16[1280,128,128]{2,1,0:T(8,128)(2,1)} %get-tuple-element.42.tiles_ref, bf16[128,32,128]{2,1,0:T(8,128)(2,1)} %copy-done.6), custom_call_target="tpu_custom_call" | custom-call | flops 10000000000 | bytes 40000000 | tf_op jit(solution)/shard_map/pallas_call | solution.py:241
  197.1 0.5 collective-permute-start.6
  197.6 2.5 %collective-permute-done.6 = f32[65,32,128]{2,1,0:T(8,128)S(1)} collective-permute-done((f32[65,32,128]{2,1,0:T(8,128)}, f32[65,32,128]{2,1,0:T(8,128)S(1)}, u32[]{:S(2)}, u32[]{:S(2)}) %collective-permute-start.6) | collective-permute-done | bytes 1064992 | tf_op jit(solution)/shard_map/ppermute | solution.py:546
  200.2 1.5 fusion.1.base_ref
  201.7 5.3 %all-to-all-done.4.got_ref = s16[128,32,128]{2,1,0:T(8,128)(2,1)S(1)} async-done(((s16[128,32,128]{2,1,0:T(8,128)(2,1)}), s16[128,32,128]{2,1,0:T(8,128)(2,1)S(1)}, u32[]{:S(2)}, u32[]{:S(2)}) %all-to-all-start.4) | async-done | bytes 1048608 | tf_op jit(solution)/shard_map/all_to_all | solution.py:543
  207.0 4.4 %collective-permute-start.7 = (s16[128,32,128]{2,1,0:T(8,128)(2,1)S(1)}, s16[128,32,128]{2,1,0:T(8,128)(2,1)S(1)}, u32[]{:S(2)}, u32[]{:S(2)}) collective-permute-start(s16[128,32,128]{2,1,0:T(8,128)(2,1)S(1)} %all-to-all-done.4.got_ref), channel_id=1, source_target_pairs={{0,1},{1,0},{2,3},{3,2},{4,5},{5,4},{6,7},{7,6},{8,9},{9,8},{10,11... | collective-permute-start | bytes 3145736 | tf_op jit(solution)/shard_map/ppermute | solution.py:546
  211.4 1.4 shard_map.120.own_ref
  212.8 0.8 collective-permute-done.7.got_ref
  213.7 2.5 %shard_map.121 = f32[64,32,128]{2,1,0:T(8,128)} custom-call(s32[128]{0:T(128)S(1)} %collective-permute-done.asked_other_ref, f32[64,32,128]{2,1,0:T(8,128)S(1)} %shard_map.120.own_ref, s16[128,32,128]{2,1,0:T(8,128)(2,1)S(1)} %collective-permute-done.7.got_ref, f32[64,32,128]{2,1,0:T(8,128)S(1)} %fusion.1.base_ref, f32[64,1,128]{2,1,0:T(1,128)S(1)} %bitcast.6), custom_call_target="tpu_custom_call" | custom-call | tf_op jit(solution)/shard_map/pallas_call | solution.py:328
  (18 shorter events, 0.0 us)
Async XLA Ops:
  0.0 46.5 %copy-start = (f32[64,32,128]{2,1,0:T(8,128)S(1)}, f32[64,32,128]{2,1,0:T(8,128)}, u32[]{:S(2)}) copy-start(f32[64,32,128]{2,1,0:T(8,128)} %emission_ref.1) | copy-start | bytes 3145732
  1.5 27.0 %all-to-all-start = ((s32[128,1,128]{2,1,0:T(1,128)}), s32[128,1,128]{2,1,0:T(1,128)S(1)}, u32[]{:S(2)}, u32[]{:S(2)}) async-start(s32[128,1,128]{2,1,0:T(1,128)} %shard_map.109), calls=%async_computation | async-start | bytes 131072 | tf_op jit(solution)/shard_map/all_to_all | solution.py:543
  17.9 0.8 copy-start.1
  18.6 0.9 copy-start.3
  19.5 0.8 copy-start.4
  20.3 26.3 %copy-start.2 = (f32[64,128]{1,0:T(8,128)S(1)}, f32[64,128]{1,0:T(8,128)}, u32[]{:S(2)}) copy-start(f32[64,128]{1,0:T(8,128)} %area_ref.1) | copy-start | bytes 98308
  30.1 21.7 %all-to-all-start.1 = ((f32[128,1,640]{2,1,0:T(1,128)}), f32[128,1,640]{2,1,0:T(1,128)S(1)}, u32[]{:S(2)}, u32[]{:S(2)}) async-start(f32[128,1,640]{2,1,0:T(1,128)} %get-tuple-element.31), calls=%async_computation.1 | async-start | bytes 655360 | tf_op jit(solution)/shard_map/all_to_all | solution.py:543
  37.8 3.4 %collective-permute-start.1 = (s32[640]{0:T(1024)}, s32[640]{0:T(1024)S(1)}, u32[]{:S(2)}, u32[]{:S(2)}) collective-permute-start(s32[640]{0:T(1024)} %param.18), channel_id=1, source_target_pairs={{0,1},{1,0},{2,3},{3,2},{4,5},{5,4},{6,7},{7,6},{8,9},{9,8},{10,11... | collective-permute-start | bytes 7688 | tf_op jit(solution)/shard_map/ppermute | solution.py:546
  39.4 1.8 collective-permute-start.2
  39.5 1.7 collective-permute-start.3
  51.8 10.5 %copy-start.7 = (f32[128,1,640]{2,1,0:T(1,128)}, f32[128,1,640]{2,1,0:T(1,128)S(1)}, u32[]{:S(2)}) copy-start(f32[128,1,640]{2,1,0:T(1,128)S(1)} %all-to-all-done.1.geometry_ref) | copy-start | bytes 983044
  51.8 39.6 %all-to-all-start.3 = ((bf16[128,32,128]{2,1,0:T(8,128)(2,1)}), bf16[128,32,128]{2,1,0:T(8,128)(2,1)S(1)}, u32[]{:S(2)}, u32[]{:S(2)}) async-start(bf16[128,32,128]{2,1,0:T(8,128)(2,1)} %get-tuple-element.44), calls=%async_computation.3 | async-start | bytes 2097152 | tf_op jit(solution)/shard_map/all_to_all | solution.py:543
  61.9 22.2 %collective-permute-start = (s32[128]{0:T(128)S(1)}, s32[128]{0:T(128)S(1)}, u32[]{:S(2)}, u32[]{:S(2)}) collective-permute-start(s32[128]{0:T(128)S(1)} %bitcast.11), channel_id=1, source_target_pairs={{0,1},{1,0},{2,3},{3,2},{4,5},{5,4},{6,7},{7,6},{8,9},{9,8},{10,11... | collective-permute-start | bytes 1544 | tf_op jit(solution)/shard_map/ppermute | solution.py:546
  91.5 7.4 %copy-start.5 = (bf16[128,32,128]{2,1,0:T(8,128)(2,1)}, bf16[128,32,128]{2,1,0:T(8,128)(2,1)S(1)}, u32[]{:S(2)}) copy-start(bf16[128,32,128]{2,1,0:T(8,128)(2,1)S(1)} %all-to-all-done.3.fetched_ref) | copy-start | bytes 3145732
  91.5 35.0 %all-to-all-start.2 = ((s16[128,32,128]{2,1,0:T(8,128)(2,1)}), s16[128,32,128]{2,1,0:T(8,128)(2,1)S(1)}, u32[]{:S(2)}, u32[]{:S(2)}) async-start(s16[128,32,128]{2,1,0:T(8,128)(2,1)} %get-tuple-element.43), calls=%async_computation.2 | async-start | bytes 2097152 | tf_op jit(solution)/shard_map/all_to_all | solution.py:543
  98.8 18.6 %copy-start.8 = (s32[64,128]{1,0:T(8,128)S(1)}, s32[64,128]{1,0:T(8,128)}, u32[]{:S(2)}) copy-start(s32[64,128]{1,0:T(8,128)} %param.15) | copy-start | bytes 98308
  98.9 18.6 %copy-start.9 = (f32[8]{0:T(128)S(1)}, f32[8]{0:T(128)}, u32[]{:S(2)}) copy-start(f32[8]{0:T(128)} %param.16) | copy-start | bytes 100
  116.8 3.2 %collective-permute-start.4 = (f32[65,32,128]{2,1,0:T(8,128)}, f32[65,32,128]{2,1,0:T(8,128)S(1)}, u32[]{:S(2)}, u32[]{:S(2)}) collective-permute-start(f32[65,32,128]{2,1,0:T(8,128)} %shard_map.115), channel_id=1, source_target_pairs={{0,1},{1,0},{2,3},{3,2},{4,5},{5,4},{6,7},{7,6},{8,9},{9,8},{10,11... | collective-permute-start | bytes 3194888 | tf_op jit(solution)/shard_map/ppermute | solution.py:546
  126.5 6.8 %collective-permute-start.5 = (s16[128,32,128]{2,1,0:T(8,128)(2,1)S(1)}, s16[128,32,128]{2,1,0:T(8,128)(2,1)S(1)}, u32[]{:S(2)}, u32[]{:S(2)}) collective-permute-start(s16[128,32,128]{2,1,0:T(8,128)(2,1)S(1)} %all-to-all-done.2.got_ref), channel_id=1, source_target_pairs={{0,1},{1,0},{2,3},{3,2},{4,5},{5,4},{6,7},{7,6},{8,9},{9,8},{10,11... | collective-permute-start | bytes 3145736 | tf_op jit(solution)/shard_map/ppermute | solution.py:546
  136.2 35.8 %all-to-all-start.5 = ((bf16[128,32,128]{2,1,0:T(8,128)(2,1)}), bf16[128,32,128]{2,1,0:T(8,128)(2,1)S(1)}, u32[]{:S(2)}, u32[]{:S(2)}) async-start(bf16[128,32,128]{2,1,0:T(8,128)(2,1)} %get-tuple-element.48), calls=%async_computation.5 | async-start | bytes 2097152 | tf_op jit(solution)/shard_map/all_to_all | solution.py:543
  172.0 7.2 %copy-start.6 = (bf16[128,32,128]{2,1,0:T(8,128)(2,1)}, bf16[128,32,128]{2,1,0:T(8,128)(2,1)S(1)}, u32[]{:S(2)}) copy-start(bf16[128,32,128]{2,1,0:T(8,128)(2,1)S(1)} %all-to-all-done.5.fetched_ref) | copy-start | bytes 3145732
  172.0 35.0 %all-to-all-start.4 = ((s16[128,32,128]{2,1,0:T(8,128)(2,1)}), s16[128,32,128]{2,1,0:T(8,128)(2,1)S(1)}, u32[]{:S(2)}, u32[]{:S(2)}) async-start(s16[128,32,128]{2,1,0:T(8,128)(2,1)} %shard_map.118), calls=%async_computation.4 | async-start | bytes 2097152 | tf_op jit(solution)/shard_map/all_to_all | solution.py:543
  197.1 3.1 %collective-permute-start.6 = (f32[65,32,128]{2,1,0:T(8,128)}, f32[65,32,128]{2,1,0:T(8,128)S(1)}, u32[]{:S(2)}, u32[]{:S(2)}) collective-permute-start(f32[65,32,128]{2,1,0:T(8,128)} %shard_map.119), channel_id=1, source_target_pairs={{0,1},{1,0},{2,3},{3,2},{4,5},{5,4},{6,7},{7,6},{8,9},{9,8},{10,11... | collective-permute-start | bytes 3194888 | tf_op jit(solution)/shard_map/ppermute | solution.py:546
  207.0 6.7 %collective-permute-start.7 = (s16[128,32,128]{2,1,0:T(8,128)(2,1)S(1)}, s16[128,32,128]{2,1,0:T(8,128)(2,1)S(1)}, u32[]{:S(2)}, u32[]{:S(2)}) collective-permute-start(s16[128,32,128]{2,1,0:T(8,128)(2,1)S(1)} %all-to-all-done.4.got_ref), channel_id=1, source_target_pairs={{0,1},{1,0},{2,3},{3,2},{4,5},{5,4},{6,7},{7,6},{8,9},{9,8},{10,11... | collective-permute-start | bytes 3145736 | tf_op jit(solution)/shard_map/ppermute | solution.py:546
